TPU v7x, 32 devices: a whole 2x2x4 slice. The times are simulated.
32 devices in a mesh: tm: 8 (over y, x, core), dp: 4 (over z).
Axes of the slice: x: 2, y: 2, z: 4, core: 2. Of those that a mesh axis runs over, the one named last changes fastest.
Arguments:
- embedded_features: bfloat16 [32, 1024, 160], P('dp', 'tm'), may hold values from -6 to 6
- earliest_seen_moment: int32 [32], P('dp'), may hold values from 0 to 511
- reach_choice: int32 [32], P('dp'), may hold values from 0 to 2
- lstm_valve_coeffs: float32 [160, 640], P('dp'), may hold values from -0.5 to 0.5
- lstm_unit_coeffs: float32 [160, 320], P('dp'), may hold values from -0.5 to 0.5
- asker_lookup_coeffs: float32 [160, 360], P('dp'), may hold values from -0.5 to 0.5
- attend_exit_coeffs: float32 [40, 160], P('dp'), may hold values from -3 to 3
- attend_unit_coeffs: float32 [160, 320], P('dp'), may hold values from -0.5 to 0.5
- skipnet_entry_coeffs: float32 [160, 160], P('dp'), may hold values from -0.5 to 0.5
- skipnet_inner_coeffs: float32 [160, 160], P('dp'), may hold values from -0.5 to 0.5
- skipnet_unit_coeffs: float32 [160, 320], P('dp'), may hold values from -0.5 to 0.5
- level_map_coeffs: float32 [160, 3], P('dp'), may hold values from -0.5 to 0.5
- bias_gain_table: float32 [160, 18], P('dp')
- block_emit_adjoint: bfloat16 [32, 1024, 160], P('dp', 'tm'), may hold values from -6 to 6
- predicted_adjoint: bfloat16 [32, 3, 1024], P('dp', None, 'tm'), may hold values from -6 to 6
Outputs:
- second_block_emit: bfloat16 [32, 1024, 160], P('dp', 'tm')
- predicted_levels: float32 [32, 3, 1024], P('dp', None, 'tm')
- grad_inputs: bfloat16 [32, 1024, 160], P('dp', 'tm')
- grad_lstm_weight: float32 [160, 640], P('dp')
- grad_lstm_glu_weight: float32 [160, 320], P('dp')
- grad_qkv_weight: float32 [160, 360], P('dp')
- grad_attn_out_weight: float32 [40, 160], P('dp')
- grad_attn_glu_weight: float32 [160, 320], P('dp')
- grad_grn_in_weight: float32 [160, 160], P('dp')
- grad_grn_mid_weight: float32 [160, 160], P('dp')
- grad_grn_glu_weight: float32 [160, 320], P('dp')
- grad_quantile_weight: float32 [160, 3], P('dp')
- grad_vectors: float32 [160, 18], P('dp')
All inputs are finite; a program needn't handle non-finite values.
Results may differ from a plain program's by a relative error of at most 0.018.
The roundings to bfloat16 on the way count: a program that leaves them out, or rounds other values in their place, can miss the bound.
Values may be sent and summed in bfloat16 or wider, within the bound.
A program may use at most 320 MiB of HBM per device.

v0:
```python
import jax
import jax.numpy as jnp
from jax import lax
from jax.sharding import PartitionSpec as P

HEADS = 4
LEVEL_TALLY = 3
DEC = 24
MICRO = 2


EPSILON = 1e-05
NEG_BIG = -1e30
attend_group = 2


def entering(value, axis, join, neutral, backward):
    count, mine = (lax.axis_size(axis), lax.axis_index(axis))
    pieces = jax.tree.map(lambda part: lax.all_gather(part, axis), value)
    if backward:
        pieces = jax.tree.map(lambda part: part[::-1], pieces)
        mine = count - 1 - mine
    so_far = jax.tree.map(
        lambda part, zero: jnp.full_like(part, 0) + jnp.asarray(zero, part.dtype), value, neutral
    )

    def turn(position, so_far):
        longer = join(so_far, jax.tree.map(lambda part: part[position], pieces))
        return jax.tree.map(lambda new, old: jnp.where(position < mine, new, old), longer, so_far)

    return lax.fori_loop(0, count - 1, turn, so_far)


def narrow_convert(values):
    return values.astype(jnp.bfloat16)


def tensor_dot_plain(left, right):
    return jnp.dot(left, right, preferred_element_type=jnp.float32)


def flipped_dot(left, right):
    return lax.dot_general(
        left, right, (((0,), (0,)), ((), ())), preferred_element_type=jnp.float32
    )


def dot_against_flipped(left, right):
    return lax.dot_general(
        left, right, (((1,), (1,)), ((), ())), preferred_element_type=jnp.float32
    )


def affine_join(earlier, later):
    return (later[0] * earlier[0], later[0] * earlier[1] + later[1])


def layer_norm(values, gains, offsets):
    centred = values - jnp.mean(values, axis=-1, keepdims=True)
    spread = jnp.mean(centred * centred, axis=-1, keepdims=True)
    return centred * lax.rsqrt(spread + EPSILON) * gains + offsets


def gated_unit(pre_act):
    half_width = pre_act.shape[-1] // 2
    return pre_act[..., :half_width] * jax.nn.sigmoid(pre_act[..., half_width:])


def lstm_gates(pre_act, keep_mask):
    quarter = pre_act.shape[-1] // 4
    forget = jax.nn.sigmoid(pre_act[..., :quarter]) * keep_mask
    inflow = jax.nn.sigmoid(pre_act[..., quarter : 2 * quarter]) * jnp.tanh(
        pre_act[..., 2 * quarter : 3 * quarter]
    )
    out_gate = jax.nn.sigmoid(pre_act[..., 3 * quarter :])
    return (forget, inflow, out_gate)


def masked_scores(query_block, key_block, query_pos, key_pos, begin_block, scale):
    raw = jnp.einsum("gqhd,gkhd->ghqk", query_block, key_block, preferred_element_type=jnp.float32)
    lowest = jnp.minimum(begin_block[:, None], query_pos[None, :])
    allowed = (key_pos[None, None, :] <= query_pos[None, :, None]) & (
        key_pos[None, None, :] >= lowest[:, :, None]
    )
    return jnp.where(allowed[:, None], raw * scale, NEG_BIG)


def score_grad(chances, dprob, row_delta, scale):
    return narrow_convert(chances * (dprob[:, None] - row_delta[..., None]) * scale)


def shards(
    embedded_features,
    earliest_seen_moment,
    reach_choice,
    lstm_valve_coeffs,
    lstm_unit_coeffs,
    asker_lookup_coeffs,
    attend_exit_coeffs,
    attend_unit_coeffs,
    skipnet_entry_coeffs,
    skipnet_inner_coeffs,
    skipnet_unit_coeffs,
    level_map_coeffs,
    bias_gain_table,
    block_emit_adjoint,
    predicted_adjoint,
):
    (
        mat_lstm,
        mat_glu_one,
        mat_qkv,
        mat_attn,
        mat_glu_two,
        mat_inner,
        mat_middle,
        mat_glu_three,
        level_dot,
        vec_table,
    ) = (
        lax.all_gather(narrow_convert(lstm_valve_coeffs), "dp", axis=0, tiled=True),
        lax.all_gather(narrow_convert(lstm_unit_coeffs), "dp", axis=0, tiled=True),
        lax.all_gather(narrow_convert(asker_lookup_coeffs), "dp", axis=0, tiled=True),
        lax.all_gather(narrow_convert(attend_exit_coeffs), "dp", axis=0, tiled=True),
        lax.all_gather(narrow_convert(attend_unit_coeffs), "dp", axis=0, tiled=True),
        lax.all_gather(narrow_convert(skipnet_entry_coeffs), "dp", axis=0, tiled=True),
        lax.all_gather(narrow_convert(skipnet_inner_coeffs), "dp", axis=0, tiled=True),
        lax.all_gather(narrow_convert(skipnet_unit_coeffs), "dp", axis=0, tiled=True),
        lax.all_gather(narrow_convert(level_map_coeffs), "dp", axis=0, tiled=True),
        lax.all_gather(narrow_convert(bias_gain_table), "dp", axis=0, tiled=True),
    )
    series_per_device, steps_per_device, model_width = embedded_features.shape
    seq_total = steps_per_device * lax.axis_size("tm")
    head_width = model_width // HEADS
    count_of_rows = series_per_device * steps_per_device
    scale = head_width ** (-0.5)
    vec_full = vec_table.astype(jnp.float32)
    time_local = lax.axis_index("tm") * steps_per_device + jnp.arange(
        steps_per_device, dtype=jnp.int32
    )
    time_all = jnp.arange(seq_total, dtype=jnp.int32)
    horizon_len = jnp.where(reach_choice == 0, 1, jnp.where(reach_choice == 1, 5, 24))
    ahead_moment_filter = (
        (
            (time_local[None, :] >= seq_total - DEC)
            & (time_local[None, :] < seq_total - DEC + horizon_len[:, None])
        )
        .astype(jnp.float32)
        .reshape(count_of_rows, 1)
    )
    keep_mask = (
        (time_local[None, :] != earliest_seen_moment[:, None])
        .astype(jnp.float32)
        .reshape(count_of_rows, 1)
    )
    group_size = series_per_device // MICRO
    group_total = series_per_device // attend_group
    state_ones = jnp.ones((group_size, model_width), jnp.float32)
    state_zeros = jnp.zeros((group_size, model_width), jnp.float32)

    def split_groups(array):
        return array.reshape((group_total, attend_group) + array.shape[1:])

    input_rows = embedded_features.reshape(count_of_rows, model_width)
    input_full = input_rows.astype(jnp.float32)
    lstm_pre = tensor_dot_plain(input_rows, mat_lstm) + vec_full[:, 0:4].T.reshape(-1)
    forget, inflow, out_gate = lstm_gates(lstm_pre, keep_mask)
    forget_seq = forget.reshape(series_per_device, steps_per_device, model_width)
    inflow_seq = inflow.reshape(series_per_device, steps_per_device, model_width)
    mult_seq, cell_local = lax.associative_scan(affine_join, (forget_seq, inflow_seq), axis=1)
    cell_parts = []
    for group in range(MICRO):
        lower_row = group * group_size
        upper_row = lower_row + group_size
        _, arriving = entering(
            (mult_seq[lower_row:upper_row, -1], cell_local[lower_row:upper_row, -1]),
            "tm",
            affine_join,
            (state_ones, state_zeros),
            False,
        )
        cell_parts.append(arriving)
    cell_in = jnp.concatenate(cell_parts, axis=0)
    cell_seq = cell_local + mult_seq * cell_in[:, None, :]
    cell_tanh = jnp.tanh(cell_seq.reshape(count_of_rows, model_width))
    hidden_low = narrow_convert(out_gate * cell_tanh)
    glu_one_pre = tensor_dot_plain(hidden_low, mat_glu_one) + vec_full[:, 4:6].T.reshape(-1)
    first_sum = input_full + gated_unit(glu_one_pre)
    first = layer_norm(first_sum, vec_full[:, 6], vec_full[:, 7])
    first_low = narrow_convert(first)
    qkv_low = narrow_convert(tensor_dot_plain(first_low, mat_qkv))
    query_low = qkv_low[:, :model_width].reshape(
        series_per_device, steps_per_device, HEADS, head_width
    )
    key_value = qkv_low[:, model_width:].reshape(
        series_per_device, steps_per_device, model_width + head_width
    )
    key_value_all = lax.all_gather(key_value, "tm", axis=1, tiled=True)
    keys_all = key_value_all[..., :model_width].reshape(
        series_per_device, seq_total, HEADS, head_width
    )
    values_all = key_value_all[..., model_width:]

    def attend_forward(block_args):
        query_block, key_block, value_block, begin_block = block_args
        scores = masked_scores(query_block, key_block, time_local, time_all, begin_block, scale)
        row_top = jnp.max(scores, axis=-1, keepdims=True)
        row_exp = jnp.exp(scores - row_top)
        row_total = jnp.sum(row_exp, axis=-1, keepdims=True)
        weights_low = narrow_convert(row_exp / row_total)
        mixed_block = jnp.einsum(
            "ghqk,gkd->gqd", weights_low, value_block, preferred_element_type=jnp.float32
        ) * (1.0 / HEADS)
        return (mixed_block, (row_top + jnp.log(row_total))[..., 0])

    mixed, log_total = lax.map(
        attend_forward,
        (
            split_groups(query_low),
            split_groups(keys_all),
            split_groups(values_all),
            split_groups(earliest_seen_moment),
        ),
    )
    mixed_low = narrow_convert(mixed.reshape(count_of_rows, head_width))
    attn_low = narrow_convert(tensor_dot_plain(mixed_low, mat_attn))
    glu_two_pre = tensor_dot_plain(attn_low, mat_glu_two) + vec_full[:, 8:10].T.reshape(-1)
    second_sum = first + gated_unit(glu_two_pre)
    second = layer_norm(second_sum, vec_full[:, 10], vec_full[:, 11])
    second_low = narrow_convert(second)
    inner_pre = tensor_dot_plain(second_low, mat_inner) + vec_full[:, 12]
    inner_low = narrow_convert(jax.nn.elu(inner_pre))
    middle_low = narrow_convert(tensor_dot_plain(inner_low, mat_middle) + vec_full[:, 13])
    glu_three_pre = tensor_dot_plain(middle_low, mat_glu_three) + vec_full[:, 14:16].T.reshape(-1)
    final_sum = second + gated_unit(glu_three_pre)
    second_block_emit = layer_norm(final_sum, vec_full[:, 16], vec_full[:, 17])
    closing_narrowed = narrow_convert(second_block_emit)
    predicted_entries = tensor_dot_plain(closing_narrowed, level_dot) * ahead_moment_filter
    predicted_levels = predicted_entries.reshape(
        series_per_device, steps_per_device, LEVEL_TALLY
    ).transpose(0, 2, 1)
    predicted_slope = narrow_convert(
        predicted_adjoint.astype(jnp.float32).transpose(0, 2, 1).reshape(count_of_rows, LEVEL_TALLY)
        * ahead_moment_filter
    )
    level_slope = flipped_dot(closing_narrowed, predicted_slope)
    final_grad = block_emit_adjoint.reshape(count_of_rows, model_width).astype(
        jnp.float32
    ) + dot_against_flipped(predicted_slope, level_dot)
    _, norm_pull = jax.vjp(layer_norm, final_sum, vec_full[:, 16], vec_full[:, 17])
    sum_three_grad, gain_three_grad, offset_three_grad = norm_pull(final_grad)
    _, glu_pull = jax.vjp(gated_unit, glu_three_pre)
    (glu_three_grad,) = glu_pull(sum_three_grad)
    glu_three_low = narrow_convert(glu_three_grad)
    grad_glu_three = flipped_dot(middle_low, glu_three_low)
    middle_grad = dot_against_flipped(glu_three_low, mat_glu_three)
    middle_grad_low = narrow_convert(middle_grad)
    grad_middle = flipped_dot(inner_low, middle_grad_low)
    inner_grad = dot_against_flipped(middle_grad_low, mat_middle)
    _, elu_pull = jax.vjp(jax.nn.elu, inner_pre)
    (inner_pre_grad,) = elu_pull(inner_grad)
    inner_pre_low = narrow_convert(inner_pre_grad)
    grad_inner = flipped_dot(second_low, inner_pre_low)
    second_grad = sum_three_grad + dot_against_flipped(inner_pre_low, mat_inner)
    _, norm_pull = jax.vjp(layer_norm, second_sum, vec_full[:, 10], vec_full[:, 11])
    sum_two_grad, gain_two_grad, offset_two_grad = norm_pull(second_grad)
    _, glu_pull = jax.vjp(gated_unit, glu_two_pre)
    (glu_two_grad,) = glu_pull(sum_two_grad)
    glu_two_low = narrow_convert(glu_two_grad)
    grad_glu_two = flipped_dot(attn_low, glu_two_low)
    attn_grad_low = narrow_convert(dot_against_flipped(glu_two_low, mat_glu_two))
    grad_attn = flipped_dot(mixed_low, attn_grad_low)
    mixed_grad_low = narrow_convert(dot_against_flipped(attn_grad_low, mat_attn))
    head_grad = (mixed_grad_low * (1.0 / HEADS)).reshape(
        series_per_device, steps_per_device, head_width
    )

    def attend_backward(block_args):
        query_block, key_block, value_block, begin_block, lse_block, dout_block = block_args
        scores = masked_scores(query_block, key_block, time_local, time_all, begin_block, scale)
        chances = jnp.exp(scores - lse_block[..., None])
        dprob = jnp.einsum(
            "gqd,gkd->gqk", dout_block, value_block, preferred_element_type=jnp.float32
        )
        row_delta = jnp.sum(chances * dprob[:, None], axis=-1)
        dscore = score_grad(chances, dprob, row_delta, scale)
        dquery = jnp.einsum(
            "ghqk,gkhd->gqhd", dscore, key_block, preferred_element_type=jnp.float32
        )
        dkey = jnp.einsum(
            "ghqk,gqhd->gkhd", dscore, query_block, preferred_element_type=jnp.float32
        )
        dvalue = jnp.einsum(
            "ghqk,gqd->gkd", narrow_convert(chances), dout_block, preferred_element_type=jnp.float32
        )
        key_terms = jnp.concatenate(
            [dkey.reshape(attend_group, seq_total, model_width), dvalue], axis=-1
        )
        return (dquery, key_terms)

    dquery, key_terms = lax.map(
        attend_backward,
        (
            split_groups(query_low),
            split_groups(keys_all),
            split_groups(values_all),
            split_groups(earliest_seen_moment),
            log_total,
            split_groups(head_grad),
        ),
    )
    own_keys = lax.psum_scatter(
        key_terms.reshape(series_per_device, seq_total, model_width + head_width),
        "tm",
        scatter_dimension=1,
        tiled=True,
    )
    qkv_grad = jnp.concatenate(
        [
            dquery.reshape(count_of_rows, model_width),
            own_keys.reshape(count_of_rows, model_width + head_width),
        ],
        axis=1,
    )
    qkv_grad_low = narrow_convert(qkv_grad)
    grad_qkv = flipped_dot(first_low, qkv_grad_low)
    first_grad = sum_two_grad + dot_against_flipped(qkv_grad_low, mat_qkv)
    _, norm_pull = jax.vjp(layer_norm, first_sum, vec_full[:, 6], vec_full[:, 7])
    sum_one_grad, gain_one_grad, offset_one_grad = norm_pull(first_grad)
    _, glu_pull = jax.vjp(gated_unit, glu_one_pre)
    (glu_one_grad,) = glu_pull(sum_one_grad)
    glu_one_low = narrow_convert(glu_one_grad)
    grad_glu_one = flipped_dot(hidden_low, glu_one_low)
    hidden_grad = dot_against_flipped(glu_one_low, mat_glu_one)
    out_gate_grad = hidden_grad * cell_tanh
    direct_grad = (hidden_grad * out_gate * (1.0 - cell_tanh * cell_tanh)).reshape(
        series_per_device, steps_per_device, model_width
    )
    next_forget = jnp.concatenate([forget_seq[:, 1:], jnp.ones_like(forget_seq[:, :1])], axis=1)
    rev_mult, rev_cell = lax.associative_scan(
        affine_join, (next_forget, direct_grad), axis=1, reverse=True
    )
    head_mult = forget_seq[:, 0] * rev_mult[:, 0]
    head_cell = forget_seq[:, 0] * rev_cell[:, 0]
    coming_parts = []
    for group in range(MICRO):
        lower_row = group * group_size
        upper_row = lower_row + group_size
        _, coming = entering(
            (head_mult[lower_row:upper_row], head_cell[lower_row:upper_row]),
            "tm",
            affine_join,
            (state_ones, state_zeros),
            True,
        )
        coming_parts.append(coming)
    coming_all = jnp.concatenate(coming_parts, axis=0)
    cell_grad = rev_cell + rev_mult * coming_all[:, None, :]
    cell_prev = jnp.concatenate([cell_in[:, None, :], cell_seq[:, :-1]], axis=1)
    forget_grad = (cell_grad * cell_prev).reshape(count_of_rows, model_width)
    _, gate_pull = jax.vjp(lambda pre_value: lstm_gates(pre_value, keep_mask), lstm_pre)
    (lstm_pre_grad,) = gate_pull(
        (forget_grad, cell_grad.reshape(count_of_rows, model_width), out_gate_grad)
    )
    lstm_low = narrow_convert(lstm_pre_grad)
    grad_lstm = flipped_dot(input_rows, lstm_low)
    input_grad = sum_one_grad + dot_against_flipped(lstm_low, mat_lstm)
    grad_table = jnp.concatenate(
        [
            jnp.sum(lstm_pre_grad, axis=0).reshape(4, model_width).T,
            jnp.sum(glu_one_grad, axis=0).reshape(2, model_width).T,
            gain_one_grad[:, None],
            offset_one_grad[:, None],
            jnp.sum(glu_two_grad, axis=0).reshape(2, model_width).T,
            gain_two_grad[:, None],
            offset_two_grad[:, None],
            jnp.sum(inner_pre_grad, axis=0)[:, None],
            jnp.sum(middle_grad, axis=0)[:, None],
            jnp.sum(glu_three_grad, axis=0).reshape(2, model_width).T,
            gain_three_grad[:, None],
            offset_three_grad[:, None],
        ],
        axis=1,
    )
    (
        whole_lstm,
        whole_glu_one,
        whole_qkv,
        whole_attn,
        whole_glu_two,
        whole_inner,
        whole_middle,
        whole_glu_three,
        whole_quant,
        whole_table,
    ) = lax.psum(
        (
            grad_lstm,
            grad_glu_one,
            grad_qkv,
            grad_attn,
            grad_glu_two,
            grad_inner,
            grad_middle,
            grad_glu_three,
            level_slope,
            grad_table,
        ),
        "tm",
    )
    summed = (
        lax.psum_scatter(
            whole_lstm.astype(jnp.bfloat16), "dp", scatter_dimension=0, tiled=True
        ).astype(jnp.float32),
        lax.psum_scatter(
            whole_glu_one.astype(jnp.bfloat16), "dp", scatter_dimension=0, tiled=True
        ).astype(jnp.float32),
        lax.psum_scatter(
            whole_qkv.astype(jnp.bfloat16), "dp", scatter_dimension=0, tiled=True
        ).astype(jnp.float32),
        lax.psum_scatter(
            whole_attn.astype(jnp.bfloat16), "dp", scatter_dimension=0, tiled=True
        ).astype(jnp.float32),
        lax.psum_scatter(
            whole_glu_two.astype(jnp.bfloat16), "dp", scatter_dimension=0, tiled=True
        ).astype(jnp.float32),
        lax.psum_scatter(
            whole_inner.astype(jnp.bfloat16), "dp", scatter_dimension=0, tiled=True
        ).astype(jnp.float32),
        lax.psum_scatter(
            whole_middle.astype(jnp.bfloat16), "dp", scatter_dimension=0, tiled=True
        ).astype(jnp.float32),
        lax.psum_scatter(
            whole_glu_three.astype(jnp.bfloat16), "dp", scatter_dimension=0, tiled=True
        ).astype(jnp.float32),
        lax.psum_scatter(
            whole_quant.astype(jnp.bfloat16), "dp", scatter_dimension=0, tiled=True
        ).astype(jnp.float32),
        lax.psum_scatter(
            whole_table.astype(jnp.bfloat16), "dp", scatter_dimension=0, tiled=True
        ).astype(jnp.float32),
    )
    final_out = second_block_emit.astype(jnp.bfloat16).reshape(
        series_per_device, steps_per_device, model_width
    )
    input_out = input_grad.astype(jnp.bfloat16).reshape(
        series_per_device, steps_per_device, model_width
    )
    return (
        final_out,
        predicted_levels,
        input_out,
        summed[0],
        summed[1],
        summed[2],
        summed[3],
        summed[4],
        summed[5],
        summed[6],
        summed[7],
        summed[8],
        summed[9],
    )


def solution(mesh):
    placed = (
        P("dp", "tm", None),
        P("dp"),
        P("dp"),
        P("dp", None),
        P("dp", None),
        P("dp", None),
        P("dp", None),
        P("dp", None),
        P("dp", None),
        P("dp", None),
        P("dp", None),
        P("dp", None),
        P("dp", None),
        P("dp", "tm", None),
        P("dp", None, "tm"),
    )
    return jax.shard_map(
        shards,
        mesh=mesh,
        in_specs=placed,
        out_specs=(
            P("dp", "tm", None),
            P("dp", None, "tm"),
            P("dp", "tm", None),
            P("dp", None),
            P("dp", None),
            P("dp", None),
            P("dp", None),
            P("dp", None),
            P("dp", None),
            P("dp", None),
            P("dp", None),
            P("dp", None),
            P("dp", None),
        ),
        check_vma=False,
    )
```

profile of v0, /device:TPU:0, one launch (start us, length us, event | category | flops | bytes accessed | tf_op | source)
XLA Modules:
  0.0 766.6 jit_solution(2776849467604627344)
XLA Ops:
  8.0 14.8 %all-gather.8 = bf16[4,40,18]{1,2,0:T(8,128)(2,1)S(1)} all-gather(bf16[1,40,18]{1,2,0:T(8,128)(2,1)S(1)} %convert_bitcast_fusion.3), channel_id=1, replica_groups=mesh['tm'=8,'dp'=4] {'dp'}, dimensions={0}, use_global_device_ids=true | all-gather | bytes 7200 | tf_op jit(solution)/shard_map/all_gather | solution.py:130
  25.7 13.9 %all_gather.69 = bf16[160,640]{1,0:T(8,128)(2,1)S(1)} all-gather(bf16[40,640]{1,0:T(8,128)(2,1)S(1)} %convert_element_type.201), channel_id=1, replica_groups=mesh['tm'=8,'dp'=4] {'dp'}, dimensions={0}, use_global_device_ids=true | all-gather | bytes 256000 | tf_op jit(solution)/shard_map/all_gather | solution.py:121
  61.2 13.4 %all_gather.76 = bf16[160,360]{1,0:T(8,128)(2,1)S(1)} all-gather(bf16[40,360]{1,0:T(8,128)(2,1)S(1)} %convert_element_type.209), channel_id=1, replica_groups=mesh['tm'=8,'dp'=4] {'dp'}, dimensions={0}, use_global_device_ids=true | all-gather | bytes 144000 | tf_op jit(solution)/shard_map/all_gather | solution.py:123
  74.7 14.2 %all_gather.75 = bf16[160,320]{1,0:T(8,128)(2,1)} all-gather(bf16[40,320]{1,0:T(8,128)(2,1)S(1)} %convert_element_type.207), channel_id=1, replica_groups=mesh['tm'=8,'dp'=4] {'dp'}, dimensions={0}, use_global_device_ids=true | all-gather | bytes 128000 | tf_op jit(solution)/shard_map/all_gather | solution.py:122
  106.4 9.1 %all-gather = f32[32,1,160]{2,1,0:T(1,128)S(1)} all-gather(f32[4,1,160]{2,1,0:T(1,128)S(1)} %get-tuple-element.924), channel_id=2, replica_groups=mesh['tm'=8,'dp'=4] {'tm'}, dimensions={0}, use_global_device_ids=true | all-gather | bytes 23040 | tf_op jit(solution)/shard_map/all_gather | solution.py:19
  115.6 9.0 %all-gather.2 = f32[32,1,160]{2,1,0:T(1,128)S(1)} all-gather(f32[4,1,160]{2,1,0:T(1,128)S(1)} %get-tuple-element.925), channel_id=4, replica_groups=mesh['tm'=8,'dp'=4] {'tm'}, dimensions={0}, use_global_device_ids=true | all-gather | bytes 23040 | tf_op jit(solution)/shard_map/all_gather | solution.py:19
  130.4 8.1 %all-gather.1 = f32[32,1,160]{2,1,0:T(1,128)S(1)} all-gather(f32[4,1,160]{2,1,0:T(1,128)S(1)} %get-tuple-element.922), channel_id=3, replica_groups=mesh['tm'=8,'dp'=4] {'tm'}, dimensions={0}, use_global_device_ids=true | all-gather | bytes 23040 | tf_op jit(solution)/shard_map/all_gather | solution.py:19
  138.9 9.0 %all-gather.3 = f32[32,1,160]{2,1,0:T(1,128)S(1)} all-gather(f32[4,1,160]{2,1,0:T(1,128)S(1)} %get-tuple-element.923), channel_id=5, replica_groups=mesh['tm'=8,'dp'=4] {'tm'}, dimensions={0}, use_global_device_ids=true | all-gather | bytes 23040 | tf_op jit(solution)/shard_map/all_gather | solution.py:19
  158.5 10.7 %all-gather.10 = bf16[4,40,3]{1,2,0:T(4,128)(2,1)S(1)} all-gather(bf16[1,40,3]{1,2,0:T(4,128)(2,1)S(1)} %convert_bitcast_fusion.6), channel_id=1, replica_groups=mesh['tm'=8,'dp'=4] {'dp'}, dimensions={0}, use_global_device_ids=true | all-gather | bytes 1200 | tf_op jit(solution)/shard_map/all_gather | solution.py:129
  169.5 13.1 %all-gather.9 = bf16[4,10,160]{2,1,0:T(8,128)(2,1)S(1)} all-gather(bf16[1,10,160]{2,1,0:T(8,128)(2,1)S(1)} %convert_bitcast_fusion.2), channel_id=1, replica_groups=mesh['tm'=8,'dp'=4] {'dp'}, dimensions={0}, use_global_device_ids=true | all-gather | bytes 16000 | tf_op jit(solution)/shard_map/all_gather | solution.py:124
  183.7 13.8 %all_gather.81 = bf16[160,160]{1,0:T(8,128)(2,1)S(1)} all-gather(bf16[40,160]{1,0:T(8,128)(2,1)S(1)} %convert_element_type.219), channel_id=1, replica_groups=mesh['tm'=8,'dp'=4] {'dp'}, dimensions={0}, use_global_device_ids=true | all-gather | bytes 64000 | tf_op jit(solution)/shard_map/all_gather | solution.py:127
  197.5 13.2 %all_gather.80 = bf16[160,160]{1,0:T(8,128)(2,1)S(1)} all-gather(bf16[40,160]{1,0:T(8,128)(2,1)S(1)} %convert_element_type.217), channel_id=1, replica_groups=mesh['tm'=8,'dp'=4] {'dp'}, dimensions={0}, use_global_device_ids=true | all-gather | bytes 64000 | tf_op jit(solution)/shard_map/all_gather | solution.py:126
  210.7 13.3 %all_gather.82 = bf16[160,320]{1,0:T(8,128)(2,1)S(1)} all-gather(bf16[40,320]{1,0:T(8,128)(2,1)S(1)} %convert_element_type.221), channel_id=1, replica_groups=mesh['tm'=8,'dp'=4] {'dp'}, dimensions={0}, use_global_device_ids=true | all-gather | bytes 128000 | tf_op jit(solution)/shard_map/all_gather | solution.py:128
  224.0 13.3 %all_gather.79 = bf16[160,320]{1,0:T(8,128)(2,1)S(1)} all-gather(bf16[40,320]{1,0:T(8,128)(2,1)S(1)} %convert_element_type.215), channel_id=1, replica_groups=mesh['tm'=8,'dp'=4] {'dp'}, dimensions={0}, use_global_device_ids=true | all-gather | bytes 128000 | tf_op jit(solution)/shard_map/all_gather | solution.py:125
  243.3 31.0 %while.84 = (s32[]{:T(128)}, bf16[4,2,128,40]{2,3,1,0:T(8,128)(2,1)S(1)}, f32[4,2,4,128]{3,2,1,0:T(4,128)}, s32[4,2]{1,0:T(4,128)}, bf16[4,2,128,4,40]{2,4,3,1,0...) while((s32[]{:T(128)}, ...), condition=%wide.region_10.11_spmd.clone.clone, body=%wide.region_6.10_spmd.clone.clone.sunk | while | flops 119940480 | bytes 15922825 | solution.py:216
  287.4 82.0 %while.85 = (s32[]{:T(128)}, bf16[4,2,128,4,40]{2,4,3,1,0:T(8,128)(2,1)}, f32[4,2,1024,200]{2,3,1,0:T(8,128)}, bf16[4,2,1024,4,40]{2,4,3,1,0:T(8,128)(2,1)}, s32...) while((s32[]{:T(128)}, ...), condition=%wide.region_22.23_spmd.clone.clone, body=%wide.region_19.22_spmd.clone.clone.sunk | while | flops 311185792 | bytes 39061188 | solution.py:301
  369.4 9.4 %copy.147 = f32[8,1024,200]{1,0,2:T(8,128)} copy(f32[8,1024,200]{1,2,0:T(8,128)} %bitcast.358) | data formatting | bytes 13107200 | tf_op jit(solution)/shard_map/reshape | solution.py:313
  415.2 24.0 %reduce-scatter.21.cloned.1.call-done = f32[8,128,200]{1,0,2:T(8,128)} async-done(((f32[8,1024,200]{1,0,2:T(8,128)}), f32[8,128,200]{1,0,2:T(8,128)}) %reduce-scatter.21.cloned.1.call-update) | async-done | bytes 819216 | tf_op jit(solution)/shard_map/reduce_scatter | solution.py:312
  504.8 6.9 rev.20
  511.7 6.8 rev.21
  518.5 9.0 %all-gather.4 = f32[32,1,160]{2,1,0:T(1,128)S(1)} all-gather(f32[4,1,160]{2,1,0:T(1,128)S(1)} %get-tuple-element.1008), channel_id=6, replica_groups=mesh['tm'=8,'dp'=4] {'tm'}, dimensions={0}, use_global_device_ids=true | all-gather | bytes 23040 | tf_op jit(solution)/shard_map/all_gather | solution.py:19
  527.6 8.2 %all-gather.5 = f32[32,1,160]{2,1,0:T(1,128)S(1)} all-gather(f32[4,1,160]{2,1,0:T(1,128)S(1)} %get-tuple-element.1006), channel_id=7, replica_groups=mesh['tm'=8,'dp'=4] {'tm'}, dimensions={0}, use_global_device_ids=true | all-gather | bytes 23040 | tf_op jit(solution)/shard_map/all_gather | solution.py:19
  536.2 9.0 %all-gather.6 = f32[32,1,160]{2,1,0:T(1,128)S(1)} all-gather(f32[4,1,160]{2,1,0:T(1,128)S(1)} %get-tuple-element.1009), channel_id=8, replica_groups=mesh['tm'=8,'dp'=4] {'tm'}, dimensions={0}, use_global_device_ids=true | all-gather | bytes 23040 | tf_op jit(solution)/shard_map/all_gather | solution.py:19
  545.3 8.4 %all-gather.7 = f32[32,1,160]{2,1,0:T(1,128)S(1)} all-gather(f32[4,1,160]{2,1,0:T(1,128)S(1)} %get-tuple-element.1007), channel_id=9, replica_groups=mesh['tm'=8,'dp'=4] {'tm'}, dimensions={0}, use_global_device_ids=true | all-gather | bytes 23040 | tf_op jit(solution)/shard_map/all_gather | solution.py:19
  565.3 54.8 %all-reduce.79 = (bf16[160,640]{1,0:T(8,128)(2,1)}, bf16[160,320]{1,0:T(8,128)(2,1)}, bf16[160,360]{1,0:T(8,128)(2,1)}, bf16[40,160]{1,0:T(8,128)(2,1)S(1)}, bf1...) all-reduce(f32[160,640]{1,0:T(8,128)} %convolution_bitcast_fusion, ...), channel_id=1, replica_groups=mesh['tm'=8,'dp'=4] {'tm'}, use_global_device_ids=true, to_apply=%region_30.31 | all-reduce | flops 374560 | bytes 2247360 | tf_op jit(solution)/shard_map/psum | solution.py:396
  628.9 19.4 %all-reduce.77 = (bf16[40,160]{1,0:T(8,128)(2,1)S(1)}, bf16[160,3]{0,1:T(4,128)(2,1)S(1)}, bf16[160,18]{0,1:T(8,128)(2,1)S(1)}) all-reduce(bf16[40,160]{1,0:T(8,128)(2,1)S(1)} %get-tuple-element.885, bf16[160,3]{0,1:T(4,128)(2,1)S(1)} %get-tuple-element.890, ...), channel_id=14, replica_groups=mesh['tm'=8,'dp'=4] {'dp'}, use_global_device_ids=true, to_apply=%region_37.38.clone | all-reduce | flops 9760 | bytes 39040
  651.6 8.3 %reduce-scatter.23.cloned.1.call-done = bf16[40,160]{1,0:T(8,128)(2,1)} async-done(((bf16[160,160]{1,0:T(8,128)(2,1)}), bf16[40,160]{1,0:T(8,128)(2,1)}) %reduce-scatter.23.cloned.1.call-update) | async-done | bytes 12816 | tf_op jit(solution)/shard_map/reduce_scatter | solution.py:427
  661.3 18.1 %reduce-scatter.35.cloned.1.call-done = bf16[40,320]{1,0:T(8,128)(2,1)} async-done(((bf16[160,320]{1,0:T(8,128)(2,1)}), bf16[40,320]{1,0:T(8,128)(2,1)}) %reduce-scatter.35.cloned.1.call-update) | async-done | bytes 25616
  680.8 18.0 %reduce-scatter.33.cloned.1.call-done = bf16[40,320]{1,0:T(8,128)(2,1)} async-done(((bf16[160,320]{1,0:T(8,128)(2,1)}), bf16[40,320]{1,0:T(8,128)(2,1)}) %reduce-scatter.33.cloned.1.call-update) | async-done | bytes 25616
  700.2 18.2 %reduce-scatter.29.cloned.1.call-done = bf16[40,320]{1,0:T(8,128)(2,1)} async-done(((bf16[160,320]{1,0:T(8,128)(2,1)}), bf16[40,320]{1,0:T(8,128)(2,1)}) %reduce-scatter.29.cloned.1.call-update) | async-done | bytes 25616
  719.8 18.1 %reduce-scatter.31.cloned.1.call-done = bf16[40,360]{1,0:T(8,128)(2,1)} async-done(((bf16[160,360]{1,0:T(8,128)(2,1)}), bf16[40,360]{1,0:T(8,128)(2,1)}) %reduce-scatter.31.cloned.1.call-update) | async-done | bytes 28816
  739.3 18.9 %reduce-scatter.27.cloned.1.call-done = bf16[40,640]{1,0:T(8,128)(2,1)} async-done(((bf16[160,640]{1,0:T(8,128)(2,1)}), bf16[40,640]{1,0:T(8,128)(2,1)}) %reduce-scatter.27.cloned.1.call-update) | async-done | bytes 51216
  (746 shorter events, 323.7 us)
Async XLA Ops:
  7.2 32.5 %copy-start = (bf16[8,128,160]{1,2,0:T(8,128)(2,1)S(1)}, bf16[8,128,160]{1,2,0:T(8,128)(2,1)}, u32[]{:S(2)}) copy-start(bf16[8,128,160]{1,2,0:T(8,128)(2,1)} %param.27) | copy-start | bytes 983044
  7.2 34.5 %copy-start.99 = (s32[8]{0:T(128)S(1)}, s32[8]{0:T(128)}, u32[]{:S(2)}) copy-start(s32[8]{0:T(128)} %param.28) | copy-start | bytes 100
  7.2 230.1 %all-gather.13.cloned.1.call-start = ((), (), s32[]{:S(2)}) async-start(), calls=%async_computation.8 | async-start | bytes 3686400 | tf_op jit(solution)/shard_map/all_gather | solution.py:198
  74.7 15.7 %copy-start.74 = (f32[8,1,160]{2,1,0:T(1,128)S(1)}, f32[8,1,160]{2,1,0:T(1,128)}, u32[]{:S(2)}) copy-start(f32[8,1,160]{2,1,0:T(1,128)} %slice.754) | copy-start | bytes 15364
  101.9 27.8 %copy-start.18 = (f32[8,128,160]{2,1,0:T(8,128)S(1)}, f32[8,128,160]{2,1,0:T(8,128)}, u32[]{:S(2)}) copy-start(f32[8,128,160]{2,1,0:T(8,128)} %pad.217) | copy-start | bytes 1966084
  156.0 13.4 %copy-start.84 = (f32[2,160]{1,0:T(2,128)S(1)}, f32[2,160]{1,0:T(2,128)}, u32[]{:S(2)}) copy-start(f32[2,160]{1,0:T(2,128)} %get-tuple-element.992) | copy-start | bytes 3844
  156.0 13.4 %copy-start.61 = (f32[40,160]{1,0:T(8,128)S(1)}, f32[40,160]{1,0:T(8,128)}, u32[]{:S(2)}) copy-start(f32[40,160]{1,0:T(8,128)} %param.35) | copy-start | bytes 76804
  156.0 13.4 %copy-start.62 = (f32[40,160]{1,0:T(8,128)S(1)}, f32[40,160]{1,0:T(8,128)}, u32[]{:S(2)}) copy-start(f32[40,160]{1,0:T(8,128)} %param.36) | copy-start | bytes 76804
  156.0 13.5 %copy-start.81 = (f32[10,160]{1,0:T(8,128)S(1)}, f32[10,160]{1,0:T(8,128)}, u32[]{:S(2)}) copy-start(f32[10,160]{1,0:T(8,128)} %param.33) | copy-start | bytes 19204
  156.1 26.6 %copy-start.59 = (f32[40,320]{1,0:T(8,128)S(1)}, f32[40,320]{1,0:T(8,128)}, u32[]{:S(2)}) copy-start(f32[40,320]{1,0:T(8,128)} %param.34) | copy-start | bytes 153604
  156.1 26.6 %copy-start.60 = (f32[40,320]{1,0:T(8,128)S(1)}, f32[40,320]{1,0:T(8,128)}, u32[]{:S(2)}) copy-start(f32[40,320]{1,0:T(8,128)} %param.37) | copy-start | bytes 153604
  156.2 26.8 %copy-start.66 = (f32[1024]{0:T(1024)}, f32[1024]{0:T(1024)S(1)}, u32[]{:S(2)}) copy-start(f32[1024]{0:T(1024)S(1)} %multiply_reduce_fusion.9) | copy-start | bytes 12292
  156.7 80.6 %copy-start.89 = (bf16[8,3,128]{2,0,1:T(8,128)(2,1)S(1)}, bf16[8,3,128]{2,0,1:T(8,128)(2,1)}, u32[]{:S(2)}) copy-start(bf16[8,3,128]{2,0,1:T(8,128)(2,1)} %param.41) | copy-start | bytes 18436
  157.7 281.5 %reduce-scatter.21.cloned.1.call-start = ((), (), s32[]{:S(2)}) async-start(), calls=%async_computation.9 | async-start | bytes 7372800 | tf_op jit(solution)/shard_map/reduce_scatter | solution.py:312
  169.3 109.6 %copy-start.76 = (bf16[160,3]{0,1:T(4,128)(2,1)}, bf16[160,3]{0,1:T(4,128)(2,1)S(1)}, u32[]{:S(2)}) copy-start(bf16[160,3]{0,1:T(4,128)(2,1)S(1)} %reshape.478) | copy-start | bytes 2884
  237.3 41.6 %copy-start.47 = (f32[1,3,8,128]{3,2,1,0:T(8,128)}, f32[1,3,8,128]{3,2,1,0:T(8,128)S(1)}, u32[]{:S(2)}) copy-start(f32[1,3,8,128]{3,2,1,0:T(8,128)S(1)} %convert_bitcast_fusion.1) | copy-start | bytes 36868
  378.8 271.5 %reduce-scatter.25.cloned.1.call-start = ((), (), s32[]{:S(2)}) async-start(), calls=%async_computation.11 | async-start | bytes 102400 | tf_op jit(solution)/shard_map/reduce_scatter | solution.py:430
  411.4 29.1 %copy-start.12 = (f32[1024,160]{0,1:T(8,128)S(1)}, f32[1024,160]{0,1:T(8,128)}, u32[]{:S(2)}) copy-start(f32[1024,160]{0,1:T(8,128)} %copy-done.11) | copy-start | bytes 1966084
  480.9 15.3 %copy-start.28 = (f32[8,64,160]{2,1,0:T(8,128)S(1)}, f32[8,64,160]{2,1,0:T(8,128)}, u32[]{:S(2)}) copy-start(f32[8,64,160]{2,1,0:T(8,128)} %add.761) | copy-start | bytes 983044
  504.8 31.1 %copy-start.51 = (f32[4,160]{1,0:T(4,128)S(1)}, f32[4,160]{1,0:T(4,128)}, u32[]{:S(2)}) copy-start(f32[4,160]{1,0:T(4,128)} %custom-call.2) | copy-start | bytes 7684
  504.8 49.1 %copy-start.50 = (f32[4,160]{1,0:T(4,128)S(1)}, f32[4,160]{1,0:T(4,128)}, u32[]{:S(2)}) copy-start(f32[4,160]{1,0:T(4,128)} %custom-call.3) | copy-start | bytes 7684
  504.8 49.4 %copy-start.70 = (f32[8,1,160]{2,1,0:T(1,128)S(1)}, f32[8,1,160]{2,1,0:T(1,128)}, u32[]{:S(2)}) copy-start(f32[8,1,160]{2,1,0:T(1,128)} %broadcast_in_dim.172) | copy-start | bytes 15364
  563.6 59.1 %copy-start.104 = (u32[32]{0:T(128)S(1)}, u32[32]{0:T(128)}, u32[]{:S(2)}) copy-start(u32[32]{0:T(128)} %constant.344) | copy-start | bytes 388
  563.6 61.0 %copy-start.14 = (bf16[1024,160]{0,1:T(8,128)(2,1)S(1)}, bf16[1024,160]{0,1:T(8,128)(2,1)}, u32[]{:S(2)}) copy-start(bf16[1024,160]{0,1:T(8,128)(2,1)} %get-tuple-element.934) | copy-start | bytes 983044
  563.6 61.0 %copy-start.56 = (f32[1024]{0:T(1024)S(1)}, f32[1024]{0:T(1024)}, u32[]{:S(2)}) copy-start(f32[1024]{0:T(1024)} %get-tuple-element.1010) | copy-start | bytes 12292
  563.6 61.0 %copy-start.77 = (bf16[160,3]{0,1:T(4,128)(2,1)S(1)}, bf16[160,3]{0,1:T(4,128)(2,1)}, u32[]{:S(2)}) copy-start(bf16[160,3]{0,1:T(4,128)(2,1)} %copy-done.76) | copy-start | bytes 2884
  620.2 39.8 %reduce-scatter.23.cloned.1.call-start = ((), (), s32[]{:S(2)}) async-start(), calls=%async_computation.10 | async-start | bytes 102400 | tf_op jit(solution)/shard_map/reduce_scatter | solution.py:427
  620.8 58.7 %reduce-scatter.35.cloned.1.call-start = ((), (), s32[]{:S(2)}) async-start(), calls=%async_computation.16 | async-start | bytes 153600
  621.3 77.5 %reduce-scatter.33.cloned.1.call-start = ((), (), s32[]{:S(2)}) async-start(), calls=%async_computation.15 | async-start | bytes 153600
  621.9 96.5 %reduce-scatter.29.cloned.1.call-start = ((), (), s32[]{:S(2)}) async-start(), calls=%async_computation.13 | async-start | bytes 153600
  622.7 115.2 %reduce-scatter.31.cloned.1.call-start = ((), (), s32[]{:S(2)}) async-start(), calls=%async_computation.14 | async-start | bytes 153600
  625.4 132.8 %reduce-scatter.27.cloned.1.call-start = ((), (), s32[]{:S(2)}) async-start(), calls=%async_computation.12 | async-start | bytes 256000
  (87 other events, 259.9 us)
Sparse Core Ops, SparseCore 0:
  157.8 33.2 all-gather.12
  378.9 60.2 reduce-scatter.20
  620.3 19.5 reduce-scatter.24
  642.6 17.3 reduce-scatter.22
  662.2 17.2 reduce-scatter.34
  681.5 17.2 reduce-scatter.32
  701.2 17.2 reduce-scatter.28
  720.7 17.1 reduce-scatter.30
  740.3 17.8 reduce-scatter.26
where the time goes:
time: 780 us; the launch traced here: 767 us
  blocking collectives  278 us (36%)
  local copies, waits for them, and re-layouts  150 us (19%)
  waiting for transfers between devices  126 us (16%)
  matrix products  113 us (14%)
  other arithmetic  79.4 us (10%)
  between operations  18.3 us (2%)
    unnamed x14, waiting for transfers between devices  93.7 us
    all_gather x8, blocking collectives, entering(): pieces = jax.tree.map(lambda part: lax.all_gather(part, axis), value)  69.8 us
    psum x1, blocking collectives, shards(): lax.psum((grad_lstm, grad_glu_one, grad_qkv, grad_attn, grad_glu_two, gra...  54.8 us
    dot_general x8, matrix products, masked_scores(): jnp.einsum('gqhd,gkhd->ghqk', query_block, key_block, preferred_element_t...  29.6 us
    pad x24, local copies, waits for them, and re-layouts, shards(): lax.associative_scan(affine_join, (next_forget, direct_grad), axis=1, rev...  27.1 us
    slice x49, local copies, waits for them, and re-layouts, shards(): lax.associative_scan(affine_join, (next_forget, direct_grad), axis=1, rev...  26.3 us
    reduce_scatter x1, waiting for transfers between devices, shards(): lax.psum_scatter(key_terms.reshape(series_per_device, seq_total, model_wi...  24 us
    dot_general x4, matrix products, attend_backward(): jnp.einsum('ghqk,gkhd->gqhd', dscore, key_block, preferred_element_type=j...  21.4 us
  transfers between devices with their start and end apart: 9, of which 7 were waited for; matrix products, arithmetic and copies ran while one was open for 7% of the time, Pallas kernels for 0%

commit v1 on v0

--- a/solution.py
+++ b/solution.py
@@ -1,6 +1,10 @@
+import types
+
 import jax
 import jax.numpy as jnp
 from jax import lax
+from jax.experimental import pallas as pl
+from jax.experimental.pallas import tpu as pltpu
 from jax.sharding import PartitionSpec as P
 
 HEADS = 4
@@ -12,6 +16,8 @@
 EPSILON = 1e-05
 NEG_BIG = -1e30
 attend_group = 2
+LOG2_E = 1.4426950408889634
+VMEM_BYTES = 60 * 2**20
 
 
 def entering(value, axis, join, neutral, backward):
@@ -463,6 +469,655 @@
     )
 
 
+def lane_head(shape, head_width, head):
+    lane = lax.broadcasted_iota(jnp.int32, shape, len(shape) - 1)
+    return (lane >= head * head_width) & (lane < (head + 1) * head_width)
+
+
+FORGET, ENTER, CANDIDATE, EXIT = 0, 256, 512, 768
+GLU_ONE_A, GLU_ONE_B = 1024, 1280
+QUERY, KEY, VALUE = 1536, 1792, 2048
+GLU_TWO_A, GLU_TWO_B = 2176, 2432
+INNER, MIDDLE = 2688, 2944
+GLU_THREE_A, GLU_THREE_B = 3200, 3456
+ATTN_OUT = 3712
+PACKED = 3968
+VECTORS = 24
+LANES = 128
+CHUNKS = 8
+TILE = 256
+
+
+def nn(left, right):
+    return jnp.dot(left, right, preferred_element_type=jnp.float32)
+
+
+def nt(left, right):
+    return lax.dot_general(
+        left, right, (((1,), (1,)), ((), ())), preferred_element_type=jnp.float32
+    )
+
+
+def tn(left, right):
+    return lax.dot_general(
+        left, right, (((0,), (0,)), ((), ())), preferred_element_type=jnp.float32
+    )
+
+
+def low(values):
+    return values.astype(jnp.bfloat16)
+
+
+def sigmoid(values):
+    return 0.5 * jnp.tanh(0.5 * values) + 0.5
+
+
+def normalise(values, gain, shift):
+    centred = values - jnp.mean(values, axis=-1, keepdims=True)
+    spread = jnp.mean(centred * centred, axis=-1, keepdims=True)
+    inverse = lax.rsqrt(spread + EPSILON)
+    unit = centred * inverse
+    return unit * gain + shift, unit, inverse
+
+
+def normalise_back(grad, unit, inverse, gain):
+    scaled = grad * gain
+    return inverse * (
+        scaled
+        - jnp.mean(scaled, axis=-1, keepdims=True)
+        - unit * jnp.mean(scaled * unit, axis=-1, keepdims=True)
+    )
+
+
+def rows_of(tile, size=TILE):
+    return pl.ds(pl.multiple_of(tile * size, size), size)
+
+
+def put_halves(ref, rows, values):
+    ref[0, rows, :] = values[:, :LANES]
+    ref[1, rows, : values.shape[1] - LANES] = values[:, LANES:]
+
+
+def get_halves(ref, rows, width):
+    return jnp.concatenate([ref[0, rows, :], ref[1, rows, : width - LANES]], axis=1)
+
+
+def row_sum(ref, column, values):
+    ref[column : column + 1, :] += jnp.sum(values, axis=0, keepdims=True)
+
+
+def series_scratch(span, width, head_width):
+    full = pltpu.VMEM((span, width), jnp.float32)
+    half = pltpu.VMEM((span, width), jnp.bfloat16)
+    scan = pltpu.VMEM((2, span, LANES), jnp.float32)
+    scan_more = pltpu.VMEM((2, span + 8, LANES), jnp.float32)
+    narrow = pltpu.VMEM((span, head_width), jnp.bfloat16)
+    column = pltpu.VMEM((span, 1), jnp.float32)
+    return dict(
+        forget=scan_more,
+        local=scan,
+        mult=scan,
+        cell=scan_more,
+        carry=pltpu.VMEM((2, CHUNKS, LANES), jnp.float32),
+        enter_gate=full,
+        candidate=full,
+        exit_gate=full,
+        cell_tanh=full,
+        hidden=half,
+        glu_one=full,
+        gate_one=full,
+        unit_one=full,
+        inverse_one=column,
+        first_low=half,
+        queries=half,
+        keys=half,
+        values=narrow,
+        head_queries=pltpu.VMEM((HEADS, span, width), jnp.bfloat16),
+        head_keys=pltpu.VMEM((HEADS, span, width), jnp.bfloat16),
+        chances=pltpu.VMEM((HEADS, span, span), jnp.float32),
+        chance_sum=pltpu.VMEM((span, span), jnp.bfloat16),
+        score_grads=pltpu.VMEM((HEADS, span, span), jnp.bfloat16),
+        block=pltpu.VMEM((TILE, span), jnp.float32),
+        mixed=narrow,
+        mixed_grad=narrow,
+        sum_two_grad=full,
+        query_grad=half,
+        key_grad=half,
+        value_grad=narrow,
+        exit_grad=half,
+    )
+
+
+def series_forward_lstm(r, w, vec, x_ref, begin):
+    span, width = x_ref.shape
+
+    def gates(tile, _):
+        rows = rows_of(tile)
+        x = x_ref[rows, :]
+
+        def pre(block, column):
+            return nn(x, w[:, block : block + width]) + vec[column : column + 1, :]
+
+        time = tile * TILE + lax.broadcasted_iota(jnp.int32, (TILE, width), 0)
+        forget = jnp.where(time != begin, sigmoid(pre(FORGET, 0)), 0.0)
+        enter = sigmoid(pre(ENTER, 1))
+        candidate = jnp.tanh(pre(CANDIDATE, 2))
+        r.enter_gate[rows, :] = enter
+        r.candidate[rows, :] = candidate
+        r.exit_gate[rows, :] = sigmoid(pre(EXIT, 3))
+        put_halves(r.forget, rows, forget)
+        put_halves(r.local, rows, enter * candidate)
+        return 0
+
+    lax.fori_loop(0, span // TILE, gates, 0)
+    steps = span // CHUNKS
+    zeros = jnp.zeros((CHUNKS, LANES), jnp.float32)
+
+    def step(t, state):
+        out = []
+        at = pl.ds(t, CHUNKS, stride=steps)
+        for half in range(2):
+            cell, mult = state[half]
+            forget = r.forget[half, at, :]
+            cell = forget * cell + r.local[half, at, :]
+            mult = mult * forget
+            r.local[half, at, :] = cell
+            r.mult[half, at, :] = mult
+            out.append((cell, mult))
+        return tuple(out)
+
+    ends = lax.fori_loop(0, steps, step, ((zeros, zeros + 1.0),) * 2, unroll=8)
+    for half in range(2):
+        cells, mults = ends[half]
+        state = jnp.zeros((1, LANES), jnp.float32)
+        r.carry[half, 0:1, :] = state
+        for chunk in range(CHUNKS - 1):
+            state = cells[chunk : chunk + 1] + mults[chunk : chunk + 1] * state
+            r.carry[half, chunk + 1 : chunk + 2, :] = state
+        r.cell[half, 0:8, :] = zeros
+
+
+def series_forward_first(r, w, vec, x_ref):
+    span, width = x_ref.shape
+    head_width = width // HEADS
+    steps = span // CHUNKS
+
+    def cells(chunk, _):
+        rows = rows_of(chunk, steps)
+        later = pl.ds(pl.multiple_of(chunk * steps + 8, 8), steps)
+        for half in range(2):
+            r.cell[half, later, :] = r.local[half, rows, :] + r.mult[half, rows, :] * r.carry[
+                half, pl.ds(chunk, 1), :
+            ]
+        tanh = jnp.tanh(get_halves(r.cell, later, width))
+        r.cell_tanh[rows, :] = tanh
+        r.hidden[rows, :] = low(r.exit_gate[rows, :] * tanh)
+        return 0
+
+    lax.fori_loop(0, CHUNKS, cells, 0)
+
+    def first(tile, _):
+        rows = rows_of(tile)
+        hidden = r.hidden[rows, :]
+        value = nn(hidden, w[:, GLU_ONE_A : GLU_ONE_A + width]) + vec[4:5, :]
+        gate = sigmoid(nn(hidden, w[:, GLU_ONE_B : GLU_ONE_B + width]) + vec[5:6, :])
+        r.glu_one[rows, :] = value
+        r.gate_one[rows, :] = gate
+        out, unit, inverse = normalise(
+            x_ref[rows, :].astype(jnp.float32) + value * gate, vec[6:7, :], vec[7:8, :]
+        )
+        r.unit_one[rows, :] = unit
+        r.inverse_one[rows, :] = inverse
+        out = low(out)
+        r.first_low[rows, :] = out
+        query = low(nn(out, w[:, QUERY : QUERY + width]))
+        key = low(nn(out, w[:, KEY : KEY + width]))
+        r.keys[rows, :] = key
+        r.values[rows, :] = low(nn(out, w[:, VALUE : VALUE + head_width]))
+        for head in range(HEADS):
+            mine = lane_head((TILE, width), head_width, head)
+            r.head_queries[head, rows, :] = jnp.where(mine, query, jnp.zeros_like(query))
+            r.head_keys[head, rows, :] = jnp.where(mine, key, jnp.zeros_like(key))
+        return 0
+
+    lax.fori_loop(0, span // TILE, first, 0)
+
+
+def series_forward_attention(r, begin):
+    span, head_width = r.values.shape
+    scale = head_width ** (-0.5) * LOG2_E
+    for tile in range(span // TILE):
+        rows = slice(tile * TILE, (tile + 1) * TILE)
+        seen = (tile + 1) * TILE
+        row = tile * TILE + lax.broadcasted_iota(jnp.int32, (TILE, seen), 0)
+        col = lax.broadcasted_iota(jnp.int32, (TILE, seen), 1)
+        r.block[:, :seen] = jnp.where(
+            (col <= row) & (col >= jnp.minimum(begin, row)), 0.0, NEG_BIG
+        )
+
+        def one_head(head, _):
+            scores = (
+                nt(r.head_queries[head, rows, :], r.keys[:seen, :]) * scale + r.block[:, :seen]
+            )
+            top = jnp.max(scores, axis=-1, keepdims=True)
+            raised = jnp.exp2(scores - top)
+            total = jnp.sum(raised, axis=-1, keepdims=True)
+            r.chances[head, rows, :seen] = raised * (1.0 / total)
+            return 0
+
+        lax.fori_loop(0, HEADS, one_head, 0)
+        weights = r.chances[0, rows, :seen]
+        for head in range(1, HEADS):
+            weights = weights + r.chances[head, rows, :seen]
+        weights = low(weights)
+        r.chance_sum[rows, :seen] = weights
+        r.mixed[rows, :] = low(nn(weights, r.values[:seen, :]) * (1.0 / HEADS))
+
+
+def series_middle(r, w, vec, level, adjoint_ref, slope_ref, horizon, out_ref, predicted_ref, g, gv):
+    span, width = out_ref.shape
+    head_width = width // HEADS
+
+    def middle(tile, last):
+        rows = rows_of(tile)
+        first = r.unit_one[rows, :] * vec[6:7, :] + vec[7:8, :]
+        mixed = r.mixed[rows, :]
+        attn = low(nn(mixed, w[:head_width, ATTN_OUT : ATTN_OUT + width]))
+        value_two = nn(attn, w[:, GLU_TWO_A : GLU_TWO_A + width]) + vec[8:9, :]
+        gate_two = sigmoid(nn(attn, w[:, GLU_TWO_B : GLU_TWO_B + width]) + vec[9:10, :])
+        second, unit_two, inverse_two = normalise(
+            first + value_two * gate_two, vec[10:11, :], vec[11:12, :]
+        )
+        second_low = low(second)
+        inner_pre = nn(second_low, w[:, INNER : INNER + width]) + vec[12:13, :]
+        inner_exp = jnp.exp(jnp.minimum(inner_pre, 0.0))
+        inner_low = low(jnp.where(inner_pre > 0, inner_pre, inner_exp - 1.0))
+        middle_low = low(nn(inner_low, w[:, MIDDLE : MIDDLE + width]) + vec[13:14, :])
+        value_three = nn(middle_low, w[:, GLU_THREE_A : GLU_THREE_A + width]) + vec[14:15, :]
+        gate_three = sigmoid(
+            nn(middle_low, w[:, GLU_THREE_B : GLU_THREE_B + width]) + vec[15:16, :]
+        )
+        final, unit_three, inverse_three = normalise(
+            second + value_three * gate_three, vec[16:17, :], vec[17:18, :]
+        )
+        final_low = low(final)
+        out_ref[rows, :] = final_low
+        grad = adjoint_ref[rows, :].astype(jnp.float32)
+        if last:
+            start = span - TILE
+            time = start + lax.broadcasted_iota(jnp.int32, (8, TILE), 1)
+            ahead = jnp.where((time >= span - DEC) & (time < span - DEC + horizon), 1.0, 0.0)
+            predicted_ref[:, :start] = jnp.zeros((8, start), jnp.float32)
+            predicted_ref[:, start:] = nt(level[...], final_low) * ahead
+            slope = low(slope_ref[:, start:].astype(jnp.float32) * ahead)
+            gv[VECTORS:, :] = nn(slope, final_low)
+            grad = grad + tn(slope, level[...])
+        row_sum(gv, 16, grad * unit_three)
+        row_sum(gv, 17, grad)
+        sum_three = normalise_back(grad, unit_three, inverse_three, vec[16:17, :])
+        grad_a = sum_three * gate_three
+        grad_b = grad_a * value_three * (1.0 - gate_three)
+        row_sum(gv, 14, grad_a)
+        row_sum(gv, 15, grad_b)
+        low_a, low_b = low(grad_a), low(grad_b)
+        g[:, GLU_THREE_A : GLU_THREE_A + width] += tn(middle_low, low_a)
+        g[:, GLU_THREE_B : GLU_THREE_B + width] += tn(middle_low, low_b)
+        middle_grad = nt(low_a, w[:, GLU_THREE_A : GLU_THREE_A + width]) + nt(
+            low_b, w[:, GLU_THREE_B : GLU_THREE_B + width]
+        )
+        row_sum(gv, 13, middle_grad)
+        middle_grad = low(middle_grad)
+        g[:, MIDDLE : MIDDLE + width] += tn(inner_low, middle_grad)
+        inner_grad = nt(middle_grad, w[:, MIDDLE : MIDDLE + width]) * jnp.where(
+            inner_pre > 0, 1.0, inner_exp
+        )
+        row_sum(gv, 12, inner_grad)
+        inner_grad = low(inner_grad)
+        g[:, INNER : INNER + width] += tn(second_low, inner_grad)
+        grad = sum_three + nt(inner_grad, w[:, INNER : INNER + width])
+        row_sum(gv, 10, grad * unit_two)
+        row_sum(gv, 11, grad)
+        sum_two = normalise_back(grad, unit_two, inverse_two, vec[10:11, :])
+        r.sum_two_grad[rows, :] = sum_two
+        grad_a = sum_two * gate_two
+        grad_b = grad_a * value_two * (1.0 - gate_two)
+        row_sum(gv, 8, grad_a)
+        row_sum(gv, 9, grad_b)
+        low_a, low_b = low(grad_a), low(grad_b)
+        g[:, GLU_TWO_A : GLU_TWO_A + width] += tn(attn, low_a)
+        g[:, GLU_TWO_B : GLU_TWO_B + width] += tn(attn, low_b)
+        attn_grad = low(
+            nt(low_a, w[:, GLU_TWO_A : GLU_TWO_A + width])
+            + nt(low_b, w[:, GLU_TWO_B : GLU_TWO_B + width])
+        )
+        g[:head_width, ATTN_OUT : ATTN_OUT + width] += tn(mixed, attn_grad)
+        r.mixed_grad[rows, :] = low(nt(attn_grad, w[:head_width, ATTN_OUT : ATTN_OUT + width]))
+        return 0
+
+    lax.fori_loop(0, span // TILE - 1, lambda tile, _: middle(tile, False), 0)
+    middle(span // TILE - 1, True)
+
+
+def series_backward_attention(r):
+    span, head_width = r.values.shape
+    width = head_width * HEADS
+    scale = head_width ** (-0.5)
+    for tile in range(span // TILE):
+        rows = slice(tile * TILE, (tile + 1) * TILE)
+        seen = (tile + 1) * TILE
+        head_grad = r.mixed_grad[rows, :] * (1.0 / HEADS)
+        r.block[:, :seen] = nt(head_grad, r.values[:seen, :]) * scale
+
+        def one_head(head, total):
+            chances = r.chances[head, rows, :seen]
+            slope = r.block[:, :seen]
+            delta = jnp.sum(chances * slope, axis=-1, keepdims=True)
+            grads = low(chances * (slope - delta))
+            r.score_grads[head, rows, :seen] = grads
+            return total + nn(grads, r.head_keys[head, :seen, :])
+
+        r.query_grad[rows, :] = low(
+            lax.fori_loop(0, HEADS, one_head, jnp.zeros((TILE, width), jnp.float32))
+        )
+    for tile in range(span // TILE):
+        cols = slice(tile * TILE, (tile + 1) * TILE)
+        start = tile * TILE
+
+        def one_key(head, total):
+            return total + tn(
+                r.score_grads[head, start:, cols], r.head_queries[head, start:, :]
+            )
+
+        r.key_grad[cols, :] = low(
+            lax.fori_loop(0, HEADS, one_key, jnp.zeros((TILE, width), jnp.float32))
+        )
+        r.value_grad[cols, :] = low(
+            tn(r.chance_sum[start:, cols], r.mixed_grad[start:, :] * (1.0 / HEADS))
+        )
+
+
+def series_backward_first(r, w, vec, g, gv):
+    span, width = r.hidden.shape
+    head_width = width // HEADS
+
+    def back(tile, _):
+        rows = rows_of(tile)
+        query, key, value = r.query_grad[rows, :], r.key_grad[rows, :], r.value_grad[rows, :]
+        grad = (
+            r.sum_two_grad[rows, :]
+            + nt(query, w[:, QUERY : QUERY + width])
+            + nt(key, w[:, KEY : KEY + width])
+            + nt(value, w[:, VALUE : VALUE + head_width])
+        )
+        first = r.first_low[rows, :]
+        g[:, QUERY : QUERY + width] += tn(first, query)
+        g[:, KEY : KEY + width] += tn(first, key)
+        g[:, VALUE : VALUE + head_width] += tn(first, value)
+        unit = r.unit_one[rows, :]
+        row_sum(gv, 6, grad * unit)
+        row_sum(gv, 7, grad)
+        sum_one = normalise_back(grad, unit, r.inverse_one[rows, :], vec[6:7, :])
+        r.sum_two_grad[rows, :] = sum_one
+        gate = r.gate_one[rows, :]
+        grad_a = sum_one * gate
+        grad_b = grad_a * r.glu_one[rows, :] * (1.0 - gate)
+        row_sum(gv, 4, grad_a)
+        row_sum(gv, 5, grad_b)
+        low_a, low_b = low(grad_a), low(grad_b)
+        hidden = r.hidden[rows, :]
+        g[:, GLU_ONE_A : GLU_ONE_A + width] += tn(hidden, low_a)
+        g[:, GLU_ONE_B : GLU_ONE_B + width] += tn(hidden, low_b)
+        hidden_grad = nt(low_a, w[:, GLU_ONE_A : GLU_ONE_A + width]) + nt(
+            low_b, w[:, GLU_ONE_B : GLU_ONE_B + width]
+        )
+        tanh, gate = r.cell_tanh[rows, :], r.exit_gate[rows, :]
+        put_halves(r.local, rows, hidden_grad * gate * (1.0 - tanh * tanh))
+        exit_grad = hidden_grad * tanh * gate * (1.0 - gate)
+        row_sum(gv, 3, exit_grad)
+        r.exit_grad[rows, :] = low(exit_grad)
+        return 0
+
+    lax.fori_loop(0, span // TILE, back, 0)
+
+
+def series_backward_lstm(r, w, x_ref, input_grad_ref, g, gv):
+    span, width = x_ref.shape
+    steps = span // CHUNKS
+    zeros = jnp.zeros((CHUNKS, LANES), jnp.float32)
+    for half in range(2):
+        r.forget[half, span:, :] = zeros
+
+    def step(count, state):
+        t = steps - 1 - count
+        out = []
+        at, after = pl.ds(t, CHUNKS, stride=steps), pl.ds(t + 1, CHUNKS, stride=steps)
+        for half in range(2):
+            grad, mult = state[half]
+            forget = r.forget[half, after, :]
+            grad = forget * grad + r.local[half, at, :]
+            mult = mult * forget
+            r.local[half, at, :] = grad
+            r.mult[half, at, :] = mult
+            out.append((grad, mult))
+        return tuple(out)
+
+    ends = lax.fori_loop(0, steps, step, ((zeros, zeros + 1.0),) * 2, unroll=8)
+    for half in range(2):
+        grads, mults = ends[half]
+        state = jnp.zeros((1, LANES), jnp.float32)
+        r.carry[half, CHUNKS - 1 : CHUNKS, :] = state
+        for chunk in range(CHUNKS - 1, 0, -1):
+            state = grads[chunk : chunk + 1] + mults[chunk : chunk + 1] * state
+            r.carry[half, chunk - 1 : chunk, :] = state
+
+    def back(chunk, _):
+        rows = rows_of(chunk, steps)
+        before = pl.ds(chunk * steps + 7, steps)
+        grad, grad_forget = [], []
+        for half in range(2):
+            one = r.local[half, rows, :] + r.mult[half, rows, :] * r.carry[
+                half, pl.ds(chunk, 1), :
+            ]
+            forget = r.forget[half, rows, :]
+            grad.append(one)
+            grad_forget.append(one * r.cell[half, before, :] * forget * (1.0 - forget))
+        grad = jnp.concatenate([grad[0], grad[1][:, : width - LANES]], axis=1)
+        grad_forget = jnp.concatenate([grad_forget[0], grad_forget[1][:, : width - LANES]], axis=1)
+        enter, candidate = r.enter_gate[rows, :], r.candidate[rows, :]
+        grad_enter = grad * candidate * enter * (1.0 - enter)
+        grad_candidate = grad * enter * (1.0 - candidate * candidate)
+        row_sum(gv, 0, grad_forget)
+        row_sum(gv, 1, grad_enter)
+        row_sum(gv, 2, grad_candidate)
+        x = x_ref[rows, :]
+        out = r.sum_two_grad[rows, :]
+        for block, one in (
+            (FORGET, low(grad_forget)),
+            (ENTER, low(grad_enter)),
+            (CANDIDATE, low(grad_candidate)),
+            (EXIT, r.exit_grad[rows, :]),
+        ):
+            g[:, block : block + width] += tn(x, one)
+            out = out + nt(one, w[:, block : block + width])
+        input_grad_ref[rows, :] = low(out)
+        return 0
+
+    lax.fori_loop(0, CHUNKS, back, 0)
+
+
+def series_kernel(
+    scalars,
+    x_ref,
+    adjoint_ref,
+    slope_ref,
+    w,
+    vec,
+    level,
+    out_ref,
+    predicted_ref,
+    input_grad_ref,
+    g,
+    gv,
+    *scratch,
+):
+    span, width = x_ref.shape
+    names = series_scratch(span, width, width // HEADS)
+    r = types.SimpleNamespace(**dict(zip(names, scratch)))
+    begin, horizon = scalars[0], scalars[1]
+    g[...] = jnp.zeros_like(g)
+    gv[...] = jnp.zeros_like(gv)
+    series_forward_lstm(r, w, vec, x_ref, begin)
+    series_forward_first(r, w, vec, x_ref)
+    series_forward_attention(r, begin)
+    series_middle(
+        r, w, vec, level, adjoint_ref, slope_ref, horizon, out_ref, predicted_ref, g, gv
+    )
+    series_backward_attention(r)
+    series_backward_first(r, w, vec, g, gv)
+    series_backward_lstm(r, w, x_ref, input_grad_ref, g, gv)
+
+
+def pack_weights(parts, width):
+    (lstm, glu_one, qkv, glu_two, inner, middle, glu_three) = parts
+    half = 2 * LANES
+
+    def spread(array, block):
+        return [
+            jnp.pad(array[:, at : at + block], ((0, 0), (0, half - block)))
+            for at in range(0, array.shape[1], block)
+        ]
+
+    pieces = spread(lstm, width) + spread(glu_one, width) + spread(qkv[:, : 2 * width], width)
+    pieces.append(jnp.pad(qkv[:, 2 * width :], ((0, 0), (0, LANES - (qkv.shape[1] - 2 * width)))))
+    pieces += spread(glu_two, width) + spread(inner, width) + spread(middle, width)
+    pieces += spread(glu_three, width)
+    return jnp.concatenate(pieces, axis=1)
+
+
+def whole_series(
+    embedded_features,
+    earliest_seen_moment,
+    reach_choice,
+    lstm_valve_coeffs,
+    lstm_unit_coeffs,
+    asker_lookup_coeffs,
+    attend_exit_coeffs,
+    attend_unit_coeffs,
+    skipnet_entry_coeffs,
+    skipnet_inner_coeffs,
+    skipnet_unit_coeffs,
+    level_map_coeffs,
+    bias_gain_table,
+    block_emit_adjoint,
+    predicted_adjoint,
+):
+    count, steps, width = embedded_features.shape
+    span = count * steps
+    head_width = width // HEADS
+    mine = lax.axis_index("tm")
+
+    def to_series(array, axis):
+        return lax.all_to_all(array, "tm", split_axis=0, concat_axis=axis, tiled=True)
+
+    def to_time(array, axis):
+        return lax.all_to_all(array, "tm", split_axis=axis, concat_axis=0, tiled=True)
+
+    x = to_series(embedded_features, 1)[0]
+    adjoint = to_series(block_emit_adjoint, 1)[0]
+    slope = jnp.pad(to_series(predicted_adjoint, 2)[0], ((0, 8 - LEVEL_TALLY), (0, 0)))
+    packed = pack_weights(
+        [
+            narrow_convert(array)
+            for array in (
+                lstm_valve_coeffs,
+                lstm_unit_coeffs,
+                asker_lookup_coeffs,
+                attend_unit_coeffs,
+                skipnet_entry_coeffs,
+                skipnet_inner_coeffs,
+                skipnet_unit_coeffs,
+            )
+        ],
+        width,
+    )
+    packed = lax.all_gather(packed, "dp", axis=0, tiled=True)
+    attn_out = lax.all_gather(narrow_convert(attend_exit_coeffs), "dp", axis=0, tiled=True)
+    packed = jnp.concatenate(
+        [
+            packed,
+            jnp.pad(attn_out, ((0, width - head_width), (0, PACKED - ATTN_OUT - width))),
+        ],
+        axis=1,
+    )
+    columns = lax.all_gather(
+        narrow_convert(jnp.concatenate([bias_gain_table, level_map_coeffs], axis=1)),
+        "dp",
+        axis=0,
+        tiled=True,
+    )
+    vectors = bias_gain_table.shape[1]
+    vec = jnp.pad(columns[:, :vectors].astype(jnp.float32).T, ((0, VECTORS - vectors), (0, 0)))
+    level = jnp.pad(columns[:, vectors:].T, ((0, 8 - LEVEL_TALLY), (0, 0)))
+    begin = earliest_seen_moment[mine]
+    choice = reach_choice[mine]
+    horizon = jnp.where(choice == 0, 1, jnp.where(choice == 1, 5, 24))
+    out, predicted, input_grad, g, gv = pl.pallas_call(
+        series_kernel,
+        out_shape=(
+            jax.ShapeDtypeStruct((span, width), jnp.bfloat16),
+            jax.ShapeDtypeStruct((8, span), jnp.float32),
+            jax.ShapeDtypeStruct((span, width), jnp.bfloat16),
+            jax.ShapeDtypeStruct((width, PACKED), jnp.float32),
+            jax.ShapeDtypeStruct((VECTORS + 8, width), jnp.float32),
+        ),
+        in_specs=[pl.BlockSpec(memory_space=pltpu.SMEM)]
+        + [pl.BlockSpec(memory_space=pltpu.VMEM)] * 6,
+        out_specs=(pl.BlockSpec(memory_space=pltpu.VMEM),) * 5,
+        scratch_shapes=list(series_scratch(span, width, head_width).values()),
+        compiler_params=pltpu.CompilerParams(vmem_limit_bytes=VMEM_BYTES),
+    )(jnp.stack([begin, horizon]), x, adjoint, slope, packed, vec, level)
+    emitted = to_time(out[None], 1)
+    input_out = to_time(input_grad[None], 1)
+    levels = to_time(predicted[None, :LEVEL_TALLY], 2)
+    vector_columns = gv.T
+    whole = lax.psum(
+        jnp.concatenate([g[:, :ATTN_OUT], vector_columns], axis=1), "tm"
+    )
+    whole = lax.psum_scatter(
+        whole.astype(jnp.bfloat16), "dp", scatter_dimension=0, tiled=True
+    ).astype(jnp.float32)
+    attn_whole = lax.psum_scatter(
+        lax.psum(g[:head_width, ATTN_OUT : ATTN_OUT + width], "tm").astype(jnp.bfloat16),
+        "dp",
+        scatter_dimension=0,
+        tiled=True,
+    ).astype(jnp.float32)
+
+    def gather(*starts):
+        return jnp.concatenate([whole[:, at : at + width] for at in starts], axis=1)
+
+    return (
+        emitted,
+        levels,
+        input_out,
+        gather(FORGET, ENTER, CANDIDATE, EXIT),
+        gather(GLU_ONE_A, GLU_ONE_B),
+        jnp.concatenate([gather(QUERY, KEY), whole[:, VALUE : VALUE + head_width]], axis=1),
+        attn_whole,
+        gather(GLU_TWO_A, GLU_TWO_B),
+        whole[:, INNER : INNER + width],
+        whole[:, MIDDLE : MIDDLE + width],
+        gather(GLU_THREE_A, GLU_THREE_B),
+        whole[:, ATTN_OUT + VECTORS : ATTN_OUT + VECTORS + LEVEL_TALLY],
+        whole[:, ATTN_OUT : ATTN_OUT + vectors],
+    )
+
+
+def on_device(embedded_features, *others):
+    one_each = embedded_features.shape[0] == lax.axis_size("tm")
+    return (whole_series if one_each else shards)(embedded_features, *others)
+
+
 def solution(mesh):
     placed = (
         P("dp", "tm", None),
@@ -482,7 +1137,7 @@
         P("dp", None, "tm"),
     )
     return jax.shard_map(
-        shards,
+        on_device,
         mesh=mesh,
         in_specs=placed,
         out_specs=(

time: 780 us -> 273 us (0.35); the launches traced: 767 us -> 271 us
  blocking collectives: 278 us -> 104 us
  local copies, waits for them, and re-layouts: 150 us -> 30.7 us
  waiting for transfers between devices: 126 us -> 12.3 us
  matrix products: 113 us -> 0 us
  Pallas kernels: 0 us -> 52.9 us
  other arithmetic: 79.4 us -> 31.6 us
  starting transfers between devices: 0.36 us -> 23.8 us
    all_gather x18 -> x2, blocking collectives: 204 us -> 26.6 us  [the longest x1 13.5 us: whole_series(): lax.all_gather(narrow_convert(jnp.concatenate([bias_gain_table, level_map...]
    dot_general x55 -> x0, matrix products: 113 us -> none  [the longest x8 29.6 us: masked_scores(): jnp.einsum('gqhd,gkhd->ghqk', query_block, key_block, preferred_element_t...]
    unnamed x14 -> x2, waiting for transfers between devices: 93.7 us -> 0.03 us
    pallas_call x0 -> x1, Pallas kernels: none -> 52.9 us  [whole_series(): pl.pallas_call(series_kernel, out_shape=(jax.ShapeDtypeStruct((span, widt...]
    pad x48 -> x2, local copies, waits for them, and re-layouts: 43.9 us -> 1.21 us  [the longest x1 0.61 us: whole_series(): jnp.pad(to_series(predicted_adjoint, 2)[0], ((0, 8 - LEVEL_TALLY), (0, 0)))]
    slice x104 -> x12, local copies, waits for them, and re-layouts: 46.5 us -> 8.3 us  [the longest x1 3.25 us: whole_series(): g[:, :ATTN_OUT]]
    reduce_scatter x3 -> x1, waiting for transfers between devices: 32.3 us -> 0.01 us  [whole_series(): lax.psum_scatter(whole.astype(jnp.bfloat16), 'dp', scatter_dimension=0, t...]
    all_to_all x0 -> x6, starting transfers between devices: none -> 23.7 us  [the longest x3 12.7 us: to_series(): lax.all_to_all(array, 'tm', split_axis=0, concat_axis=axis, tiled=True)]
  transfers between devices with their start and end apart: 9 -> 8, of which waited for: 7 -> 3; matrix products, arithmetic and copies ran while one was open for 7% -> 13% of each run, Pallas kernels for 0% -> 0%
where the time goes in v1:
time: 273 us; the launch traced here: 271 us
  blocking collectives  104 us (38%)
  Pallas kernels  52.9 us (19%)
  other arithmetic  31.6 us (12%)
  local copies, waits for them, and re-layouts  30.7 us (11%)
  starting transfers between devices  23.8 us (9%)
  between operations  16.3 us (6%)
  waiting for transfers between devices  12.3 us (5%)
    psum x1, blocking collectives, whole_series(): lax.psum(jnp.concatenate([g[:, :ATTN_OUT], vector_columns], axis=1), 'tm')  57.9 us
    pallas_call x1, Pallas kernels, whole_series(): pl.pallas_call(series_kernel, out_shape=(jax.ShapeDtypeStruct((span, widt...  52.9 us
    unnamed x1, blocking collectives  19.1 us
    unnamed x10, other arithmetic  14.1 us
    unnamed x39, local copies, waits for them, and re-layouts  13.7 us
    all_gather x1, blocking collectives, whole_series(): lax.all_gather(narrow_convert(jnp.concatenate([bias_gain_table, level_map...  13.5 us
    all_gather x1, blocking collectives, whole_series(): lax.all_gather(narrow_convert(attend_exit_coeffs), 'dp', axis=0, tiled=True)  13.1 us
    all_to_all x3, starting transfers between devices, to_series(): lax.all_to_all(array, 'tm', split_axis=0, concat_axis=axis, tiled=True)  12.7 us
  transfers between devices with their start and end apart: 8, of which 3 were waited for; matrix products, arithmetic and copies ran while one was open for 13% of the time, Pallas kernels for 0%

profile of v1, /device:TPU:0, one launch (start us, length us, event | category | flops | bytes accessed | tf_op | source)
XLA Modules:
  0.0 271.3 jit_solution(17701929631952533026)
XLA Ops:
  17.7 1.3 copy.59
  19.0 5.2 %all-to-all-start.2 = ((bf16[8,3,128]{2,1,0:T(4,128)(2,1)}), bf16[8,3,128]{2,1,0:T(4,128)(2,1)S(1)}, u32[]{:S(2)}, u32[]{:S(2)}) async-start(bf16[8,3,128]{2,1,0:T(4,128)(2,1)} %copy.59), calls=%async_computation.2 | async-start | bytes 16384 | tf_op jit(solution)/shard_map/all_to_all | solution.py:1020
  25.6 1.2 dynamic_slice.7
  27.5 13.5 %all-gather.1 = bf16[4,40,21]{1,2,0:T(8,128)(2,1)S(1)} all-gather(bf16[1,40,21]{1,2,0:T(8,128)(2,1)S(1)} %maximum_bitcast_fusion), channel_id=1, replica_groups=mesh['tm'=8,'dp'=4] {'dp'}, dimensions={0}, use_global_device_ids=true | all-gather | bytes 8400 | tf_op jit(solution)/shard_map/all_gather | solution.py:1052
  42.4 1.2 dynamic_slice.6
  43.8 13.1 %all-gather = bf16[4,10,160]{2,1,0:T(8,128)(2,1)S(1)} all-gather(bf16[1,10,160]{2,1,0:T(8,128)(2,1)S(1)} %convert_bitcast_fusion), channel_id=1, replica_groups=mesh['tm'=8,'dp'=4] {'dp'}, dimensions={0}, use_global_device_ids=true | all-gather | bytes 16000 | tf_op jit(solution)/shard_map/all_gather | solution.py:1044
  56.9 4.1 %all-to-all-start.1 = ((bf16[8,128,160]{1,2,0:T(8,128)(2,1)}), bf16[8,128,160]{1,2,0:T(8,128)(2,1)S(1)}, u32[]{:S(2)}, u32[]{:S(2)}) async-start(bf16[8,128,160]{1,2,0:T(8,128)(2,1)} %param.28), calls=%async_computation.1 | async-start | bytes 655360 | tf_op jit(solution)/shard_map/all_to_all | solution.py:1020
  61.6 1.2 pad_add_fusion.scalars
  62.8 5.8 %all-to-all-done.1 = bf16[8,128,160]{1,2,0:T(8,128)(2,1)S(1)} async-done(((bf16[8,128,160]{1,2,0:T(8,128)(2,1)}), bf16[8,128,160]{1,2,0:T(8,128)(2,1)S(1)}, u32[]{:S(2)}, u32[]{:S(2)}) %all-to-all-start.1) | async-done | bytes 327712 | tf_op jit(solution)/shard_map/all_to_all | solution.py:1020
  68.6 3.4 %all-to-all-start = ((bf16[8,128,160]{1,2,0:T(8,128)(2,1)}), bf16[8,128,160]{1,2,0:T(8,128)(2,1)S(1)}, u32[]{:S(2)}, u32[]{:S(2)}) async-start(bf16[8,128,160]{1,2,0:T(8,128)(2,1)} %param.15), calls=%async_computation | async-start | bytes 655360 | tf_op jit(solution)/shard_map/all_to_all | solution.py:1020
  73.4 1.0 copy.58
  74.4 5.3 %all-to-all-done = bf16[8,128,160]{1,2,0:T(8,128)(2,1)S(1)} async-done(((bf16[8,128,160]{1,2,0:T(8,128)(2,1)}), bf16[8,128,160]{1,2,0:T(8,128)(2,1)S(1)}, u32[]{:S(2)}, u32[]{:S(2)}) %all-to-all-start) | async-done | bytes 327712 | tf_op jit(solution)/shard_map/all_to_all | solution.py:1020
  79.6 1.0 copy.57
  80.7 2.4 fusion.1.w
  83.1 52.9 %shard_map.246 = (bf16[1024,160]{1,0:T(8,128)(2,1)}, f32[8,1024]{1,0:T(8,128)}, bf16[1024,160]{1,0:T(8,128)(2,1)}, f32[160,3968]{1,0:T(8,128)}, f32[32,160]{1,0:T(8,128)}) custom-call(s32[2]{0:T(128)} %pad_add_fusion.scalars, bf16[1024,160]{1,0:T(8,128)(2,1)} %bitcast.49, bf16[1024,160]{1,0:T(8,128)(2,1)} %bitcast.48, bf16[8,1024]{1,0:T(8,128)(2,1)} %pad.65.slope_ref, ...), custom_call_target="tpu_custom_call" | custom-call | tf_op jit(solution)/shard_map/pallas_call | solution.py:1064
  136.8 3.2 %slice.129 = f32[160,3712]{1,0:T(8,128)} slice(f32[160,3968]{1,0:T(8,128)} %get-tuple-element.21), slice={[0:160], [0:3712]} | slice | bytes 4751360 | tf_op jit(solution)/shard_map/slice | solution.py:1084
  140.2 1.8 pad_maximum_fusion
  142.0 57.9 %all-reduce.17 = (bf16[160,3744]{1,0:T(8,128)(2,1)}, bf16[40,160]{1,0:T(8,128)(2,1)S(1)}) all-reduce(f32[160,3744]{1,0:T(8,128)S(1)} %pad_maximum_fusion, f32[40,160]{1,0:T(8,128)S(1)} %slice.139), channel_id=1, replica_groups=mesh['tm'=8,'dp'=4] {'tm'}, use_global_device_ids=true, to_apply=%region_0.1 | all-reduce | flops 605440 | bytes 3632640 | tf_op jit(solution)/shard_map/psum | solution.py:1083
  200.9 1.9 reduce.1
  202.8 1.0 reshape.60
  203.8 3.5 %all-to-all-start.4 = ((f32[8,1,384]{2,1,0:T(1,128)}), f32[8,1,384]{2,1,0:T(1,128)S(1)}, u32[]{:S(2)}, u32[]{:S(2)}) async-start(f32[8,1,384]{2,1,0:T(1,128)} %reshape.60), calls=%async_computation.4 | async-start | bytes 24576 | tf_op jit(solution)/shard_map/all_to_all | solution.py:1023
  208.6 4.0 %reduce = bf16[1024,160]{1,0:T(8,128)(2,1)S(1)} reduce(bf16[1024,1,160]{2,1,0:T(2,128)(2,1)S(1)} %bitcast.40, bf16[]{:T(256)} %broadcast.66), dimensions={1}, to_apply=%bitcast.39.reduce_sub_computation | reduce | bytes 655362
  212.6 1.5 reshape.58
  214.2 4.1 %all-to-all-start.3 = ((bf16[8,2,10240]{2,1,0:T(2,128)(2,1)}), bf16[8,2,10240]{2,1,0:T(2,128)(2,1)S(1)}, u32[]{:S(2)}, u32[]{:S(2)}) async-start(bf16[8,2,10240]{2,1,0:T(2,128)(2,1)} %reshape.58), calls=%async_computation.3 | async-start | bytes 655360 | tf_op jit(solution)/shard_map/all_to_all | solution.py:1023
  219.1 4.0 %reduce.3 = bf16[1024,160]{1,0:T(8,128)(2,1)S(1)} reduce(bf16[1024,1,160]{2,1,0:T(2,128)(2,1)S(1)} %bitcast.41, bf16[]{:T(256)} %broadcast.66), dimensions={1}, to_apply=%bitcast.38.reduce_sub_computation | reduce | bytes 655362
  223.2 1.5 reshape.62
  224.7 1.2 all-to-all-done.3
  225.9 3.4 %all-to-all-start.5 = ((bf16[8,2,10240]{2,1,0:T(2,128)(2,1)}), bf16[8,2,10240]{2,1,0:T(2,128)(2,1)S(1)}, u32[]{:S(2)}, u32[]{:S(2)}) async-start(bf16[8,2,10240]{2,1,0:T(2,128)(2,1)} %reshape.62), calls=%async_computation.5 | async-start | bytes 655360 | tf_op jit(solution)/shard_map/all_to_all | solution.py:1023
  230.6 19.1 %all-reduce.14 = bf16[40,160]{1,0:T(8,128)(2,1)S(1)} all-reduce(bf16[40,160]{1,0:T(8,128)(2,1)S(1)} %get-tuple-element.76), channel_id=3, replica_groups=mesh['tm'=8,'dp'=4] {'dp'}, use_global_device_ids=true, to_apply=%region_3.4.clone | all-reduce | flops 6400 | bytes 25600
  253.6 0.9 copy.68
  255.5 0.9 copy.69
  259.3 1.6 fusion.2
  (87 shorter events, 30.4 us)
Async XLA Ops:
  7.2 73.5 %all-gather.4.cloned.1.call-start = ((), (), s32[]{:S(2)}) async-start(), calls=%async_computation.7 | async-start | bytes 1484800 | tf_op jit(solution)/shard_map/all_gather | solution.py:1043
  17.0 0.7 copy-start.2
  19.0 37.9 %all-to-all-start.2 = ((bf16[8,3,128]{2,1,0:T(4,128)(2,1)}), bf16[8,3,128]{2,1,0:T(4,128)(2,1)S(1)}, u32[]{:S(2)}, u32[]{:S(2)}) async-start(bf16[8,3,128]{2,1,0:T(4,128)(2,1)} %copy.59), calls=%async_computation.2 | async-start | bytes 16384 | tf_op jit(solution)/shard_map/all_to_all | solution.py:1020
  56.9 11.7 %all-to-all-start.1 = ((bf16[8,128,160]{1,2,0:T(8,128)(2,1)}), bf16[8,128,160]{1,2,0:T(8,128)(2,1)S(1)}, u32[]{:S(2)}, u32[]{:S(2)}) async-start(bf16[8,128,160]{1,2,0:T(8,128)(2,1)} %param.28), calls=%async_computation.1 | async-start | bytes 655360 | tf_op jit(solution)/shard_map/all_to_all | solution.py:1020
  68.6 11.0 %all-to-all-start = ((bf16[8,128,160]{1,2,0:T(8,128)(2,1)}), bf16[8,128,160]{1,2,0:T(8,128)(2,1)S(1)}, u32[]{:S(2)}, u32[]{:S(2)}) async-start(bf16[8,128,160]{1,2,0:T(8,128)(2,1)} %param.15), calls=%async_computation | async-start | bytes 655360 | tf_op jit(solution)/shard_map/all_to_all | solution.py:1020
  72.1 184.4 %reduce-scatter.2.cloned.1.call-start = ((), (), s32[]{:S(2)}) async-start(), calls=%async_computation.8 | async-start | bytes 1536000 | tf_op jit(solution)/shard_map/reduce_scatter | solution.py:1086
  136.8 3.3 %copy-start.3 = (f32[32,160]{1,0:T(8,128)S(1)}, f32[32,160]{1,0:T(8,128)}, u32[]{:S(2)}) copy-start(f32[32,160]{1,0:T(8,128)} %get-tuple-element.22) | copy-start | bytes 61444
  142.0 58.0 %copy-start.4 = (f32[8,1024]{1,0:T(8,128)S(1)}, f32[8,1024]{1,0:T(8,128)}, u32[]{:S(2)}) copy-start(f32[8,1024]{1,0:T(8,128)} %get-tuple-element.19) | copy-start | bytes 98308
  142.0 65.2 %copy-start.1 = (bf16[1024,160]{1,0:T(8,128)(2,1)S(1)}, bf16[1024,160]{1,0:T(8,128)(2,1)}, u32[]{:S(2)}) copy-start(bf16[1024,160]{1,0:T(8,128)(2,1)} %get-tuple-element.18) | copy-start | bytes 983044
  203.8 14.5 %copy-start = (bf16[1024,160]{1,0:T(8,128)(2,1)S(1)}, bf16[1024,160]{1,0:T(8,128)(2,1)}, u32[]{:S(2)}) copy-start(bf16[1024,160]{1,0:T(8,128)(2,1)} %get-tuple-element.20) | copy-start | bytes 983044
  203.8 10.4 %all-to-all-start.4 = ((f32[8,1,384]{2,1,0:T(1,128)}), f32[8,1,384]{2,1,0:T(1,128)S(1)}, u32[]{:S(2)}, u32[]{:S(2)}) async-start(f32[8,1,384]{2,1,0:T(1,128)} %reshape.60), calls=%async_computation.4 | async-start | bytes 24576 | tf_op jit(solution)/shard_map/all_to_all | solution.py:1023
  214.2 11.8 %all-to-all-start.3 = ((bf16[8,2,10240]{2,1,0:T(2,128)(2,1)}), bf16[8,2,10240]{2,1,0:T(2,128)(2,1)S(1)}, u32[]{:S(2)}, u32[]{:S(2)}) async-start(bf16[8,2,10240]{2,1,0:T(2,128)(2,1)} %reshape.58), calls=%async_computation.3 | async-start | bytes 655360 | tf_op jit(solution)/shard_map/all_to_all | solution.py:1023
  218.3 11.1 %copy-start.5 = (u32[32]{0:T(128)S(1)}, u32[32]{0:T(128)}, u32[]{:S(2)}) copy-start(u32[32]{0:T(128)} %constant.63) | copy-start | bytes 388
  225.9 28.6 %all-to-all-start.5 = ((bf16[8,2,10240]{2,1,0:T(2,128)(2,1)}), bf16[8,2,10240]{2,1,0:T(2,128)(2,1)S(1)}, u32[]{:S(2)}, u32[]{:S(2)}) async-start(bf16[8,2,10240]{2,1,0:T(2,128)(2,1)} %reshape.62), calls=%async_computation.5 | async-start | bytes 655360 | tf_op jit(solution)/shard_map/all_to_all | solution.py:1023
Sparse Core Ops, SparseCore 0:
  17.9 33.9 all-gather.3
  200.1 30.2 reduce-scatter.1

commit v2 on v1

--- a/solution.py
+++ b/solution.py
@@ -549,6 +549,7 @@
 def series_scratch(span, width, head_width):
     full = pltpu.VMEM((span, width), jnp.float32)
     half = pltpu.VMEM((span, width), jnp.bfloat16)
+    flat = pltpu.VMEM((width, span), jnp.bfloat16)
     scan = pltpu.VMEM((2, span, LANES), jnp.float32)
     scan_more = pltpu.VMEM((2, span + 8, LANES), jnp.float32)
     narrow = pltpu.VMEM((span, head_width), jnp.bfloat16)
@@ -574,9 +575,15 @@
         values=narrow,
         head_queries=pltpu.VMEM((HEADS, span, width), jnp.bfloat16),
         head_keys=pltpu.VMEM((HEADS, span, width), jnp.bfloat16),
-        chances=pltpu.VMEM((HEADS, span, span), jnp.float32),
+        **{
+            "chances%d" % tile: pltpu.VMEM((HEADS, TILE, (tile + 1) * TILE), jnp.float32)
+            for tile in range(span // TILE)
+        },
         chance_sum=pltpu.VMEM((span, span), jnp.bfloat16),
-        score_grads=pltpu.VMEM((HEADS, span, span), jnp.bfloat16),
+        **{
+            "score_grads%d" % tile: pltpu.VMEM((HEADS, span - tile * TILE, TILE), jnp.bfloat16)
+            for tile in range(span // TILE)
+        },
         block=pltpu.VMEM((TILE, span), jnp.float32),
         mixed=narrow,
         mixed_grad=narrow,
@@ -584,32 +591,43 @@
         query_grad=half,
         key_grad=half,
         value_grad=narrow,
-        exit_grad=half,
-    )
-
-
-def series_forward_lstm(r, w, vec, x_ref, begin):
-    span, width = x_ref.shape
-
-    def gates(tile, _):
-        rows = rows_of(tile)
-        x = x_ref[rows, :]
-
-        def pre(block, column):
-            return nn(x, w[:, block : block + width]) + vec[column : column + 1, :]
-
-        time = tile * TILE + lax.broadcasted_iota(jnp.int32, (TILE, width), 0)
-        forget = jnp.where(time != begin, sigmoid(pre(FORGET, 0)), 0.0)
-        enter = sigmoid(pre(ENTER, 1))
-        candidate = jnp.tanh(pre(CANDIDATE, 2))
-        r.enter_gate[rows, :] = enter
-        r.candidate[rows, :] = candidate
-        r.exit_gate[rows, :] = sigmoid(pre(EXIT, 3))
-        put_halves(r.forget, rows, forget)
-        put_halves(r.local, rows, enter * candidate)
-        return 0
-
-    lax.fori_loop(0, span // TILE, gates, 0)
+        gate_grads=pltpu.VMEM((4, span, width), jnp.bfloat16),
+        x=half,
+        x_flat=flat,
+        adjoint=flat,
+        out=flat,
+        input_grad=flat,
+        w=pltpu.VMEM((width, PACKED), jnp.bfloat16),
+        g=pltpu.VMEM((width, PACKED), jnp.float32),
+        gv=pltpu.VMEM((VECTORS + 8, width), jnp.float32),
+        vec=pltpu.VMEM((VECTORS, width), jnp.float32),
+        level=pltpu.VMEM((8, width), jnp.bfloat16),
+    )
+
+
+def series_gates(r, begin, chunk, steps):
+    w, vec = r.w, r.vec
+    width = r.x.shape[1]
+    rows = rows_of(chunk, steps)
+    x = r.x_flat[:, rows].T
+    r.x[rows, :] = x
+
+    def pre(block, column):
+        return nn(x, w[:, block : block + width]) + vec[column : column + 1, :]
+
+    time = chunk * steps + lax.broadcasted_iota(jnp.int32, (steps, width), 0)
+    forget = jnp.where(time != begin, sigmoid(pre(FORGET, 0)), 0.0)
+    enter = sigmoid(pre(ENTER, 1))
+    candidate = jnp.tanh(pre(CANDIDATE, 2))
+    r.enter_gate[rows, :] = enter
+    r.candidate[rows, :] = candidate
+    r.exit_gate[rows, :] = sigmoid(pre(EXIT, 3))
+    put_halves(r.forget, rows, forget)
+    put_halves(r.local, rows, enter * candidate)
+
+
+def series_forward_scan(r):
+    span = r.x.shape[0]
     steps = span // CHUNKS
     zeros = jnp.zeros((CHUNKS, LANES), jnp.float32)
 
@@ -637,8 +655,9 @@
         r.cell[half, 0:8, :] = zeros
 
 
-def series_forward_first(r, w, vec, x_ref):
-    span, width = x_ref.shape
+def series_forward_first(r):
+    w, vec = r.w, r.vec
+    span, width = r.x.shape
     head_width = width // HEADS
     steps = span // CHUNKS
 
@@ -664,7 +683,7 @@
         r.glu_one[rows, :] = value
         r.gate_one[rows, :] = gate
         out, unit, inverse = normalise(
-            x_ref[rows, :].astype(jnp.float32) + value * gate, vec[6:7, :], vec[7:8, :]
+            r.x[rows, :].astype(jnp.float32) + value * gate, vec[6:7, :], vec[7:8, :]
         )
         r.unit_one[rows, :] = unit
         r.inverse_one[rows, :] = inverse
@@ -691,6 +710,7 @@
         seen = (tile + 1) * TILE
         row = tile * TILE + lax.broadcasted_iota(jnp.int32, (TILE, seen), 0)
         col = lax.broadcasted_iota(jnp.int32, (TILE, seen), 1)
+        chances = getattr(r, "chances%d" % tile)
         r.block[:, :seen] = jnp.where(
             (col <= row) & (col >= jnp.minimum(begin, row)), 0.0, NEG_BIG
         )
@@ -702,20 +722,21 @@
             top = jnp.max(scores, axis=-1, keepdims=True)
             raised = jnp.exp2(scores - top)
             total = jnp.sum(raised, axis=-1, keepdims=True)
-            r.chances[head, rows, :seen] = raised * (1.0 / total)
+            chances[head] = raised * (1.0 / total)
             return 0
 
         lax.fori_loop(0, HEADS, one_head, 0)
-        weights = r.chances[0, rows, :seen]
+        weights = chances[0]
         for head in range(1, HEADS):
-            weights = weights + r.chances[head, rows, :seen]
+            weights = weights + chances[head]
         weights = low(weights)
         r.chance_sum[rows, :seen] = weights
         r.mixed[rows, :] = low(nn(weights, r.values[:seen, :]) * (1.0 / HEADS))
 
 
-def series_middle(r, w, vec, level, adjoint_ref, slope_ref, horizon, out_ref, predicted_ref, g, gv):
-    span, width = out_ref.shape
+def series_middle(r, horizon):
+    w, vec, g, gv = r.w, r.vec, r.g, r.gv
+    span, width = r.x.shape
     head_width = width // HEADS
 
     def middle(tile, last):
@@ -741,17 +762,20 @@
             second + value_three * gate_three, vec[16:17, :], vec[17:18, :]
         )
         final_low = low(final)
-        out_ref[rows, :] = final_low
-        grad = adjoint_ref[rows, :].astype(jnp.float32)
+        r.out[:, rows] = final_low.T
+        grad = r.adjoint[:, rows].T.astype(jnp.float32)
         if last:
             start = span - TILE
             time = start + lax.broadcasted_iota(jnp.int32, (8, TILE), 1)
             ahead = jnp.where((time >= span - DEC) & (time < span - DEC + horizon), 1.0, 0.0)
-            predicted_ref[:, :start] = jnp.zeros((8, start), jnp.float32)
-            predicted_ref[:, start:] = nt(level[...], final_low) * ahead
-            slope = low(slope_ref[:, start:].astype(jnp.float32) * ahead)
-            gv[VECTORS:, :] = nn(slope, final_low)
-            grad = grad + tn(slope, level[...])
+            steps = r.slope.shape[1]
+            r.predicted[...] = (nt(r.level[...], final_low) * ahead)[:, TILE - steps :]
+            slope = jnp.concatenate(
+                [jnp.zeros((8, TILE - steps), jnp.float32), r.slope[...]], axis=1
+            )
+            slope = low(slope * ahead)
+            gv[VECTORS : VECTORS + 8, :] = nn(slope, final_low)
+            grad = grad + tn(slope, r.level[...])
         row_sum(gv, 16, grad * unit_three)
         row_sum(gv, 17, grad)
         sum_three = normalise_back(grad, unit_three, inverse_three, vec[16:17, :])
@@ -805,15 +829,19 @@
     for tile in range(span // TILE):
         rows = slice(tile * TILE, (tile + 1) * TILE)
         seen = (tile + 1) * TILE
+        held = getattr(r, "chances%d" % tile)
         head_grad = r.mixed_grad[rows, :] * (1.0 / HEADS)
         r.block[:, :seen] = nt(head_grad, r.values[:seen, :]) * scale
 
         def one_head(head, total):
-            chances = r.chances[head, rows, :seen]
+            chances = held[head]
             slope = r.block[:, :seen]
             delta = jnp.sum(chances * slope, axis=-1, keepdims=True)
             grads = low(chances * (slope - delta))
-            r.score_grads[head, rows, :seen] = grads
+            for part in range(tile + 1):
+                getattr(r, "score_grads%d" % part)[
+                    head, (tile - part) * TILE : (tile - part + 1) * TILE, :
+                ] = grads[:, part * TILE : (part + 1) * TILE]
             return total + nn(grads, r.head_keys[head, :seen, :])
 
         r.query_grad[rows, :] = low(
@@ -825,7 +853,7 @@
 
         def one_key(head, total):
             return total + tn(
-                r.score_grads[head, start:, cols], r.head_queries[head, start:, :]
+                getattr(r, "score_grads%d" % tile)[head], r.head_queries[head, start:, :]
             )
 
         r.key_grad[cols, :] = low(
@@ -836,7 +864,8 @@
         )
 
 
-def series_backward_first(r, w, vec, g, gv):
+def series_backward_first(r):
+    w, vec, g, gv = r.w, r.vec, r.g, r.gv
     span, width = r.hidden.shape
     head_width = width // HEADS
 
@@ -874,14 +903,14 @@
         put_halves(r.local, rows, hidden_grad * gate * (1.0 - tanh * tanh))
         exit_grad = hidden_grad * tanh * gate * (1.0 - gate)
         row_sum(gv, 3, exit_grad)
-        r.exit_grad[rows, :] = low(exit_grad)
+        r.gate_grads[3, rows, :] = low(exit_grad)
         return 0
 
     lax.fori_loop(0, span // TILE, back, 0)
 
 
-def series_backward_lstm(r, w, x_ref, input_grad_ref, g, gv):
-    span, width = x_ref.shape
+def series_backward_scan(r):
+    span = r.x.shape[0]
     steps = span // CHUNKS
     zeros = jnp.zeros((CHUNKS, LANES), jnp.float32)
     for half in range(2):
@@ -909,6 +938,12 @@
         for chunk in range(CHUNKS - 1, 0, -1):
             state = grads[chunk : chunk + 1] + mults[chunk : chunk + 1] * state
             r.carry[half, chunk - 1 : chunk, :] = state
+
+
+def series_gate_grads(r):
+    gv = r.gv
+    span, width = r.x.shape
+    steps = span // CHUNKS
 
     def back(chunk, _):
         rows = rows_of(chunk, steps)
@@ -929,192 +964,626 @@
         row_sum(gv, 0, grad_forget)
         row_sum(gv, 1, grad_enter)
         row_sum(gv, 2, grad_candidate)
-        x = x_ref[rows, :]
-        out = r.sum_two_grad[rows, :]
-        for block, one in (
-            (FORGET, low(grad_forget)),
-            (ENTER, low(grad_enter)),
-            (CANDIDATE, low(grad_candidate)),
-            (EXIT, r.exit_grad[rows, :]),
-        ):
-            g[:, block : block + width] += tn(x, one)
-            out = out + nt(one, w[:, block : block + width])
-        input_grad_ref[rows, :] = low(out)
+        r.gate_grads[0, rows, :] = low(grad_forget)
+        r.gate_grads[1, rows, :] = low(grad_enter)
+        r.gate_grads[2, rows, :] = low(grad_candidate)
         return 0
 
     lax.fori_loop(0, CHUNKS, back, 0)
 
 
+def series_input_grad(r, chunk, steps):
+    width = r.x.shape[1]
+    rows = rows_of(chunk, steps)
+    out = r.sum_two_grad[rows, :].T
+    for gate, block in enumerate((FORGET, ENTER, CANDIDATE, EXIT)):
+        out = out + nt(r.w[:, block : block + width], r.gate_grads[gate, rows, :])
+    r.input_grad[:, rows] = low(out)
+
+
+class Exchange:
+    def __init__(self, sems, axis, source, target):
+        self.sems, self.axis, self.source, self.target = sems, axis, source, target
+        self.count, self.me = lax.axis_size(axis), lax.axis_index(axis)
+
+    def other(self, step):
+        return lax.rem(self.me + step, self.count)
+
+    def copy(self, to, origin):
+        return pltpu.make_async_remote_copy(
+            src_ref=self.source(to),
+            dst_ref=self.target(origin),
+            send_sem=self.sems.at[0, to],
+            recv_sem=self.sems.at[1, origin],
+            device_id={self.axis: to},
+            device_id_type=pl.DeviceIdType.MESH,
+        )
+
+    def send(self, to):
+        self.copy(to, self.me).start()
+
+    def arrive(self, origin):
+        self.copy(origin, origin).wait_recv()
+
+    def start(self):
+        for step in range(1, self.count):
+            self.send(self.other(step))
+
+    def arrive_all(self):
+        for step in range(1, self.count):
+            self.arrive(self.other(step))
+
+    def sent(self):
+        for step in range(1, self.count):
+            to = self.other(step)
+            self.copy(to, self.me).wait_send()
+
+
+PAD_ROWS = 48
+GROUP_COLUMNS = (384, 384, 768)
+BLOCKS_MIDDLE = (GLU_TWO_A, GLU_TWO_B, INNER, MIDDLE, GLU_THREE_A, GLU_THREE_B, ATTN_OUT)
+BLOCKS_FIRST = (GLU_ONE_A, GLU_ONE_B, QUERY, KEY)
+BLOCKS_LSTM = (FORGET, ENTER, CANDIDATE, EXIT)
+
+
+def travel_scratch(count, groups, steps, width, rows):
+    half, wide = LANES, 2 * LANES
+
+    def pieces(lanes):
+        return dict(
+            send=pltpu.VMEM((count, width, lanes), jnp.bfloat16),
+            land=pltpu.VMEM((count, width, lanes), jnp.bfloat16),
+            part=pltpu.VMEM((groups, rows, lanes), jnp.float32),
+            parts=pltpu.VMEM((groups, rows, lanes), jnp.float32),
+        )
+
+    out = dict(
+        slope=pltpu.VMEM((8, steps), jnp.float32),
+        slopes=pltpu.VMEM((count, 8, steps), jnp.float32),
+        levels=pltpu.VMEM((count, 8, steps), jnp.float32),
+        predicted=pltpu.VMEM((8, steps), jnp.float32),
+        stage=pltpu.VMEM((width, 2 * GROUP_COLUMNS[2]), jnp.float32),
+        attn_stage=pltpu.VMEM((width, wide), jnp.float32),
+        table_stage=pltpu.VMEM((PAD_ROWS, LANES), jnp.float32),
+    )
+    for group, columns in enumerate(GROUP_COLUMNS):
+        out["params%d" % group] = pltpu.VMEM((2, groups, PAD_ROWS, columns), jnp.bfloat16)
+        out["params%d_dp" % group] = pltpu.SemaphoreType.DMA((2, groups))
+        out["params%d_core" % group] = pltpu.SemaphoreType.DMA((2, groups))
+    for name, lanes in (("middle", wide), ("first", half), ("lstm", half)):
+        for what, shape in pieces(lanes).items():
+            out[name + "_" + what] = shape
+        out[name + "_tm"] = pltpu.SemaphoreType.DMA((2, count))
+        out[name + "_dp"] = pltpu.SemaphoreType.DMA((2, groups))
+        out[name + "_all"] = pltpu.SemaphoreType.DMA((2, count))
+    for name in ("x", "adjoint", "out", "input", "slope", "predicted"):
+        out[name + "_sems"] = pltpu.SemaphoreType.DMA((2, count))
+    out["own_sems"] = pltpu.SemaphoreType.DMA((4,))
+    return out
+
+
+class Parameters:
+    def __init__(self, r, group):
+        self.buffer = getattr(r, "params%d" % group)
+        self.mine, self.core = lax.axis_index("dp"), lax.rem(lax.axis_index("tm"), 2)
+        self.count = lax.axis_size("dp")
+        buffer, core, mine = self.buffer, self.core, self.mine
+        self.over = Exchange(
+            getattr(r, "params%d_dp" % group),
+            "dp",
+            lambda to: buffer.at[core, mine],
+            lambda origin: buffer.at[core, origin],
+        )
+        self.sems = getattr(r, "params%d_core" % group)
+        self.sibling = lax.axis_index("tm") + 1 - 2 * core
+
+    def hand(self, origin, core):
+        return pltpu.make_async_remote_copy(
+            src_ref=self.buffer.at[core, origin],
+            dst_ref=self.buffer.at[core, origin],
+            send_sem=self.sems.at[0, origin],
+            recv_sem=self.sems.at[1, origin],
+            device_id={"tm": self.sibling},
+            device_id_type=pl.DeviceIdType.MESH,
+        )
+
+    def pass_on(self):
+        for step in range(1, self.count):
+            origin = self.over.other(step)
+            self.over.arrive(origin)
+            self.hand(origin, self.core).start()
+
+    def arrive(self):
+        for step in range(1, self.count):
+            self.hand(self.over.other(step), 1 - self.core).wait_recv()
+
+    def sent(self):
+        self.over.sent()
+        for step in range(1, self.count):
+            self.hand(self.over.other(step), self.core).wait_send()
+
+
+class Reduction:
+    def __init__(self, r, name, final, owners):
+        self.send, self.land = getattr(r, name + "_send"), getattr(r, name + "_land")
+        self.part, self.parts = getattr(r, name + "_part"), getattr(r, name + "_parts")
+        self.final, self.owners = final, owners
+        self.me, self.mine = lax.axis_index("tm"), lax.axis_index("dp")
+        self.count, self.groups = lax.axis_size("tm"), lax.axis_size("dp")
+        send, land, part, parts, me, mine = (
+            self.send, self.land, self.part, self.parts, self.me, self.mine
+        )
+        self.over_time = Exchange(
+            getattr(r, name + "_tm"), "tm", lambda to: send.at[to], lambda origin: land.at[origin]
+        )
+        self.over_series = Exchange(
+            getattr(r, name + "_dp"), "dp", lambda to: part.at[to], lambda origin: parts.at[origin]
+        )
+        self.to_all = Exchange(
+            getattr(r, name + "_all"), "tm", lambda to: final.at[me], lambda origin: final.at[origin]
+        )
+
+    def owned(self, index, action):
+        if self.owners == self.count:
+            action()
+        else:
+            pl.when(index < self.owners)(action)
+
+    def start(self):
+        for step in range(1, self.count):
+            to = self.over_time.other(step)
+            self.owned(to, lambda: self.over_time.send(to))
+
+    def sum_time(self):
+        def action():
+            self.over_time.arrive_all()
+            self.land[self.me] = self.send[self.me]
+            total = self.land[0].astype(jnp.float32)
+            for origin in range(1, self.count):
+                total = total + self.land[origin].astype(jnp.float32)
+            rows = self.part.shape[1]
+            for group in range(self.groups):
+                self.part[group] = total[group * rows : (group + 1) * rows]
+            self.over_series.start()
+
+        self.owned(self.me, action)
+
+    def sum_series(self):
+        def action():
+            self.over_series.arrive_all()
+            self.parts[self.mine] = self.part[self.mine]
+            total = self.parts[0]
+            for origin in range(1, self.groups):
+                total = total + self.parts[origin]
+            self.final[self.me] = total
+            self.to_all.start()
+
+        self.owned(self.me, action)
+
+    def finish(self):
+        for step in range(1, self.count):
+            origin = self.to_all.other(step)
+            self.owned(origin, lambda: self.to_all.arrive(origin))
+        for step in range(1, self.count):
+            to = self.over_time.other(step)
+            self.owned(to, lambda: self.over_time.copy(to, self.me).wait_send())
+
+        def action():
+            self.over_series.sent()
+            self.to_all.sent()
+
+        self.owned(self.me, action)
+
+
+def greet():
+    barrier = pltpu.get_barrier_semaphore()
+    total = 0
+    for axis in ("tm", "dp"):
+        me, count = lax.axis_index(axis), lax.axis_size(axis)
+        for step in range(1, count):
+            pl.semaphore_signal(
+                barrier,
+                inc=1,
+                device_id={axis: lax.rem(me + step, count)},
+                device_id_type=pl.DeviceIdType.MESH,
+            )
+            total += 1
+    return lambda: pl.semaphore_wait(barrier, total)
+
+
+def pack_params(r, group, params):
+    mine = lax.axis_index("dp")
+    buffer = getattr(r, "params%d" % group)
+
+    def put(half, column, array, rows):
+        buffer[half, mine, :rows, column : column + array.shape[1]] = low(array)
+
+    if group == 0:
+        lstm, table, level = params
+        rows = lstm.shape[0]
+        split = GROUP_COLUMNS[0]
+        put(0, 0, lstm[:, :split], rows)
+        put(1, 0, lstm[:, split:], rows)
+        r.table_stage[...] = jnp.zeros_like(r.table_stage)
+        r.table_stage[: table.shape[0], :rows] = table[...]
+        r.table_stage[VECTORS : VECTORS + LEVEL_TALLY, :rows] = level[...]
+        put(1, lstm.shape[1] - split, r.table_stage[...], PAD_ROWS)
+    elif group == 1:
+        glu_one, qkv = params
+        put(0, 0, glu_one[...], glu_one.shape[0])
+        put(1, 0, qkv[...], qkv.shape[0])
+    else:
+        glu_two, glu_three, inner, middle, attn = params
+        rows = glu_two.shape[0]
+        put(0, 0, glu_two[...], rows)
+        put(0, 3 * LANES, glu_three[...], rows)
+        put(1, 0, inner[...], rows)
+        put(1, 2 * LANES, middle[...], rows)
+        put(1, 4 * LANES, attn[...], attn.shape[0])
+
+
+def unpack_params(r, group, rows, attn_rows):
+    width = r.w.shape[0]
+    head_width = width // HEADS
+    buffer, stage = getattr(r, "params%d" % group), r.stage
+    columns = GROUP_COLUMNS[group]
+    for half in range(2):
+        for origin in range(buffer.shape[1]):
+            stage[origin * rows : (origin + 1) * rows, half * columns : (half + 1) * columns] = (
+                buffer[half, origin].astype(jnp.float32)[:rows]
+            )
+
+    def place(block, column, size):
+        r.w[:, block : block + size] = low(stage[:, column : column + size])
+
+    if group == 0:
+        for gate, block in enumerate(BLOCKS_LSTM):
+            place(block, gate * width, width)
+        vectors = jnp.concatenate(
+            [
+                buffer[1, origin][:, columns - LANES :].astype(jnp.float32)[: VECTORS + 8, :rows]
+                for origin in range(buffer.shape[1])
+            ],
+            axis=1,
+        )
+        r.vec[...] = vectors[:VECTORS]
+        r.level[...] = low(vectors[VECTORS:])
+    elif group == 1:
+        place(GLU_ONE_A, 0, width)
+        place(GLU_ONE_B, width, width)
+        place(QUERY, columns, width)
+        place(KEY, columns + width, width)
+        place(VALUE, columns + 2 * width, head_width)
+    else:
+        place(GLU_TWO_A, 0, width)
+        place(GLU_TWO_B, width, width)
+        place(GLU_THREE_A, 3 * LANES, width)
+        place(GLU_THREE_B, 3 * LANES + width, width)
+        place(INNER, columns, width)
+        place(MIDDLE, columns + 2 * LANES, width)
+        for origin in range(buffer.shape[1]):
+            r.attn_stage[origin * attn_rows : (origin + 1) * attn_rows, :] = stage[
+                origin * rows : origin * rows + attn_rows, columns + 4 * LANES :
+            ]
+        r.w[:head_width, ATTN_OUT : ATTN_OUT + width] = low(r.attn_stage[:head_width, :width])
+
+
 def series_kernel(
-    scalars,
-    x_ref,
-    adjoint_ref,
-    slope_ref,
-    w,
-    vec,
+    begins,
+    reaches,
+    x_hbm,
+    adjoint_hbm,
+    slopes,
+    lstm,
+    glu_one,
+    qkv,
+    attn,
+    glu_two,
+    inner,
+    middle,
+    glu_three,
     level,
-    out_ref,
-    predicted_ref,
-    input_grad_ref,
-    g,
-    gv,
+    table,
+    out_hbm,
+    predicted_out,
+    input_hbm,
+    final_middle,
+    final_first,
+    final_lstm,
     *scratch,
 ):
-    span, width = x_ref.shape
-    names = series_scratch(span, width, width // HEADS)
-    r = types.SimpleNamespace(**dict(zip(names, scratch)))
-    begin, horizon = scalars[0], scalars[1]
-    g[...] = jnp.zeros_like(g)
-    gv[...] = jnp.zeros_like(gv)
-    series_forward_lstm(r, w, vec, x_ref, begin)
-    series_forward_first(r, w, vec, x_ref)
-    series_forward_attention(r, begin)
-    series_middle(
-        r, w, vec, level, adjoint_ref, slope_ref, horizon, out_ref, predicted_ref, g, gv
-    )
-    series_backward_attention(r)
-    series_backward_first(r, w, vec, g, gv)
-    series_backward_lstm(r, w, x_ref, input_grad_ref, g, gv)
-
-
-def pack_weights(parts, width):
-    (lstm, glu_one, qkv, glu_two, inner, middle, glu_three) = parts
-    half = 2 * LANES
-
-    def spread(array, block):
-        return [
-            jnp.pad(array[:, at : at + block], ((0, 0), (0, half - block)))
-            for at in range(0, array.shape[1], block)
-        ]
-
-    pieces = spread(lstm, width) + spread(glu_one, width) + spread(qkv[:, : 2 * width], width)
-    pieces.append(jnp.pad(qkv[:, 2 * width :], ((0, 0), (0, LANES - (qkv.shape[1] - 2 * width)))))
-    pieces += spread(glu_two, width) + spread(inner, width) + spread(middle, width)
-    pieces += spread(glu_three, width)
-    return jnp.concatenate(pieces, axis=1)
-
-
-def whole_series(
-    embedded_features,
-    earliest_seen_moment,
-    reach_choice,
-    lstm_valve_coeffs,
-    lstm_unit_coeffs,
-    asker_lookup_coeffs,
-    attend_exit_coeffs,
-    attend_unit_coeffs,
-    skipnet_entry_coeffs,
-    skipnet_inner_coeffs,
-    skipnet_unit_coeffs,
-    level_map_coeffs,
-    bias_gain_table,
-    block_emit_adjoint,
-    predicted_adjoint,
-):
-    count, steps, width = embedded_features.shape
+    count, width, steps = x_hbm.shape
     span = count * steps
     head_width = width // HEADS
-    mine = lax.axis_index("tm")
-
-    def to_series(array, axis):
-        return lax.all_to_all(array, "tm", split_axis=0, concat_axis=axis, tiled=True)
-
-    def to_time(array, axis):
-        return lax.all_to_all(array, "tm", split_axis=axis, concat_axis=0, tiled=True)
-
-    x = to_series(embedded_features, 1)[0]
-    adjoint = to_series(block_emit_adjoint, 1)[0]
-    slope = jnp.pad(to_series(predicted_adjoint, 2)[0], ((0, 8 - LEVEL_TALLY), (0, 0)))
-    packed = pack_weights(
-        [
-            narrow_convert(array)
-            for array in (
-                lstm_valve_coeffs,
-                lstm_unit_coeffs,
-                asker_lookup_coeffs,
-                attend_unit_coeffs,
-                skipnet_entry_coeffs,
-                skipnet_inner_coeffs,
-                skipnet_unit_coeffs,
+    groups = lax.axis_size("dp")
+    rows = lstm.shape[0]
+    names = series_scratch(span, width, head_width)
+    names.update(travel_scratch(count, groups, steps, width, rows))
+    r = types.SimpleNamespace(**dict(zip(names, scratch)))
+    me = lax.axis_index("tm")
+    last = count - 1
+
+    def block(ref, index):
+        return ref.at[:, rows_of(index, steps)]
+
+    x_over = Exchange(r.x_sems, "tm", lambda to: x_hbm.at[to], lambda origin: block(r.x_flat, origin))
+    adjoint_over = Exchange(
+        r.adjoint_sems, "tm", lambda to: adjoint_hbm.at[to], lambda origin: block(r.adjoint, origin)
+    )
+    out_over = Exchange(
+        r.out_sems, "tm", lambda to: block(r.out, to), lambda origin: out_hbm.at[origin]
+    )
+    input_over = Exchange(
+        r.input_sems, "tm", lambda to: block(r.input_grad, to), lambda origin: input_hbm.at[origin]
+    )
+    slope_over = Exchange(
+        r.slope_sems, "tm", lambda to: r.slopes.at[to], lambda origin: r.slope
+    )
+    predicted_over = Exchange(
+        r.predicted_sems, "tm", lambda to: r.predicted, lambda origin: r.levels.at[origin]
+    )
+    params = [Parameters(r, group) for group in range(3)]
+    middle_sum = Reduction(r, "middle", final_middle, len(BLOCKS_MIDDLE))
+    first_sum = Reduction(r, "first", final_first, count)
+    lstm_sum = Reduction(r, "lstm", final_lstm, count)
+
+    own_x = pltpu.make_async_copy(x_hbm.at[me], block(r.x_flat, me), r.own_sems.at[0])
+    own_adjoint = pltpu.make_async_copy(adjoint_hbm.at[me], block(r.adjoint, me), r.own_sems.at[1])
+    own_out = pltpu.make_async_copy(block(r.out, me), out_hbm.at[me], r.own_sems.at[2])
+    own_input = pltpu.make_async_copy(block(r.input_grad, me), input_hbm.at[me], r.own_sems.at[3])
+
+    everyone_here = greet()
+    own_x.start()
+    own_adjoint.start()
+    pack_params(r, 0, (lstm, table, level))
+    everyone_here()
+    x_over.start()
+    params[0].over.start()
+    pack_params(r, 1, (glu_one, qkv))
+    params[1].over.start()
+    pack_params(r, 2, (glu_two, glu_three, inner, middle, attn))
+    params[2].over.start()
+    for track in range(count):
+        r.slopes[track] = jnp.concatenate(
+            [
+                slopes[level_at].astype(jnp.float32)[track : track + 1]
+                for level_at in range(LEVEL_TALLY)
+            ]
+            + [jnp.zeros((8 - LEVEL_TALLY, steps), jnp.float32)],
+            axis=0,
+        )
+
+    @pl.when(me == last)
+    def _():
+        slope_over.start()
+        r.slope[...] = r.slopes[last]
+
+    r.g[...] = jnp.zeros_like(r.g)
+    r.gv[...] = jnp.zeros_like(r.gv)
+    begin = begins[me]
+    choice = reaches[me]
+    horizon = jnp.where(choice == 0, 1, jnp.where(choice == 1, 5, 24))
+
+    params[0].pass_on()
+    params[0].arrive()
+    unpack_params(r, 0, rows, attn.shape[0])
+    own_x.wait()
+    series_gates(r, begin, me, steps)
+
+    def arriving(step, _):
+        origin = x_over.other(step)
+        x_over.arrive(origin)
+        series_gates(r, begin, origin, steps)
+        return 0
+
+    lax.fori_loop(1, count, arriving, 0)
+    adjoint_over.start()
+    params[1].pass_on()
+    series_forward_scan(r)
+    params[1].arrive()
+    unpack_params(r, 1, rows, attn.shape[0])
+    series_forward_first(r)
+    params[2].pass_on()
+    series_forward_attention(r, begin)
+    params[2].arrive()
+    unpack_params(r, 2, rows, attn.shape[0])
+    own_adjoint.wait()
+    adjoint_over.arrive_all()
+
+    @pl.when(me != last)
+    def _():
+        slope_over.arrive(last)
+
+    series_middle(r, horizon)
+    own_out.start()
+    out_over.start()
+
+    @pl.when(me != last)
+    def _():
+        predicted_over.send(last)
+
+    for index, column in enumerate(BLOCKS_MIDDLE[:-1]):
+        middle_sum.send[index] = low(r.g[:, column : column + 2 * LANES])
+    r.attn_stage[...] = jnp.zeros_like(r.attn_stage)
+    small = attn.shape[0]
+    for group in range(groups):
+        r.attn_stage[group * rows : group * rows + small, :] = r.g[
+            group * small : (group + 1) * small, ATTN_OUT : ATTN_OUT + 2 * LANES
+        ]
+    middle_sum.send[len(BLOCKS_MIDDLE) - 1] = low(r.attn_stage[...])
+    middle_sum.start()
+    series_backward_attention(r)
+    middle_sum.sum_time()
+    series_backward_first(r)
+    for index, column in enumerate(BLOCKS_FIRST):
+        for part in range(2):
+            at = column + part * LANES
+            piece = r.g[:, at : at + LANES]
+            if column == QUERY and part == 1:
+                spare = width - LANES
+                piece = jnp.concatenate(
+                    [
+                        piece[:, :spare],
+                        r.g[:, VALUE : VALUE + head_width],
+                        jnp.zeros((width, LANES - spare - head_width), jnp.float32),
+                    ],
+                    axis=1,
+                )
+            first_sum.send[2 * index + part] = low(piece)
+    first_sum.start()
+    middle_sum.sum_series()
+    series_backward_scan(r)
+    series_gate_grads(r)
+    first_sum.sum_time()
+    spare = width - LANES
+    r.attn_stage[...] = jnp.zeros_like(r.attn_stage)
+    for group in range(groups):
+        r.attn_stage[group * rows : group * rows + VECTORS + 8, spare : spare + rows] = r.gv[
+            :, group * rows : (group + 1) * rows
+        ]
+    for gate in range(4):
+        grad = nn(r.x_flat[...], r.gate_grads[gate])
+        lstm_sum.send[2 * gate] = low(grad[:, :LANES])
+        rest = [grad[:, LANES:], jnp.zeros((width, LANES - spare), jnp.float32)]
+        if gate == 0:
+            rest = [grad[:, LANES:], r.attn_stage[:, spare:LANES]]
+        lstm_sum.send[2 * gate + 1] = low(jnp.concatenate(rest, axis=1))
+    lstm_sum.start()
+    first_sum.sum_series()
+    for step in range(1, count):
+        to = input_over.other(step)
+        series_input_grad(r, to, steps)
+        input_over.send(to)
+    series_input_grad(r, me, steps)
+    own_input.start()
+    lstm_sum.sum_time()
+
+    @pl.when(me != last)
+    def _():
+        predicted_over.copy(last, me).wait_send()
+        predicted_out[...] = jnp.zeros_like(predicted_out)
+
+    @pl.when(me == last)
+    def _():
+        slope_over.sent()
+        predicted_over.arrive_all()
+        r.levels[last] = r.predicted[...]
+        for level_at in range(LEVEL_TALLY):
+            predicted_out[level_at] = jnp.concatenate(
+                [r.levels[track][level_at : level_at + 1] for track in range(count)], axis=0
             )
-        ],
-        width,
-    )
-    packed = lax.all_gather(packed, "dp", axis=0, tiled=True)
-    attn_out = lax.all_gather(narrow_convert(attend_exit_coeffs), "dp", axis=0, tiled=True)
-    packed = jnp.concatenate(
-        [
-            packed,
-            jnp.pad(attn_out, ((0, width - head_width), (0, PACKED - ATTN_OUT - width))),
-        ],
-        axis=1,
-    )
-    columns = lax.all_gather(
-        narrow_convert(jnp.concatenate([bias_gain_table, level_map_coeffs], axis=1)),
-        "dp",
-        axis=0,
-        tiled=True,
-    )
-    vectors = bias_gain_table.shape[1]
-    vec = jnp.pad(columns[:, :vectors].astype(jnp.float32).T, ((0, VECTORS - vectors), (0, 0)))
-    level = jnp.pad(columns[:, vectors:].T, ((0, 8 - LEVEL_TALLY), (0, 0)))
-    begin = earliest_seen_moment[mine]
-    choice = reach_choice[mine]
-    horizon = jnp.where(choice == 0, 1, jnp.where(choice == 1, 5, 24))
-    out, predicted, input_grad, g, gv = pl.pallas_call(
+
+    lstm_sum.sum_series()
+    x_over.sent()
+    adjoint_over.sent()
+    for group in params:
+        group.sent()
+    own_out.wait()
+    out_over.arrive_all()
+    out_over.sent()
+    middle_sum.finish()
+    first_sum.finish()
+    own_input.wait()
+    input_over.arrive_all()
+    input_over.sent()
+    lstm_sum.finish()
+
+
+def unpack_kernel(
+    final_middle,
+    final_first,
+    final_lstm,
+    lstm,
+    glu_one,
+    qkv,
+    attn,
+    glu_two,
+    inner,
+    middle,
+    glu_three,
+    level,
+    table,
+):
+    width = inner.shape[1]
+    spare = width - LANES
+
+    def halves(out, column, final, index):
+        out[:, column : column + LANES] = final[index]
+        out[:, column + LANES : column + width] = final[index + 1][:, :spare]
+
+    for gate in range(4):
+        halves(lstm, gate * width, final_lstm, 2 * gate)
+    vectors = final_lstm[1][:, spare : spare + table.shape[1]]
+    table[...] = vectors[: table.shape[0]]
+    level[...] = vectors[VECTORS : VECTORS + LEVEL_TALLY]
+    for index in range(2):
+        halves(glu_one, index * width, final_first, 2 * index)
+        halves(qkv, index * width, final_first, 4 + 2 * index)
+        glu_two[:, index * width : (index + 1) * width] = final_middle[index][:, :width]
+        glu_three[:, index * width : (index + 1) * width] = final_middle[4 + index][:, :width]
+    qkv[:, 2 * width :] = final_first[5][:, spare : spare + qkv.shape[1] - 2 * width]
+    inner[...] = final_middle[2][:, :width]
+    middle[...] = final_middle[3][:, :width]
+    attn[...] = final_middle[6][: attn.shape[0], :width]
+
+
+def whole_series(embedded_features, earliest_seen_moment, reach_choice, *others):
+    count, steps, width = embedded_features.shape
+    features = embedded_features.swapaxes(1, 2)
+    adjoint = others[-2].swapaxes(1, 2)
+    slopes = others[-1].swapaxes(0, 1)
+    params = others[:-4] + (others[-4].T, others[-3].T)
+    head_width = width // HEADS
+    groups = lax.axis_size("dp")
+    rows = params[0].shape[0]
+    names = series_scratch(count * steps, width, head_width)
+    names.update(travel_scratch(count, groups, steps, width, rows))
+    smem, vmem, anywhere = (
+        pl.BlockSpec(memory_space=space) for space in (pltpu.SMEM, pltpu.VMEM, pl.ANY)
+    )
+    out, predicted, input_grad, *finals = pl.pallas_call(
         series_kernel,
         out_shape=(
-            jax.ShapeDtypeStruct((span, width), jnp.bfloat16),
-            jax.ShapeDtypeStruct((8, span), jnp.float32),
-            jax.ShapeDtypeStruct((span, width), jnp.bfloat16),
-            jax.ShapeDtypeStruct((width, PACKED), jnp.float32),
-            jax.ShapeDtypeStruct((VECTORS + 8, width), jnp.float32),
+            jax.ShapeDtypeStruct(features.shape, jnp.bfloat16),
+            jax.ShapeDtypeStruct(slopes.shape, jnp.float32),
+            jax.ShapeDtypeStruct(features.shape, jnp.bfloat16),
+            jax.ShapeDtypeStruct((count, rows, 2 * LANES), jnp.float32),
+            jax.ShapeDtypeStruct((count, rows, LANES), jnp.float32),
+            jax.ShapeDtypeStruct((count, rows, LANES), jnp.float32),
         ),
-        in_specs=[pl.BlockSpec(memory_space=pltpu.SMEM)]
-        + [pl.BlockSpec(memory_space=pltpu.VMEM)] * 6,
-        out_specs=(pl.BlockSpec(memory_space=pltpu.VMEM),) * 5,
-        scratch_shapes=list(series_scratch(span, width, head_width).values()),
-        compiler_params=pltpu.CompilerParams(vmem_limit_bytes=VMEM_BYTES),
-    )(jnp.stack([begin, horizon]), x, adjoint, slope, packed, vec, level)
-    emitted = to_time(out[None], 1)
-    input_out = to_time(input_grad[None], 1)
-    levels = to_time(predicted[None, :LEVEL_TALLY], 2)
-    vector_columns = gv.T
-    whole = lax.psum(
-        jnp.concatenate([g[:, :ATTN_OUT], vector_columns], axis=1), "tm"
-    )
-    whole = lax.psum_scatter(
-        whole.astype(jnp.bfloat16), "dp", scatter_dimension=0, tiled=True
-    ).astype(jnp.float32)
-    attn_whole = lax.psum_scatter(
-        lax.psum(g[:head_width, ATTN_OUT : ATTN_OUT + width], "tm").astype(jnp.bfloat16),
-        "dp",
-        scatter_dimension=0,
-        tiled=True,
-    ).astype(jnp.float32)
-
-    def gather(*starts):
-        return jnp.concatenate([whole[:, at : at + width] for at in starts], axis=1)
-
+        in_specs=[smem, smem, anywhere, anywhere] + [vmem] * 11,
+        out_specs=(anywhere, vmem, anywhere) + (vmem,) * 3,
+        scratch_shapes=list(names.values()),
+        compiler_params=pltpu.CompilerParams(
+            vmem_limit_bytes=VMEM_BYTES, collective_id=0, has_side_effects=True
+        ),
+    )(
+        earliest_seen_moment,
+        reach_choice,
+        features,
+        adjoint,
+        slopes,
+        *params,
+    )
+    *grads, level_grad, table_grad = pl.pallas_call(
+        unpack_kernel,
+        out_shape=tuple(jax.ShapeDtypeStruct(param.shape, jnp.float32) for param in params),
+        in_specs=[vmem] * 3,
+        out_specs=(vmem,) * len(params),
+    )(*finals)
     return (
-        emitted,
-        levels,
-        input_out,
-        gather(FORGET, ENTER, CANDIDATE, EXIT),
-        gather(GLU_ONE_A, GLU_ONE_B),
-        jnp.concatenate([gather(QUERY, KEY), whole[:, VALUE : VALUE + head_width]], axis=1),
-        attn_whole,
-        gather(GLU_TWO_A, GLU_TWO_B),
-        whole[:, INNER : INNER + width],
-        whole[:, MIDDLE : MIDDLE + width],
-        gather(GLU_THREE_A, GLU_THREE_B),
-        whole[:, ATTN_OUT + VECTORS : ATTN_OUT + VECTORS + LEVEL_TALLY],
-        whole[:, ATTN_OUT : ATTN_OUT + vectors],
+        out.swapaxes(1, 2),
+        predicted.swapaxes(0, 1),
+        input_grad.swapaxes(1, 2),
+        *grads,
+        level_grad.T,
+        table_grad.T,
     )
 
 
 def on_device(embedded_features, *others):
-    one_each = embedded_features.shape[0] == lax.axis_size("tm")
+    count, steps, _ = embedded_features.shape
+    one_each = count == lax.axis_size("tm") == CHUNKS and steps == LANES
     return (whole_series if one_each else shards)(embedded_features, *others)
 
 

time: 273 us -> 89 us (0.33)
  blocking collectives: 104 us -> 0 us
  Pallas kernels: 52.9 us -> 86 us
  other arithmetic: 31.6 us -> 0 us
  local copies, waits for them, and re-layouts: 30.7 us -> 2.06 us
  starting transfers between devices: 23.8 us -> 0 us
  between operations: 16.3 us -> 0.69 us
  waiting for transfers between devices: 12.3 us -> 0 us
    psum x1 -> x0, blocking collectives: 57.9 us -> none  [whole_series(): lax.psum(jnp.concatenate([g[:, :ATTN_OUT], vector_columns], axis=1), 'tm')]
    pallas_call x1 -> x2, Pallas kernels: 52.9 us -> 86 us  [the longest x1 84 us: whole_series(): pl.pallas_call(series_kernel, out_shape=(jax.ShapeDtypeStruct(features.sh...]
    all_gather x2 -> x0, blocking collectives: 26.6 us -> none  [the longest x1 13.5 us: whole_series(): lax.all_gather(narrow_convert(jnp.concatenate([bias_gain_table, level_map...]
    all_to_all x6 -> x0, starting transfers between devices: 23.7 us -> none  [the longest x3 12.7 us: to_series(): lax.all_to_all(array, 'tm', split_axis=0, concat_axis=axis, tiled=True)]
    unnamed x1 -> x0, blocking collectives: 19.1 us -> none
    unnamed x10 -> x0, other arithmetic: 14.1 us -> none
    all_to_all x6 -> x0, waiting for transfers between devices: 12.3 us -> none  [the longest x3 11.1 us: to_series(): lax.all_to_all(array, 'tm', split_axis=0, concat_axis=axis, tiled=True)]
    unnamed x39 -> x9, local copies, waits for them, and re-layouts: 13.7 us -> 2.06 us
  transfers between devices with their start and end apart: 8 -> 0, of which waited for: 3 -> 0; matrix products, arithmetic and copies ran while one was open for 13% -> 0% of each run, Pallas kernels for 0% -> 0%
where the time goes in v2:
time: 89 us; the launch traced here: 88.8 us
  Pallas kernels  86 us (97%)
  local copies, waits for them, and re-layouts  2.06 us (2%)
    pallas_call x1, Pallas kernels, whole_series(): pl.pallas_call(series_kernel, out_shape=(jax.ShapeDtypeStruct(features.sh...  84 us
    unnamed x9, local copies, waits for them, and re-layouts  2.06 us
    pallas_call x1, Pallas kernels, whole_series(): pl.pallas_call(unpack_kernel, out_shape=tuple((jax.ShapeDtypeStruct(param...  1.99 us

profile of v2, /device:TPU:0, one launch (start us, length us, event | category | flops | bytes accessed | tf_op | source)
XLA Modules:
  0.0 88.8 jit_solution(1200628878097470941)
XLA Ops:
  0.7 84.0 %shard_map.246 = (bf16[8,160,128]{2,1,0:T(8,128)(2,1)}, f32[3,8,128]{2,1,0:T(8,128)}, bf16[8,160,128]{2,1,0:T(8,128)(2,1)}, f32[8,40,256]{2,1,0:T(8,128)}, f32[8,40,128]{2,1,0:T(8,128)}, /*index=5*/f32[8,40,128]{2,1,0:T(8,128)}) custom-call(s32[8]{0:T(128)} %begins.1, s32[8]{0:T(128)} %reaches.1, bf16[8,160,128]{2,1,0:T(8,128)(2,1)} %bitcast.10, ...), custom_call_target="tpu_custom_call" | custom-call | tf_op jit(solution)/shard_map/pallas_call | solution.py:1544
  84.7 0.0 copy-start.1
  84.7 2.0 %shard_map.247 = (f32[40,640]{1,0:T(8,128)}, f32[40,320]{1,0:T(8,128)}, f32[40,360]{1,0:T(8,128)}, f32[10,160]{1,0:T(8,128)}, f32[40,320]{1,0:T(8,128)}, /*index...) custom-call(f32[8,40,256]{2,1,0:T(8,128)} %get-tuple-element.32.final_middle, ...), custom_call_target="tpu_custom_call" | custom-call | tf_op jit(solution)/shard_map/pallas_call | solution.py:1568
  86.7 0.0 copy-done.1
  86.7 0.0 copy-start.2
  86.7 0.0 copy-start
  86.7 0.7 copy.31
  87.4 0.0 copy-done.2
  87.4 0.6 copy.32
  88.0 0.0 copy-done
  88.0 0.7 copy.33
Async XLA Ops:
  84.7 2.0 %copy-start.1 = (bf16[8,160,128]{2,1,0:T(8,128)(2,1)S(1)}, bf16[8,160,128]{2,1,0:T(8,128)(2,1)}, u32[]{:S(2)}) copy-start(bf16[8,160,128]{2,1,0:T(8,128)(2,1)} %get-tuple-element.29) | copy-start | bytes 983044
  86.7 0.7 copy-start.2
  86.7 1.3 %copy-start = (bf16[8,160,128]{2,1,0:T(8,128)(2,1)S(1)}, bf16[8,160,128]{2,1,0:T(8,128)(2,1)}, u32[]{:S(2)}) copy-start(bf16[8,160,128]{2,1,0:T(8,128)(2,1)} %get-tuple-element.31) | copy-start | bytes 983044

commit v3 on v2

--- a/solution.py
+++ b/solution.py
@@ -486,6 +486,7 @@
 LANES = 128
 CHUNKS = 8
 TILE = 256
+DENSE = 1024
 
 
 def nn(left, right):
@@ -676,7 +677,7 @@
     lax.fori_loop(0, CHUNKS, cells, 0)
 
     def first(tile, _):
-        rows = rows_of(tile)
+        rows = rows_of(tile, DENSE)
         hidden = r.hidden[rows, :]
         value = nn(hidden, w[:, GLU_ONE_A : GLU_ONE_A + width]) + vec[4:5, :]
         gate = sigmoid(nn(hidden, w[:, GLU_ONE_B : GLU_ONE_B + width]) + vec[5:6, :])
@@ -694,12 +695,12 @@
         r.keys[rows, :] = key
         r.values[rows, :] = low(nn(out, w[:, VALUE : VALUE + head_width]))
         for head in range(HEADS):
-            mine = lane_head((TILE, width), head_width, head)
+            mine = lane_head((DENSE, width), head_width, head)
             r.head_queries[head, rows, :] = jnp.where(mine, query, jnp.zeros_like(query))
             r.head_keys[head, rows, :] = jnp.where(mine, key, jnp.zeros_like(key))
         return 0
 
-    lax.fori_loop(0, span // TILE, first, 0)
+    lax.fori_loop(0, span // DENSE, first, 0)
 
 
 def series_forward_attention(r, begin):
@@ -725,7 +726,7 @@
             chances[head] = raised * (1.0 / total)
             return 0
 
-        lax.fori_loop(0, HEADS, one_head, 0)
+        lax.fori_loop(0, HEADS, one_head, 0, unroll=True)
         weights = chances[0]
         for head in range(1, HEADS):
             weights = weights + chances[head]
@@ -740,7 +741,7 @@
     head_width = width // HEADS
 
     def middle(tile, last):
-        rows = rows_of(tile)
+        rows = rows_of(tile, DENSE)
         first = r.unit_one[rows, :] * vec[6:7, :] + vec[7:8, :]
         mixed = r.mixed[rows, :]
         attn = low(nn(mixed, w[:head_width, ATTN_OUT : ATTN_OUT + width]))
@@ -765,13 +766,13 @@
         r.out[:, rows] = final_low.T
         grad = r.adjoint[:, rows].T.astype(jnp.float32)
         if last:
-            start = span - TILE
-            time = start + lax.broadcasted_iota(jnp.int32, (8, TILE), 1)
+            start = span - DENSE
+            time = start + lax.broadcasted_iota(jnp.int32, (8, DENSE), 1)
             ahead = jnp.where((time >= span - DEC) & (time < span - DEC + horizon), 1.0, 0.0)
             steps = r.slope.shape[1]
-            r.predicted[...] = (nt(r.level[...], final_low) * ahead)[:, TILE - steps :]
+            r.predicted[...] = (nt(r.level[...], final_low) * ahead)[:, DENSE - steps :]
             slope = jnp.concatenate(
-                [jnp.zeros((8, TILE - steps), jnp.float32), r.slope[...]], axis=1
+                [jnp.zeros((8, DENSE - steps), jnp.float32), r.slope[...]], axis=1
             )
             slope = low(slope * ahead)
             gv[VECTORS : VECTORS + 8, :] = nn(slope, final_low)
@@ -818,8 +819,8 @@
         r.mixed_grad[rows, :] = low(nt(attn_grad, w[:head_width, ATTN_OUT : ATTN_OUT + width]))
         return 0
 
-    lax.fori_loop(0, span // TILE - 1, lambda tile, _: middle(tile, False), 0)
-    middle(span // TILE - 1, True)
+    lax.fori_loop(0, span // DENSE - 1, lambda tile, _: middle(tile, False), 0)
+    middle(span // DENSE - 1, True)
 
 
 def series_backward_attention(r):
@@ -845,7 +846,7 @@
             return total + nn(grads, r.head_keys[head, :seen, :])
 
         r.query_grad[rows, :] = low(
-            lax.fori_loop(0, HEADS, one_head, jnp.zeros((TILE, width), jnp.float32))
+            lax.fori_loop(0, HEADS, one_head, jnp.zeros((TILE, width), jnp.float32), unroll=True)
         )
     for tile in range(span // TILE):
         cols = slice(tile * TILE, (tile + 1) * TILE)
@@ -857,7 +858,7 @@
             )
 
         r.key_grad[cols, :] = low(
-            lax.fori_loop(0, HEADS, one_key, jnp.zeros((TILE, width), jnp.float32))
+            lax.fori_loop(0, HEADS, one_key, jnp.zeros((TILE, width), jnp.float32), unroll=True)
         )
         r.value_grad[cols, :] = low(
             tn(r.chance_sum[start:, cols], r.mixed_grad[start:, :] * (1.0 / HEADS))
@@ -870,7 +871,7 @@
     head_width = width // HEADS
 
     def back(tile, _):
-        rows = rows_of(tile)
+        rows = rows_of(tile, DENSE)
         query, key, value = r.query_grad[rows, :], r.key_grad[rows, :], r.value_grad[rows, :]
         grad = (
             r.sum_two_grad[rows, :]
@@ -906,7 +907,7 @@
         r.gate_grads[3, rows, :] = low(exit_grad)
         return 0
 
-    lax.fori_loop(0, span // TILE, back, 0)
+    lax.fori_loop(0, span // DENSE, back, 0)
 
 
 def series_backward_scan(r):

time: 89 us -> 78.8 us (0.89)
  Pallas kernels: 86 us -> 75.8 us
    pallas_call x1, Pallas kernels: 84 us -> 73.8 us  [whole_series(): pl.pallas_call(series_kernel, out_shape=(jax.ShapeDtypeStruct(features.sh...]
where the time goes in v3:
time: 78.8 us; the launch traced here: 78.6 us
  Pallas kernels  75.8 us (96%)
  local copies, waits for them, and re-layouts  2.06 us (3%)
    pallas_call x1, Pallas kernels, whole_series(): pl.pallas_call(series_kernel, out_shape=(jax.ShapeDtypeStruct(features.sh...  73.8 us
    unnamed x9, local copies, waits for them, and re-layouts  2.06 us
    pallas_call x1, Pallas kernels, whole_series(): pl.pallas_call(unpack_kernel, out_shape=tuple((jax.ShapeDtypeStruct(param...  1.99 us

profile of v3, /device:TPU:0, one launch (start us, length us, event | category | flops | bytes accessed | tf_op | source)
XLA Modules:
  0.0 78.6 jit_solution(12674955566435743766)
XLA Ops:
  0.7 73.8 %shard_map.246 = (bf16[8,160,128]{2,1,0:T(8,128)(2,1)}, f32[3,8,128]{2,1,0:T(8,128)}, bf16[8,160,128]{2,1,0:T(8,128)(2,1)}, f32[8,40,256]{2,1,0:T(8,128)}, f32[8,40,128]{2,1,0:T(8,128)}, /*index=5*/f32[8,40,128]{2,1,0:T(8,128)}) custom-call(s32[8]{0:T(128)} %begins.1, s32[8]{0:T(128)} %reaches.1, bf16[8,160,128]{2,1,0:T(8,128)(2,1)} %bitcast.10, ...), custom_call_target="tpu_custom_call" | custom-call | tf_op jit(solution)/shard_map/pallas_call | solution.py:1545
  74.5 0.0 copy-start.1
  74.5 2.0 %shard_map.247 = (f32[40,640]{1,0:T(8,128)}, f32[40,320]{1,0:T(8,128)}, f32[40,360]{1,0:T(8,128)}, f32[10,160]{1,0:T(8,128)}, f32[40,320]{1,0:T(8,128)}, /*index...) custom-call(f32[8,40,256]{2,1,0:T(8,128)} %get-tuple-element.32.final_middle, ...), custom_call_target="tpu_custom_call" | custom-call | tf_op jit(solution)/shard_map/pallas_call | solution.py:1569
  76.5 0.0 copy-done.1
  76.5 0.0 copy-start.2
  76.5 0.0 copy-start
  76.5 0.7 copy.31
  77.3 0.0 copy-done.2
  77.3 0.6 copy.32
  77.9 0.0 copy-done
  77.9 0.7 copy.33
Async XLA Ops:
  74.5 2.0 %copy-start.1 = (bf16[8,160,128]{2,1,0:T(8,128)(2,1)S(1)}, bf16[8,160,128]{2,1,0:T(8,128)(2,1)}, u32[]{:S(2)}) copy-start(bf16[8,160,128]{2,1,0:T(8,128)(2,1)} %get-tuple-element.29) | copy-start | bytes 983044
  76.5 0.7 copy-start.2
  76.5 1.3 %copy-start = (bf16[8,160,128]{2,1,0:T(8,128)(2,1)S(1)}, bf16[8,160,128]{2,1,0:T(8,128)(2,1)}, u32[]{:S(2)}) copy-start(bf16[8,160,128]{2,1,0:T(8,128)(2,1)} %get-tuple-element.31) | copy-start | bytes 983044

commit v4 on v0

--- a/solution.py
+++ b/solution.py
@@ -1,6 +1,10 @@
+import types
+
 import jax
 import jax.numpy as jnp
 from jax import lax
+from jax.experimental import pallas as pl
+from jax.experimental.pallas import tpu as pltpu
 from jax.sharding import PartitionSpec as P
 
 HEADS = 4
@@ -12,6 +16,8 @@
 EPSILON = 1e-05
 NEG_BIG = -1e30
 attend_group = 2
+LOG2_E = 1.4426950408889634
+VMEM_BYTES = 60 * 2**20
 
 
 def entering(value, axis, join, neutral, backward):
@@ -463,6 +469,1073 @@
     )
 
 
+def lane_head(shape, head_width, head):
+    lane = lax.broadcasted_iota(jnp.int32, shape, len(shape) - 1)
+    return (lane >= head * head_width) & (lane < (head + 1) * head_width)
+
+
+FORGET, ENTER, CANDIDATE, EXIT = 0, 256, 512, 768
+GLU_ONE_A, GLU_ONE_B = 1024, 1280
+QUERY, KEY, VALUE = 1536, 1792, 2048
+GLU_TWO_A, GLU_TWO_B = 2176, 2432
+INNER, MIDDLE = 2688, 2944
+GLU_THREE_A, GLU_THREE_B = 3200, 3456
+ATTN_OUT = 3712
+PACKED = 3968
+VECTORS = 24
+LANES = 128
+CHUNKS = 8
+TILE = 256
+
+
+def nn(left, right):
+    return jnp.dot(left, right, preferred_element_type=jnp.float32)
+
+
+def nt(left, right):
+    return lax.dot_general(
+        left, right, (((1,), (1,)), ((), ())), preferred_element_type=jnp.float32
+    )
+
+
+def tn(left, right):
+    return lax.dot_general(
+        left, right, (((0,), (0,)), ((), ())), preferred_element_type=jnp.float32
+    )
+
+
+def low(values):
+    return values.astype(jnp.bfloat16)
+
+
+def sigmoid(values):
+    return 0.5 * jnp.tanh(0.5 * values) + 0.5
+
+
+def normalise(values, gain, shift):
+    centred = values - jnp.mean(values, axis=-1, keepdims=True)
+    spread = jnp.mean(centred * centred, axis=-1, keepdims=True)
+    inverse = lax.rsqrt(spread + EPSILON)
+    unit = centred * inverse
+    return unit * gain + shift, unit, inverse
+
+
+def normalise_back(grad, unit, inverse, gain):
+    scaled = grad * gain
+    return inverse * (
+        scaled
+        - jnp.mean(scaled, axis=-1, keepdims=True)
+        - unit * jnp.mean(scaled * unit, axis=-1, keepdims=True)
+    )
+
+
+def rows_of(tile, size):
+    return pl.ds(pl.multiple_of(tile * size, size), size)
+
+
+def put_halves(ref, rows, values):
+    ref[0, rows, :] = values[:, :LANES]
+    ref[1, rows, : values.shape[1] - LANES] = values[:, LANES:]
+
+
+def get_halves(ref, rows, width):
+    return jnp.concatenate([ref[0, rows, :], ref[1, rows, : width - LANES]], axis=1)
+
+
+def row_sum(ref, column, values):
+    ref[column : column + 1, :] = jnp.sum(values, axis=0, keepdims=True)
+
+
+def series_scratch(span, width, head_width):
+    full = pltpu.VMEM((span, width), jnp.float32)
+    half = pltpu.VMEM((span, width), jnp.bfloat16)
+    flat = pltpu.VMEM((width, span), jnp.bfloat16)
+    scan = pltpu.VMEM((2, span, LANES), jnp.float32)
+    scan_more = pltpu.VMEM((2, span + 8, LANES), jnp.float32)
+    narrow = pltpu.VMEM((span, head_width), jnp.bfloat16)
+    column = pltpu.VMEM((span, 1), jnp.float32)
+    tiles = span // TILE
+    return dict(
+        forget=scan_more,
+        local=scan,
+        mult=scan,
+        cell=scan_more,
+        carry=pltpu.VMEM((2, CHUNKS, LANES), jnp.float32),
+        enter_gate=full,
+        candidate=full,
+        exit_gate=full,
+        cell_tanh=full,
+        hidden=half,
+        glu_one=full,
+        gate_one=full,
+        unit_one=full,
+        inverse_one=column,
+        first_low=half,
+        keys=half,
+        values=narrow,
+        head_queries=pltpu.VMEM((HEADS, span, width), jnp.bfloat16),
+        head_keys=pltpu.VMEM((HEADS, span, width), jnp.bfloat16),
+        **{
+            "chances%d" % tile: pltpu.VMEM((HEADS, TILE, (tile + 1) * TILE), jnp.float32)
+            for tile in range(tiles)
+        },
+        chance_sum=pltpu.VMEM((span, span), jnp.bfloat16),
+        **{
+            "score_grads%d" % tile: pltpu.VMEM((HEADS, span - tile * TILE, TILE), jnp.bfloat16)
+            for tile in range(tiles)
+        },
+        block=pltpu.VMEM((TILE, span), jnp.float32),
+        mixed=narrow,
+        mixed_grad=narrow,
+        sum_two_grad=full,
+        query_grad=half,
+        key_grad=half,
+        value_grad=narrow,
+        gate_grads=pltpu.VMEM((4, span, width), jnp.bfloat16),
+        x=half,
+        x_flat=flat,
+        adjoint=flat,
+        out=flat,
+        input_grad=flat,
+        w=pltpu.VMEM((width, PACKED), jnp.bfloat16),
+        vec=pltpu.VMEM((VECTORS, width), jnp.float32),
+        level=pltpu.VMEM((8, width), jnp.bfloat16),
+        gv=pltpu.VMEM((VECTORS + 8, width), jnp.float32),
+        slope=pltpu.VMEM((8, LANES), jnp.float32),
+        predicted=pltpu.VMEM((8, LANES), jnp.float32),
+        attn_flat=pltpu.VMEM((width, 2 * width // 5), jnp.float32),
+        lstm_flat=pltpu.VMEM((width, 4 * LANES), jnp.float32),
+        middle_send=pltpu.VMEM((2, width, GROUP_LANES["middle"]), jnp.bfloat16),
+        first_send=pltpu.VMEM((2, width, GROUP_LANES["first"]), jnp.bfloat16),
+        lstm_send=pltpu.VMEM((2, width, GROUP_LANES["lstm"]), jnp.bfloat16),
+    )
+
+
+def series_turn(r, chunk, steps):
+    rows = rows_of(chunk, steps)
+    r.x[rows, :] = r.x_flat[:, rows].T
+
+
+def series_gates(r, begin):
+    w, vec = r.w, r.vec
+    span, width = r.x.shape
+    rows = slice(0, span)
+    x = r.x[...]
+
+    def pre(block, column):
+        return nn(x, w[:, block : block + width]) + vec[column : column + 1, :]
+
+    time = lax.broadcasted_iota(jnp.int32, (span, width), 0)
+    put_halves(r.forget, rows, jnp.where(time != begin, sigmoid(pre(FORGET, 0)), 0.0))
+    enter = sigmoid(pre(ENTER, 1))
+    candidate = jnp.tanh(pre(CANDIDATE, 2))
+    r.enter_gate[...] = enter
+    r.candidate[...] = candidate
+    put_halves(r.local, rows, enter * candidate)
+    r.exit_gate[...] = sigmoid(pre(EXIT, 3))
+
+
+def series_forward_scan(r):
+    span = r.x.shape[0]
+    steps = span // CHUNKS
+    zeros = jnp.zeros((CHUNKS, LANES), jnp.float32)
+
+    def step(t, state):
+        out = []
+        at = pl.ds(t, CHUNKS, stride=steps)
+        for half in range(2):
+            cell, mult = state[half]
+            forget = r.forget[half, at, :]
+            cell = forget * cell + r.local[half, at, :]
+            mult = mult * forget
+            r.local[half, at, :] = cell
+            r.mult[half, at, :] = mult
+            out.append((cell, mult))
+        return tuple(out)
+
+    ends = lax.fori_loop(0, steps, step, ((zeros, zeros + 1.0),) * 2, unroll=8)
+    for half in range(2):
+        cells, mults = ends[half]
+        state = jnp.zeros((1, LANES), jnp.float32)
+        r.carry[half, 0:1, :] = state
+        for chunk in range(CHUNKS - 1):
+            state = cells[chunk : chunk + 1] + mults[chunk : chunk + 1] * state
+            r.carry[half, chunk + 1 : chunk + 2, :] = state
+        r.cell[half, 0:8, :] = zeros
+
+
+def series_forward_first(r):
+    w, vec = r.w, r.vec
+    span, width = r.x.shape
+    head_width = width // HEADS
+    steps = span // CHUNKS
+    for chunk in range(CHUNKS):
+        rows = slice(chunk * steps, (chunk + 1) * steps)
+        later = slice(chunk * steps + 8, (chunk + 1) * steps + 8)
+        for half in range(2):
+            r.cell[half, later, :] = (
+                r.local[half, rows, :]
+                + r.mult[half, rows, :] * r.carry[half, chunk : chunk + 1, :]
+            )
+    tanh = jnp.tanh(get_halves(r.cell, slice(8, 8 + span), width))
+    r.cell_tanh[...] = tanh
+    hidden = low(r.exit_gate[...] * tanh)
+    r.hidden[...] = hidden
+    value = nn(hidden, w[:, GLU_ONE_A : GLU_ONE_A + width]) + vec[4:5, :]
+    gate = sigmoid(nn(hidden, w[:, GLU_ONE_B : GLU_ONE_B + width]) + vec[5:6, :])
+    r.glu_one[...] = value
+    r.gate_one[...] = gate
+    out, unit, inverse = normalise(
+        r.x[...].astype(jnp.float32) + value * gate, vec[6:7, :], vec[7:8, :]
+    )
+    r.unit_one[...] = unit
+    r.inverse_one[...] = inverse
+    out = low(out)
+    r.first_low[...] = out
+    query = low(nn(out, w[:, QUERY : QUERY + width]))
+    key = low(nn(out, w[:, KEY : KEY + width]))
+    r.keys[...] = key
+    r.values[...] = low(nn(out, w[:, VALUE : VALUE + head_width]))
+    for head in range(HEADS):
+        mine = lane_head((span, width), head_width, head)
+        r.head_queries[head] = jnp.where(mine, query, jnp.zeros_like(query))
+        r.head_keys[head] = jnp.where(mine, key, jnp.zeros_like(key))
+
+
+def series_forward_attention(r, begin):
+    span, head_width = r.values.shape
+    scale = head_width ** (-0.5) * LOG2_E
+    for tile in range(span // TILE):
+        rows = slice(tile * TILE, (tile + 1) * TILE)
+        seen = (tile + 1) * TILE
+        row = tile * TILE + lax.broadcasted_iota(jnp.int32, (TILE, seen), 0)
+        col = lax.broadcasted_iota(jnp.int32, (TILE, seen), 1)
+        chances = getattr(r, "chances%d" % tile)
+        r.block[:, :seen] = jnp.where(
+            (col <= row) & (col >= jnp.minimum(begin, row)), 0.0, NEG_BIG
+        )
+        for head in range(HEADS):
+            scores = (
+                nt(r.head_queries[head, rows, :], r.keys[:seen, :]) * scale + r.block[:, :seen]
+            )
+            top = jnp.max(scores, axis=-1, keepdims=True)
+            raised = jnp.exp2(scores - top)
+            total = jnp.sum(raised, axis=-1, keepdims=True)
+            chances[head] = raised * (1.0 / total)
+        weights = chances[0]
+        for head in range(1, HEADS):
+            weights = weights + chances[head]
+        weights = low(weights)
+        r.chance_sum[rows, :seen] = weights
+        r.mixed[rows, :] = low(nn(weights, r.values[:seen, :]) * (1.0 / HEADS))
+
+
+def series_middle(r, horizon, after_forward):
+    w, vec, gv = r.w, r.vec, r.gv
+    span, width = r.x.shape
+    head_width = width // HEADS
+    first = r.unit_one[...] * vec[6:7, :] + vec[7:8, :]
+    mixed = r.mixed[...]
+    attn = low(nn(mixed, w[:head_width, ATTN_OUT : ATTN_OUT + width]))
+    value_two = nn(attn, w[:, GLU_TWO_A : GLU_TWO_A + width]) + vec[8:9, :]
+    gate_two = sigmoid(nn(attn, w[:, GLU_TWO_B : GLU_TWO_B + width]) + vec[9:10, :])
+    second, unit_two, inverse_two = normalise(
+        first + value_two * gate_two, vec[10:11, :], vec[11:12, :]
+    )
+    second_low = low(second)
+    inner_pre = nn(second_low, w[:, INNER : INNER + width]) + vec[12:13, :]
+    inner_exp = jnp.exp(jnp.minimum(inner_pre, 0.0))
+    inner_low = low(jnp.where(inner_pre > 0, inner_pre, inner_exp - 1.0))
+    middle_low = low(nn(inner_low, w[:, MIDDLE : MIDDLE + width]) + vec[13:14, :])
+    value_three = nn(middle_low, w[:, GLU_THREE_A : GLU_THREE_A + width]) + vec[14:15, :]
+    gate_three = sigmoid(nn(middle_low, w[:, GLU_THREE_B : GLU_THREE_B + width]) + vec[15:16, :])
+    final, unit_three, inverse_three = normalise(
+        second + value_three * gate_three, vec[16:17, :], vec[17:18, :]
+    )
+    final_low = low(final)
+    r.out[...] = final_low.T
+    steps = r.slope.shape[1]
+    time = span - steps + lax.broadcasted_iota(jnp.int32, (8, steps), 1)
+    ahead = jnp.where((time >= span - DEC) & (time < span - DEC + horizon), 1.0, 0.0)
+    r.predicted[...] = nt(r.level[...], final_low[span - steps :]) * ahead
+    after_forward()
+    slope = low(r.slope[...] * ahead)
+    gv[VECTORS : VECTORS + 8, :] = nn(slope, final_low[span - steps :])
+    grad = r.adjoint[...].T.astype(jnp.float32)
+    grad = jnp.concatenate(
+        [grad[: span - steps], grad[span - steps :] + tn(slope, r.level[...])], axis=0
+    )
+    row_sum(gv, 16, grad * unit_three)
+    row_sum(gv, 17, grad)
+    sum_three = normalise_back(grad, unit_three, inverse_three, vec[16:17, :])
+    grad_a = sum_three * gate_three
+    grad_b = grad_a * value_three * (1.0 - gate_three)
+    row_sum(gv, 14, grad_a)
+    row_sum(gv, 15, grad_b)
+    low_a, low_b = low(grad_a), low(grad_b)
+    send = r.middle_send
+    send[1, :, :width] = low(tn(middle_low, low_a))
+    send[1, :, width : 2 * width] = low(tn(middle_low, low_b))
+    middle_grad = nt(low_a, w[:, GLU_THREE_A : GLU_THREE_A + width]) + nt(
+        low_b, w[:, GLU_THREE_B : GLU_THREE_B + width]
+    )
+    row_sum(gv, 13, middle_grad)
+    middle_grad = low(middle_grad)
+    send[1, :, 2 * width : 3 * width] = low(tn(inner_low, middle_grad))
+    inner_grad = nt(middle_grad, w[:, MIDDLE : MIDDLE + width]) * jnp.where(
+        inner_pre > 0, 1.0, inner_exp
+    )
+    row_sum(gv, 12, inner_grad)
+    inner_grad = low(inner_grad)
+    send[0, :, 2 * width : 3 * width] = low(tn(second_low, inner_grad))
+    grad = sum_three + nt(inner_grad, w[:, INNER : INNER + width])
+    row_sum(gv, 10, grad * unit_two)
+    row_sum(gv, 11, grad)
+    sum_two = normalise_back(grad, unit_two, inverse_two, vec[10:11, :])
+    r.sum_two_grad[...] = sum_two
+    grad_a = sum_two * gate_two
+    grad_b = grad_a * value_two * (1.0 - gate_two)
+    row_sum(gv, 8, grad_a)
+    row_sum(gv, 9, grad_b)
+    low_a, low_b = low(grad_a), low(grad_b)
+    attn_grad = low(
+        nt(low_a, w[:, GLU_TWO_A : GLU_TWO_A + width])
+        + nt(low_b, w[:, GLU_TWO_B : GLU_TWO_B + width])
+    )
+    r.mixed_grad[...] = low(nt(attn_grad, w[:head_width, ATTN_OUT : ATTN_OUT + width]))
+    send[0, :, :width] = low(tn(attn, low_a))
+    send[0, :, width : 2 * width] = low(tn(attn, low_b))
+    attn_weight = tn(mixed, attn_grad)
+    rows, small = head_width, head_width // HEADS
+    spare = width // 5
+    r.attn_flat[...] = jnp.zeros_like(r.attn_flat)
+    for group in range(HEADS):
+        for piece in range(5):
+            at = group * rows + small * (piece % 4)
+            half = piece // 4
+            r.attn_flat[at : at + small, half * spare : (half + 1) * spare] = attn_weight[
+                group * small : (group + 1) * small, piece * spare : (piece + 1) * spare
+            ]
+    for half in range(2):
+        send[half, :, 3 * width :] = low(r.attn_flat[:, half * spare : (half + 1) * spare])
+
+
+def series_backward_attention(r, between):
+    span, head_width = r.values.shape
+    width = head_width * HEADS
+    scale = head_width ** (-0.5)
+    for tile in range(span // TILE):
+        rows = slice(tile * TILE, (tile + 1) * TILE)
+        seen = (tile + 1) * TILE
+        held = getattr(r, "chances%d" % tile)
+        head_grad = r.mixed_grad[rows, :] * (1.0 / HEADS)
+        r.block[:, :seen] = nt(head_grad, r.values[:seen, :]) * scale
+        total = jnp.zeros((TILE, width), jnp.float32)
+        for head in range(HEADS):
+            chances = held[head]
+            slope = r.block[:, :seen]
+            delta = jnp.sum(chances * slope, axis=-1, keepdims=True)
+            grads = low(chances * (slope - delta))
+            for part in range(tile + 1):
+                getattr(r, "score_grads%d" % part)[
+                    head, (tile - part) * TILE : (tile - part + 1) * TILE, :
+                ] = grads[:, part * TILE : (part + 1) * TILE]
+            total = total + nn(grads, r.head_keys[head, :seen, :])
+        r.query_grad[rows, :] = low(total)
+        between(tile)
+    for tile in range(span // TILE):
+        cols = slice(tile * TILE, (tile + 1) * TILE)
+        start = tile * TILE
+        total = jnp.zeros((TILE, width), jnp.float32)
+        for head in range(HEADS):
+            total = total + tn(
+                getattr(r, "score_grads%d" % tile)[head], r.head_queries[head, start:, :]
+            )
+        r.key_grad[cols, :] = low(total)
+        r.value_grad[cols, :] = low(
+            tn(r.chance_sum[start:, cols], r.mixed_grad[start:, :] * (1.0 / HEADS))
+        )
+
+
+def series_backward_first(r):
+    w, vec, gv = r.w, r.vec, r.gv
+    span, width = r.hidden.shape
+    head_width = width // HEADS
+    rows = slice(0, span)
+    send = r.first_send
+    query, key, value = r.query_grad[...], r.key_grad[...], r.value_grad[...]
+    grad = (
+        r.sum_two_grad[...]
+        + nt(query, w[:, QUERY : QUERY + width])
+        + nt(key, w[:, KEY : KEY + width])
+        + nt(value, w[:, VALUE : VALUE + head_width])
+    )
+    first = r.first_low[...]
+    send[1, :, :width] = low(tn(first, query))
+    send[1, :, width : 2 * width] = low(tn(first, key))
+    send[1, :, 2 * width : 2 * width + head_width] = low(tn(first, value))
+    unit = r.unit_one[...]
+    row_sum(gv, 6, grad * unit)
+    row_sum(gv, 7, grad)
+    sum_one = normalise_back(grad, unit, r.inverse_one[...], vec[6:7, :])
+    r.sum_two_grad[...] = sum_one
+    gate = r.gate_one[...]
+    grad_a = sum_one * gate
+    grad_b = grad_a * r.glu_one[...] * (1.0 - gate)
+    row_sum(gv, 4, grad_a)
+    row_sum(gv, 5, grad_b)
+    low_a, low_b = low(grad_a), low(grad_b)
+    hidden_grad = nt(low_a, w[:, GLU_ONE_A : GLU_ONE_A + width]) + nt(
+        low_b, w[:, GLU_ONE_B : GLU_ONE_B + width]
+    )
+    tanh, gate = r.cell_tanh[...], r.exit_gate[...]
+    put_halves(r.local, rows, hidden_grad * gate * (1.0 - tanh * tanh))
+    exit_grad = hidden_grad * tanh * gate * (1.0 - gate)
+    row_sum(gv, 3, exit_grad)
+    exit_grad = low(exit_grad)
+    r.gate_grads[3] = exit_grad
+    hidden = r.hidden[...]
+    send[0, :, :width] = low(tn(hidden, low_a))
+    send[0, :, width : 2 * width] = low(tn(hidden, low_b))
+    send[0, :, 2 * width : 3 * width] = low(nn(r.x_flat[...], exit_grad))
+
+
+def series_backward_scan(r):
+    span = r.x.shape[0]
+    steps = span // CHUNKS
+    zeros = jnp.zeros((CHUNKS, LANES), jnp.float32)
+    for half in range(2):
+        r.forget[half, span:, :] = zeros
+
+    def step(count, state):
+        t = steps - 1 - count
+        out = []
+        at, after = pl.ds(t, CHUNKS, stride=steps), pl.ds(t + 1, CHUNKS, stride=steps)
+        for half in range(2):
+            grad, mult = state[half]
+            forget = r.forget[half, after, :]
+            grad = forget * grad + r.local[half, at, :]
+            mult = mult * forget
+            r.local[half, at, :] = grad
+            r.mult[half, at, :] = mult
+            out.append((grad, mult))
+        return tuple(out)
+
+    ends = lax.fori_loop(0, steps, step, ((zeros, zeros + 1.0),) * 2, unroll=8)
+    for half in range(2):
+        grads, mults = ends[half]
+        state = jnp.zeros((1, LANES), jnp.float32)
+        r.carry[half, CHUNKS - 1 : CHUNKS, :] = state
+        for chunk in range(CHUNKS - 1, 0, -1):
+            state = grads[chunk : chunk + 1] + mults[chunk : chunk + 1] * state
+            r.carry[half, chunk - 1 : chunk, :] = state
+
+
+def series_gate_grads(r):
+    gv = r.gv
+    span, width = r.x.shape
+    steps = span // CHUNKS
+    for half in range(2):
+        for chunk in range(CHUNKS):
+            rows = slice(chunk * steps, (chunk + 1) * steps)
+            r.local[half, rows, :] += r.mult[half, rows, :] * r.carry[half, chunk : chunk + 1, :]
+    grad = get_halves(r.local, slice(0, span), width)
+    forget = get_halves(r.forget, slice(0, span), width)
+    before = get_halves(r.cell, slice(7, 7 + span), width)
+    enter, candidate = r.enter_gate[...], r.candidate[...]
+    for gate, one in enumerate(
+        (
+            grad * before * forget * (1.0 - forget),
+            grad * candidate * enter * (1.0 - enter),
+            grad * enter * (1.0 - candidate * candidate),
+        )
+    ):
+        row_sum(gv, gate, one)
+        one = low(one)
+        r.gate_grads[gate] = one
+        r.lstm_flat[:, gate * width : (gate + 1) * width] = nn(r.x_flat[...], one)
+    r.lstm_flat[:, 3 * width :] = gv[...].T
+    lanes = r.lstm_send.shape[2]
+    for half in range(2):
+        r.lstm_send[half] = low(r.lstm_flat[:, half * lanes : (half + 1) * lanes])
+
+
+def series_input_grad(r):
+    width = r.x.shape[1]
+    out = r.sum_two_grad[...].T
+    for gate, block in enumerate((FORGET, ENTER, CANDIDATE, EXIT)):
+        out = out + nt(r.w[:, block : block + width], r.gate_grads[gate])
+    r.input_grad[...] = low(out)
+
+
+class Exchange:
+    def __init__(self, sems, devices, source, target):
+        self.sems, self.source, self.target = sems, source, target
+        self.count, self.me, self.device = devices
+
+    def other(self, step):
+        return lax.rem(self.me + step, self.count)
+
+    def copy(self, to, origin):
+        return pltpu.make_async_remote_copy(
+            src_ref=self.source(to),
+            dst_ref=self.target(origin),
+            send_sem=self.sems.at[0, to],
+            recv_sem=self.sems.at[1, origin],
+            device_id=self.device(to),
+            device_id_type=pl.DeviceIdType.MESH,
+        )
+
+    def send(self, to):
+        self.copy(to, self.me).start()
+
+    def arrive(self, origin):
+        self.copy(origin, origin).wait_recv()
+
+    def start(self):
+        for step in range(1, self.count):
+            self.send(self.other(step))
+
+    def arrive_all(self):
+        for step in range(1, self.count):
+            self.arrive(self.other(step))
+
+    def sent(self):
+        for step in range(1, self.count):
+            self.copy(self.other(step), self.me).wait_send()
+
+
+def over_time():
+    return lax.axis_size("tm"), lax.axis_index("tm"), lambda to: {"tm": to}
+
+
+def over_series():
+    return lax.axis_size("dp"), lax.axis_index("dp"), lambda to: {"dp": to}
+
+
+def over_chips():
+    core = my_core()
+    return (
+        lax.axis_size("tm") // 2,
+        lax.div(lax.axis_index("tm"), 2),
+        lambda to: {"tm": 2 * to + core},
+    )
+
+
+def my_core():
+    return lax.rem(lax.axis_index("tm"), 2)
+
+
+def to_other_core(source, target, sems, index):
+    return pltpu.make_async_remote_copy(
+        src_ref=source,
+        dst_ref=target,
+        send_sem=sems.at[0, index],
+        recv_sem=sems.at[1, index],
+        device_id={"tm": lax.axis_index("tm") + 1 - 2 * my_core()},
+        device_id_type=pl.DeviceIdType.MESH,
+    )
+
+
+PAD_ROWS = 48
+GROUP_COLUMNS = (384, 384, 640)
+GROUP_LANES = {"middle": 512, "first": 512, "lstm": 256}
+
+
+def travel_scratch(count, groups, steps, width, params):
+    rows = params[0].shape[0]
+    out = dict(
+        slopes=pltpu.VMEM((count, 8, steps), jnp.float32),
+        levels=pltpu.VMEM((count, 8, steps), jnp.float32),
+        stage=pltpu.VMEM((width, 2 * GROUP_COLUMNS[2]), jnp.float32),
+        attn_stage=pltpu.VMEM((width, width), jnp.float32),
+        table_stage=pltpu.VMEM((PAD_ROWS, LANES), jnp.float32),
+    )
+    for index, param in enumerate(params):
+        out["param%d" % index] = pltpu.VMEM(param.shape, jnp.float32)
+    out["load_sems"] = pltpu.SemaphoreType.DMA((len(params),))
+    for group, columns in enumerate(GROUP_COLUMNS):
+        out["params%d" % group] = pltpu.VMEM((2, groups, PAD_ROWS, columns), jnp.bfloat16)
+        out["params%d_dp" % group] = pltpu.SemaphoreType.DMA((2, groups))
+        out["params%d_core" % group] = pltpu.SemaphoreType.DMA((2, groups))
+    for name, lanes in GROUP_LANES.items():
+        out[name + "_near"] = pltpu.VMEM((width, lanes), jnp.bfloat16)
+        out[name + "_part"] = pltpu.VMEM((groups, PAD_ROWS, lanes), jnp.bfloat16)
+        out[name + "_parts"] = pltpu.VMEM((groups, PAD_ROWS, lanes), jnp.bfloat16)
+        out[name + "_chips"] = pltpu.VMEM((count // 2, PAD_ROWS, lanes), jnp.bfloat16)
+        out[name + "_core_sems"] = pltpu.SemaphoreType.DMA((2, 2))
+        out[name + "_dp_sems"] = pltpu.SemaphoreType.DMA((2, groups))
+        out[name + "_chip_sems"] = pltpu.SemaphoreType.DMA((2, count // 2))
+    for name in ("x", "adjoint", "out", "input", "slope", "predicted"):
+        out[name + "_sems"] = pltpu.SemaphoreType.DMA((2, count))
+    out["own_sems"] = pltpu.SemaphoreType.DMA((4,))
+    return out
+
+
+class Parameters:
+    def __init__(self, r, group):
+        self.buffer = buffer = getattr(r, "params%d" % group)
+        self.core = core = my_core()
+        self.over = Exchange(
+            getattr(r, "params%d_dp" % group),
+            over_series(),
+            lambda to: buffer.at[core, lax.axis_index("dp")],
+            lambda origin: buffer.at[core, origin],
+        )
+        self.sems = getattr(r, "params%d_core" % group)
+
+    def hand(self, origin, core):
+        block = self.buffer.at[core, origin]
+        return to_other_core(block, block, self.sems, origin)
+
+    def pass_on(self):
+        for step in range(1, self.over.count):
+            origin = self.over.other(step)
+            self.over.arrive(origin)
+            self.hand(origin, self.core).start()
+
+    def arrive(self):
+        for step in range(1, self.over.count):
+            self.hand(self.over.other(step), 1 - self.core).wait_recv()
+
+    def sent(self):
+        self.over.sent()
+        for step in range(1, self.over.count):
+            self.hand(self.over.other(step), self.core).wait_send()
+
+
+class Reduction:
+    def __init__(self, r, name, final):
+        self.send, self.near = getattr(r, name + "_send"), getattr(r, name + "_near")
+        self.part, self.parts = getattr(r, name + "_part"), getattr(r, name + "_parts")
+        self.chips, self.final = getattr(r, name + "_chips"), final
+        self.core, self.rows = my_core(), final.shape[1]
+        self.core_sems = getattr(r, name + "_core_sems")
+        part, parts, chips = self.part, self.parts, self.chips
+        self.to_series = Exchange(
+            getattr(r, name + "_dp_sems"),
+            over_series(),
+            lambda to: part.at[to],
+            lambda origin: parts.at[origin],
+        )
+        chip = over_chips()[1]
+        self.to_chips = Exchange(
+            getattr(r, name + "_chip_sems"),
+            over_chips(),
+            lambda to: chips.at[chip],
+            lambda origin: chips.at[origin],
+        )
+
+    def out(self):
+        return to_other_core(self.send.at[1 - self.core], self.near, self.core_sems, 0)
+
+    def back(self, core):
+        return to_other_core(self.final.at[core], self.final.at[core], self.core_sems, 1)
+
+    def sum_of(self, ref):
+        total = ref[0, : self.rows].astype(jnp.float32)
+        for index in range(1, ref.shape[0]):
+            total = total + ref[index, : self.rows].astype(jnp.float32)
+        return total
+
+    def start(self):
+        self.out().start()
+
+    def across_series(self):
+        self.out().wait_recv()
+        total = self.send[self.core].astype(jnp.float32) + self.near[...].astype(jnp.float32)
+        for group in range(self.to_series.count):
+            self.part[group, : self.rows] = low(total[group * self.rows : (group + 1) * self.rows])
+        self.to_series.start()
+
+    def across_chips(self):
+        self.to_series.arrive_all()
+        self.parts[self.to_series.me] = self.part[self.to_series.me]
+        self.chips[self.to_chips.me, : self.rows] = low(self.sum_of(self.parts))
+        self.to_chips.start()
+
+    def to_both(self):
+        self.to_chips.arrive_all()
+        self.final[self.core] = self.sum_of(self.chips)
+        self.back(self.core).start()
+
+    def finish(self):
+        self.back(1 - self.core).wait_recv()
+        self.out().wait_send()
+        self.to_series.sent()
+        self.to_chips.sent()
+        self.back(self.core).wait_send()
+
+
+def greet():
+    barrier = pltpu.get_barrier_semaphore()
+    total = 0
+    for count, me, device in (over_time(), over_series()):
+        for step in range(1, count):
+            pl.semaphore_signal(
+                barrier,
+                inc=1,
+                device_id=device(lax.rem(me + step, count)),
+                device_id_type=pl.DeviceIdType.MESH,
+            )
+            total += 1
+    return lambda: pl.semaphore_wait(barrier, total)
+
+
+def pack_params(r, group, params):
+    mine = lax.axis_index("dp")
+    buffer = getattr(r, "params%d" % group)
+
+    def put(half, column, array):
+        rows, columns = array.shape
+        buffer[half, mine, :rows, column : column + columns] = low(array[...])
+
+    if group == 0:
+        lstm, table, level = params
+        rows, columns = lstm.shape
+        split = GROUP_COLUMNS[0]
+        buffer[0, mine, :rows, :] = low(lstm[:, :split])
+        buffer[1, mine, :rows, : columns - split] = low(lstm[:, split:])
+        r.table_stage[...] = jnp.zeros_like(r.table_stage)
+        r.table_stage[: table.shape[0], :rows] = table[...]
+        r.table_stage[VECTORS : VECTORS + LEVEL_TALLY, :rows] = level[...]
+        put(1, columns - split, r.table_stage)
+    elif group == 1:
+        glu_one, qkv = params
+        put(0, 0, glu_one)
+        put(1, 0, qkv)
+    else:
+        glu_two, glu_three, inner, middle, attn = params
+        put(0, 0, glu_two)
+        put(0, glu_two.shape[1], glu_three)
+        put(1, 0, inner)
+        put(1, inner.shape[1], middle)
+        put(1, 2 * inner.shape[1], attn)
+
+
+def unpack_params(r, group, rows, attn_rows):
+    width = r.w.shape[0]
+    head_width = width // HEADS
+    buffer, stage = getattr(r, "params%d" % group), r.stage
+    columns = GROUP_COLUMNS[group]
+    for half in range(2):
+        for origin in range(buffer.shape[1]):
+            stage[origin * rows : (origin + 1) * rows, half * columns : (half + 1) * columns] = (
+                buffer[half, origin].astype(jnp.float32)[:rows]
+            )
+
+    def place(block, column, size):
+        r.w[:, block : block + size] = low(stage[:, column : column + size])
+
+    if group == 0:
+        for gate, block in enumerate((FORGET, ENTER, CANDIDATE, EXIT)):
+            place(block, gate * width, width)
+        vectors = jnp.concatenate(
+            [
+                buffer[1, origin][:, columns - LANES :].astype(jnp.float32)[: VECTORS + 8, :rows]
+                for origin in range(buffer.shape[1])
+            ],
+            axis=1,
+        )
+        r.vec[...] = vectors[:VECTORS]
+        r.level[...] = low(vectors[VECTORS:])
+    elif group == 1:
+        place(GLU_ONE_A, 0, width)
+        place(GLU_ONE_B, width, width)
+        place(QUERY, columns, width)
+        place(KEY, columns + width, width)
+        place(VALUE, columns + 2 * width, head_width)
+    else:
+        place(GLU_TWO_A, 0, width)
+        place(GLU_TWO_B, width, width)
+        place(GLU_THREE_A, 2 * width, width)
+        place(GLU_THREE_B, 3 * width, width)
+        place(INNER, columns, width)
+        place(MIDDLE, columns + width, width)
+        for origin in range(buffer.shape[1]):
+            r.attn_stage[origin * attn_rows : (origin + 1) * attn_rows, :] = stage[
+                origin * rows : origin * rows + attn_rows,
+                columns + 2 * width : columns + 3 * width,
+            ]
+        r.w[:head_width, ATTN_OUT : ATTN_OUT + width] = low(r.attn_stage[:head_width, :])
+
+
+def series_kernel(begins, reaches, x_hbm, adjoint_hbm, slopes, *others):
+    params, others = others[:10], others[10:]
+    (out_hbm, predicted_out, input_hbm, final_middle, final_first, final_lstm), scratch = (
+        others[:6],
+        others[6:],
+    )
+    count, width, steps = x_hbm.shape
+    span = count * steps
+    groups = lax.axis_size("dp")
+    names = series_scratch(span, width, width // HEADS)
+    names.update(travel_scratch(count, groups, steps, width, params))
+    r = types.SimpleNamespace(**dict(zip(names, scratch)))
+    me = lax.axis_index("tm")
+    last = count - 1
+
+    def block(ref, index):
+        return ref.at[:, rows_of(index, steps)]
+
+    x_over = Exchange(
+        r.x_sems, over_time(), lambda to: x_hbm.at[to], lambda origin: block(r.x_flat, origin)
+    )
+    adjoint_over = Exchange(
+        r.adjoint_sems,
+        over_time(),
+        lambda to: adjoint_hbm.at[to],
+        lambda origin: block(r.adjoint, origin),
+    )
+    out_over = Exchange(
+        r.out_sems, over_time(), lambda to: block(r.out, to), lambda origin: out_hbm.at[origin]
+    )
+    input_over = Exchange(
+        r.input_sems,
+        over_time(),
+        lambda to: block(r.input_grad, to),
+        lambda origin: input_hbm.at[origin],
+    )
+    slope_over = Exchange(
+        r.slope_sems, over_time(), lambda to: r.slopes.at[to], lambda origin: r.slope
+    )
+    predicted_over = Exchange(
+        r.predicted_sems, over_time(), lambda to: r.predicted, lambda origin: r.levels.at[origin]
+    )
+    travelling = [Parameters(r, group) for group in range(3)]
+    middle_sum = Reduction(r, "middle", final_middle)
+    first_sum = Reduction(r, "first", final_first)
+    lstm_sum = Reduction(r, "lstm", final_lstm)
+    own_x = pltpu.make_async_copy(x_hbm.at[me], block(r.x_flat, me), r.own_sems.at[0])
+    own_adjoint = pltpu.make_async_copy(adjoint_hbm.at[me], block(r.adjoint, me), r.own_sems.at[1])
+    own_out = pltpu.make_async_copy(block(r.out, me), out_hbm.at[me], r.own_sems.at[2])
+    own_input = pltpu.make_async_copy(block(r.input_grad, me), input_hbm.at[me], r.own_sems.at[3])
+    held = [getattr(r, "param%d" % index) for index in range(len(params))]
+    loads = [
+        pltpu.make_async_copy(param, here, r.load_sems.at[index])
+        for index, (param, here) in enumerate(zip(params, held))
+    ]
+
+    def pack(group, *indices):
+        for index in indices:
+            loads[index].wait()
+        pack_params(r, group, [held[index] for index in indices])
+
+    everyone_here = greet()
+    for load in loads:
+        load.start()
+    own_x.start()
+    own_adjoint.start()
+    pack(0, 0, 9, 8)
+    everyone_here()
+    travelling[0].over.start()
+    x_over.start()
+    pack(1, 1, 2)
+    pack(2, 4, 7, 5, 6, 3)
+    for track in range(count):
+        r.slopes[track] = jnp.concatenate(
+            [
+                slopes[level_at].astype(jnp.float32)[track : track + 1]
+                for level_at in range(LEVEL_TALLY)
+            ]
+            + [jnp.zeros((8 - LEVEL_TALLY, steps), jnp.float32)],
+            axis=0,
+        )
+    begin = begins[me]
+    choice = reaches[me]
+    horizon = jnp.where(choice == 0, 1, jnp.where(choice == 1, 5, 24))
+    rows, attn_rows = params[0].shape[0], params[3].shape[0]
+    r.gv[...] = jnp.zeros_like(r.gv)
+    own_x.wait()
+    series_turn(r, me, steps)
+    travelling[0].pass_on()
+    travelling[1].over.start()
+
+    def arriving(step, _):
+        origin = x_over.other(step)
+        x_over.arrive(origin)
+        series_turn(r, origin, steps)
+        return 0
+
+    lax.fori_loop(1, count, arriving, 0)
+    travelling[0].arrive()
+    unpack_params(r, 0, rows, attn_rows)
+    series_gates(r, begin)
+    adjoint_over.start()
+
+    @pl.when(me == last)
+    def _():
+        slope_over.start()
+        r.slope[...] = r.slopes[last]
+
+    series_forward_scan(r)
+    travelling[1].pass_on()
+    travelling[2].over.start()
+    travelling[1].arrive()
+    unpack_params(r, 1, rows, attn_rows)
+    series_forward_first(r)
+    series_forward_attention(r, begin)
+    travelling[2].pass_on()
+    travelling[2].arrive()
+    unpack_params(r, 2, rows, attn_rows)
+    own_adjoint.wait()
+    adjoint_over.arrive_all()
+
+    @pl.when(me != last)
+    def _():
+        slope_over.arrive(last)
+
+    def forward_done():
+        own_out.start()
+        out_over.start()
+
+        @pl.when(me != last)
+        def _():
+            predicted_over.send(last)
+
+    series_middle(r, horizon, forward_done)
+    middle_sum.start()
+
+    def between(tile):
+        if tile == 2:
+            middle_sum.across_series()
+
+    series_backward_attention(r, between)
+    series_backward_first(r)
+    first_sum.start()
+    series_backward_scan(r)
+    first_sum.across_series()
+    series_gate_grads(r)
+    lstm_sum.start()
+    middle_sum.across_chips()
+    series_input_grad(r)
+    own_input.start()
+    input_over.start()
+    lstm_sum.across_series()
+    middle_sum.to_both()
+    first_sum.across_chips()
+
+    @pl.when(me != last)
+    def _():
+        predicted_over.copy(last, me).wait_send()
+        predicted_out[...] = jnp.zeros_like(predicted_out)
+
+    @pl.when(me == last)
+    def _():
+        slope_over.sent()
+        predicted_over.arrive_all()
+        r.levels[last] = r.predicted[...]
+        for level_at in range(LEVEL_TALLY):
+            predicted_out[level_at] = jnp.concatenate(
+                [r.levels[track][level_at : level_at + 1] for track in range(count)], axis=0
+            )
+
+    lstm_sum.across_chips()
+    first_sum.to_both()
+    x_over.sent()
+    adjoint_over.sent()
+    for group in travelling:
+        group.sent()
+    own_out.wait()
+    out_over.arrive_all()
+    out_over.sent()
+    middle_sum.finish()
+    first_sum.finish()
+    lstm_sum.to_both()
+    own_input.wait()
+    input_over.arrive_all()
+    input_over.sent()
+    lstm_sum.finish()
+
+
+def unpack_kernel(final_middle, final_first, final_lstm, out_in, predicted_in, input_in, *others):
+    (lstm, glu_one, qkv, attn, glu_two, inner, middle, glu_three, level, table) = others[:10]
+    out, predicted, input_grad = others[10:]
+    predicted[...] = predicted_in[...]
+    rows, width = inner.shape
+    lanes = final_lstm.shape[2]
+    for ref, at in ((glu_two, 0), (glu_three, 1)):
+        ref[...] = final_middle[at, :, : 2 * width]
+    for ref, at in ((inner, 0), (middle, 1)):
+        ref[...] = final_middle[at, :, 2 * width : 3 * width]
+    small, spare = attn.shape[0], width // 5
+    for piece in range(5):
+        at = small * (piece % 4)
+        attn[:, piece * spare : (piece + 1) * spare] = final_middle[
+            piece // 4, at : at + small, 3 * width : 3 * width + spare
+        ]
+    glu_one[...] = final_first[0, :, : 2 * width]
+    qkv[...] = final_first[1, :, : qkv.shape[1]]
+    lstm[:, :lanes] = final_lstm[0]
+    lstm[:, lanes : 3 * width] = final_lstm[1, :, : 3 * width - lanes]
+    lstm[:, 3 * width :] = final_first[0, :, 2 * width : 3 * width]
+    vectors = final_lstm[1, :, 3 * width - lanes :].T
+    table[...] = vectors[: table.shape[0]]
+    level[...] = vectors[VECTORS : VECTORS + LEVEL_TALLY]
+    out[...] = out_in[...]
+    input_grad[...] = input_in[...]
+
+
+def whole_series(embedded_features, earliest_seen_moment, reach_choice, *others):
+    count, steps, width = embedded_features.shape
+    features = embedded_features.swapaxes(1, 2)
+    adjoint = others[-2].swapaxes(1, 2)
+    slopes = others[-1].swapaxes(0, 1)
+    params = others[:-4] + (others[-4].T, others[-3].T)
+    groups = lax.axis_size("dp")
+    rows = params[0].shape[0]
+    names = series_scratch(count * steps, width, width // HEADS)
+    names.update(travel_scratch(count, groups, steps, width, params))
+    smem, vmem, anywhere = (
+        pl.BlockSpec(memory_space=space) for space in (pltpu.SMEM, pltpu.VMEM, pl.ANY)
+    )
+    moved = (
+        jax.ShapeDtypeStruct(features.shape, jnp.bfloat16),
+        jax.ShapeDtypeStruct(slopes.shape, jnp.float32),
+        jax.ShapeDtypeStruct(features.shape, jnp.bfloat16),
+    )
+    out, predicted, input_grad, *finals = pl.pallas_call(
+        series_kernel,
+        out_shape=moved
+        + tuple(
+            jax.ShapeDtypeStruct((2, rows, lanes), jnp.float32) for lanes in GROUP_LANES.values()
+        ),
+        in_specs=[smem, smem, anywhere, anywhere, vmem] + [anywhere] * len(params),
+        out_specs=(anywhere, vmem, anywhere) + (vmem,) * 3,
+        scratch_shapes=list(names.values()),
+        compiler_params=pltpu.CompilerParams(
+            vmem_limit_bytes=VMEM_BYTES, collective_id=0, has_side_effects=True
+        ),
+    )(
+        earliest_seen_moment,
+        reach_choice,
+        features,
+        adjoint,
+        slopes,
+        *params,
+    )
+    *grads, level_grad, table_grad, out, predicted, input_grad = pl.pallas_call(
+        unpack_kernel,
+        out_shape=tuple(jax.ShapeDtypeStruct(param.shape, jnp.float32) for param in params) + moved,
+        in_specs=[vmem] * 6,
+        out_specs=(vmem,) * (len(params) + 3),
+    )(*finals, out, predicted, input_grad)
+    return (
+        out.swapaxes(1, 2),
+        predicted.swapaxes(0, 1),
+        input_grad.swapaxes(1, 2),
+        *grads,
+        level_grad.T,
+        table_grad.T,
+    )
+
+
+def on_device(embedded_features, *others):
+    count, steps, _ = embedded_features.shape
+    one_each = count == lax.axis_size("tm") == CHUNKS and steps == LANES
+    return (whole_series if one_each else shards)(embedded_features, *others)
+
+
 def solution(mesh):
     placed = (
         P("dp", "tm", None),
@@ -482,7 +1555,7 @@
         P("dp", None, "tm"),
     )
     return jax.shard_map(
-        shards,
+        on_device,
         mesh=mesh,
         in_specs=placed,
         out_specs=(

time: 780 us -> 60.9 us (0.08); the launches traced: 767 us -> 60.7 us
  blocking collectives: 278 us -> 0 us
  local copies, waits for them, and re-layouts: 150 us -> 0 us
  waiting for transfers between devices: 126 us -> 0 us
  matrix products: 113 us -> 0 us
  other arithmetic: 79.4 us -> 0 us
  Pallas kernels: 0 us -> 59.9 us
  between operations: 18.3 us -> 0.74 us
    all_gather x18 -> x0, blocking collectives: 204 us -> none  [the longest x8 69.8 us: entering(): pieces = jax.tree.map(lambda part: lax.all_gather(part, axis), value)]
    dot_general x55 -> x0, matrix products: 113 us -> none  [the longest x8 29.6 us: masked_scores(): jnp.einsum('gqhd,gkhd->ghqk', query_block, key_block, preferred_element_t...]
    unnamed x14 -> x0, waiting for transfers between devices: 93.7 us -> none
    pallas_call x0 -> x2, Pallas kernels: none -> 59.9 us  [the longest x1 57.6 us: whole_series(): pl.pallas_call(series_kernel, out_shape=moved + tuple((jax.ShapeDtypeStru...]
    psum x1 -> x0, blocking collectives: 54.8 us -> none  [shards(): lax.psum((grad_lstm, grad_glu_one, grad_qkv, grad_attn, grad_glu_two, gra...]
    slice x104 -> x0, local copies, waits for them, and re-layouts: 46.5 us -> none  [the longest x49 26.3 us: shards(): lax.associative_scan(affine_join, (next_forget, direct_grad), axis=1, rev...]
    pad x48 -> x0, local copies, waits for them, and re-layouts: 43.9 us -> none  [the longest x24 27.1 us: shards(): lax.associative_scan(affine_join, (next_forget, direct_grad), axis=1, rev...]
    reduce_scatter x3 -> x0, waiting for transfers between devices: 32.3 us -> none  [the longest x1 24 us: shards(): lax.psum_scatter(key_terms.reshape(series_per_device, seq_total, model_wi...]
  transfers between devices with their start and end apart: 9 -> 0, of which waited for: 7 -> 0; matrix products, arithmetic and copies ran while one was open for 7% -> 0% of each run, Pallas kernels for 0% -> 0%
where the time goes in v4:
time: 60.9 us; the launch traced here: 60.7 us
  Pallas kernels  59.9 us (98%)
  between operations  0.74 us (1%)
    pallas_call x1, Pallas kernels, whole_series(): pl.pallas_call(series_kernel, out_shape=moved + tuple((jax.ShapeDtypeStru...  57.6 us
    pallas_call x1, Pallas kernels, whole_series(): pl.pallas_call(unpack_kernel, out_shape=tuple((jax.ShapeDtypeStruct(param...  2.31 us

profile of v4, /device:TPU:0, one launch (start us, length us, event | category | flops | bytes accessed | tf_op | source)
XLA Modules:
  0.0 60.7 jit_solution(7001723847087644261)
XLA Ops:
  0.7 57.6 %shard_map.246 = (bf16[8,160,128]{2,1,0:T(8,128)(2,1)}, f32[3,8,128]{2,1,0:T(8,128)}, bf16[8,160,128]{2,1,0:T(8,128)(2,1)}, f32[2,40,512]{2,1,0:T(8,128)}, f32[2,40,512]{2,1,0:T(8,128)}, /*index=5*/f32[2,40,256]{2,1,0:T(8,128)}) custom-call(s32[8]{0:T(128)} %begins.1, s32[8]{0:T(128)} %reaches.1, bf16[8,160,128]{2,1,0:T(8,128)(2,1)} %bitcast.10, ...), custom_call_target="tpu_custom_call" | custom-call | tf_op jit(solution)/shard_map/pallas_call | solution.py:1497
  58.3 2.3 %shard_map.247 = (f32[40,640]{1,0:T(8,128)}, f32[40,320]{1,0:T(8,128)}, f32[40,360]{1,0:T(8,128)}, f32[10,160]{1,0:T(8,128)}, f32[40,320]{1,0:T(8,128)}, /*index...) custom-call(f32[2,40,512]{2,1,0:T(8,128)} %get-tuple-element.32.fina, ...), custom_call_target="tpu_custom_call" | custom-call | tf_op jit(solution)/shard_map/pallas_call | solution.py:1517

commit v5 on v4

--- a/solution.py
+++ b/solution.py
@@ -900,7 +900,7 @@
     send[0, :, 2 * width : 3 * width] = low(nn(r.x_flat[...], exit_grad))
 
 
-def series_backward_scan(r):
+def series_backward_scan(r, between):
     span = r.x.shape[0]
     steps = span // CHUNKS
     zeros = jnp.zeros((CHUNKS, LANES), jnp.float32)
@@ -921,7 +921,9 @@
             out.append((grad, mult))
         return tuple(out)
 
-    ends = lax.fori_loop(0, steps, step, ((zeros, zeros + 1.0),) * 2, unroll=8)
+    ends = lax.fori_loop(0, steps // 2, step, ((zeros, zeros + 1.0),) * 2, unroll=8)
+    between()
+    ends = lax.fori_loop(steps // 2, steps, step, ends, unroll=8)
     for half in range(2):
         grads, mults = ends[half]
         state = jnp.zeros((1, LANES), jnp.float32)
@@ -1037,9 +1039,19 @@
     )
 
 
-PAD_ROWS = 48
 GROUP_COLUMNS = (384, 384, 640)
 GROUP_LANES = {"middle": 512, "first": 512, "lstm": 256}
+DIRECT = ("lstm",)
+
+
+def fold(values):
+    lanes = values.shape[1] // 2
+    return low(jnp.concatenate([values[:, :lanes], values[:, lanes:]], axis=0))
+
+
+def unfold(values):
+    rows = values.shape[0] // 2
+    return jnp.concatenate([values[:rows], values[rows:]], axis=1)
 
 
 def travel_scratch(count, groups, steps, width, params):
@@ -1049,23 +1061,27 @@
         levels=pltpu.VMEM((count, 8, steps), jnp.float32),
         stage=pltpu.VMEM((width, 2 * GROUP_COLUMNS[2]), jnp.float32),
         attn_stage=pltpu.VMEM((width, width), jnp.float32),
-        table_stage=pltpu.VMEM((PAD_ROWS, LANES), jnp.float32),
+        table_stage=pltpu.VMEM((rows, LANES), jnp.float32),
+        pack_stage=pltpu.VMEM((rows, GROUP_COLUMNS[2]), jnp.float32),
     )
     for index, param in enumerate(params):
         out["param%d" % index] = pltpu.VMEM(param.shape, jnp.float32)
     out["load_sems"] = pltpu.SemaphoreType.DMA((len(params),))
     for group, columns in enumerate(GROUP_COLUMNS):
-        out["params%d" % group] = pltpu.VMEM((2, groups, PAD_ROWS, columns), jnp.bfloat16)
+        slab = -(-rows * columns // LANES // 16) * 16
+        out["params%d" % group] = pltpu.VMEM((2, groups, slab, LANES), jnp.bfloat16)
         out["params%d_dp" % group] = pltpu.SemaphoreType.DMA((2, groups))
         out["params%d_core" % group] = pltpu.SemaphoreType.DMA((2, groups))
     for name, lanes in GROUP_LANES.items():
         out[name + "_near"] = pltpu.VMEM((width, lanes), jnp.bfloat16)
-        out[name + "_part"] = pltpu.VMEM((groups, PAD_ROWS, lanes), jnp.bfloat16)
-        out[name + "_parts"] = pltpu.VMEM((groups, PAD_ROWS, lanes), jnp.bfloat16)
-        out[name + "_chips"] = pltpu.VMEM((count // 2, PAD_ROWS, lanes), jnp.bfloat16)
+        folded = (2 * rows, lanes // 2)
+        out[name + "_part"] = pltpu.VMEM((groups,) + folded, jnp.bfloat16)
+        out[name + "_parts"] = pltpu.VMEM((groups,) + folded, jnp.bfloat16)
+        places = count if name in DIRECT else count // 2
+        out[name + "_chips"] = pltpu.VMEM((places,) + folded, jnp.bfloat16)
         out[name + "_core_sems"] = pltpu.SemaphoreType.DMA((2, 2))
         out[name + "_dp_sems"] = pltpu.SemaphoreType.DMA((2, groups))
-        out[name + "_chip_sems"] = pltpu.SemaphoreType.DMA((2, count // 2))
+        out[name + "_chip_sems"] = pltpu.SemaphoreType.DMA((2, places))
     for name in ("x", "adjoint", "out", "input", "slope", "predicted"):
         out[name + "_sems"] = pltpu.SemaphoreType.DMA((2, count))
     out["own_sems"] = pltpu.SemaphoreType.DMA((4,))
@@ -1118,11 +1134,13 @@
             lambda to: part.at[to],
             lambda origin: parts.at[origin],
         )
-        chip = over_chips()[1]
+        self.direct = name in DIRECT
+        devices = over_time() if self.direct else over_chips()
+        place = devices[1]
         self.to_chips = Exchange(
             getattr(r, name + "_chip_sems"),
-            over_chips(),
-            lambda to: chips.at[chip],
+            devices,
+            lambda to: chips.at[place],
             lambda origin: chips.at[origin],
         )
 
@@ -1132,10 +1150,10 @@
     def back(self, core):
         return to_other_core(self.final.at[core], self.final.at[core], self.core_sems, 1)
 
-    def sum_of(self, ref):
-        total = ref[0, : self.rows].astype(jnp.float32)
-        for index in range(1, ref.shape[0]):
-            total = total + ref[index, : self.rows].astype(jnp.float32)
+    def sum_of(self, ref, first=0, stride=1):
+        total = ref[first].astype(jnp.float32)
+        for index in range(first + stride, ref.shape[0], stride):
+            total = total + ref[index].astype(jnp.float32)
         return total
 
     def start(self):
@@ -1145,26 +1163,31 @@
         self.out().wait_recv()
         total = self.send[self.core].astype(jnp.float32) + self.near[...].astype(jnp.float32)
         for group in range(self.to_series.count):
-            self.part[group, : self.rows] = low(total[group * self.rows : (group + 1) * self.rows])
+            self.part[group] = fold(total[group * self.rows : (group + 1) * self.rows])
         self.to_series.start()
 
     def across_chips(self):
         self.to_series.arrive_all()
         self.parts[self.to_series.me] = self.part[self.to_series.me]
-        self.chips[self.to_chips.me, : self.rows] = low(self.sum_of(self.parts))
+        self.chips[self.to_chips.me] = low(self.sum_of(self.parts))
         self.to_chips.start()
 
     def to_both(self):
         self.to_chips.arrive_all()
-        self.final[self.core] = self.sum_of(self.chips)
-        self.back(self.core).start()
+        if self.direct:
+            for core in range(2):
+                self.final[core] = unfold(self.sum_of(self.chips, core, 2))
+        else:
+            self.final[self.core] = unfold(self.sum_of(self.chips))
+            self.back(self.core).start()
 
     def finish(self):
-        self.back(1 - self.core).wait_recv()
+        if not self.direct:
+            self.back(1 - self.core).wait_recv()
+            self.back(self.core).wait_send()
         self.out().wait_send()
         self.to_series.sent()
         self.to_chips.sent()
-        self.back(self.core).wait_send()
 
 
 def greet():
@@ -1184,33 +1207,35 @@
 
 def pack_params(r, group, params):
     mine = lax.axis_index("dp")
-    buffer = getattr(r, "params%d" % group)
-
-    def put(half, column, array):
-        rows, columns = array.shape
-        buffer[half, mine, :rows, column : column + columns] = low(array[...])
+    buffer, stage = getattr(r, "params%d" % group), r.pack_stage
+    columns = GROUP_COLUMNS[group]
+
+    def put(half, *arrays):
+        at = 0
+        for array in arrays:
+            rows, width = array.shape
+            stage[:rows, at : at + width] = array[...]
+            at += width
+        tiles = [stage[:, tile : tile + LANES] for tile in range(0, columns, LANES)]
+        spare = buffer.shape[2] - stage.shape[0] * len(tiles)
+        tiles.append(jnp.zeros((spare, LANES), jnp.float32))
+        buffer[half, mine] = low(jnp.concatenate(tiles, axis=0))
 
     if group == 0:
         lstm, table, level = params
-        rows, columns = lstm.shape
-        split = GROUP_COLUMNS[0]
-        buffer[0, mine, :rows, :] = low(lstm[:, :split])
-        buffer[1, mine, :rows, : columns - split] = low(lstm[:, split:])
+        rows = lstm.shape[0]
         r.table_stage[...] = jnp.zeros_like(r.table_stage)
         r.table_stage[: table.shape[0], :rows] = table[...]
         r.table_stage[VECTORS : VECTORS + LEVEL_TALLY, :rows] = level[...]
-        put(1, columns - split, r.table_stage)
+        put(0, lstm[:, :columns])
+        put(1, lstm[:, columns:], r.table_stage)
     elif group == 1:
-        glu_one, qkv = params
-        put(0, 0, glu_one)
-        put(1, 0, qkv)
+        for half, array in enumerate(params):
+            put(half, array)
     else:
         glu_two, glu_three, inner, middle, attn = params
-        put(0, 0, glu_two)
-        put(0, glu_two.shape[1], glu_three)
-        put(1, 0, inner)
-        put(1, inner.shape[1], middle)
-        put(1, 2 * inner.shape[1], attn)
+        put(0, glu_two, glu_three)
+        put(1, inner, middle, attn)
 
 
 def unpack_params(r, group, rows, attn_rows):
@@ -1220,9 +1245,12 @@
     columns = GROUP_COLUMNS[group]
     for half in range(2):
         for origin in range(buffer.shape[1]):
-            stage[origin * rows : (origin + 1) * rows, half * columns : (half + 1) * columns] = (
-                buffer[half, origin].astype(jnp.float32)[:rows]
-            )
+            tiles = buffer[half, origin].astype(jnp.float32)
+            for tile in range(columns // LANES):
+                at = half * columns + tile * LANES
+                stage[origin * rows : (origin + 1) * rows, at : at + LANES] = tiles[
+                    tile * rows : (tile + 1) * rows
+                ]
 
     def place(block, column, size):
         r.w[:, block : block + size] = low(stage[:, column : column + size])
@@ -1232,7 +1260,7 @@
             place(block, gate * width, width)
         vectors = jnp.concatenate(
             [
-                buffer[1, origin][:, columns - LANES :].astype(jnp.float32)[: VECTORS + 8, :rows]
+                stage[origin * rows : origin * rows + VECTORS + 8, 4 * width : 4 * width + rows]
                 for origin in range(buffer.shape[1])
             ],
             axis=1,
@@ -1403,8 +1431,7 @@
     series_backward_attention(r, between)
     series_backward_first(r)
     first_sum.start()
-    series_backward_scan(r)
-    first_sum.across_series()
+    series_backward_scan(r, first_sum.across_series)
     series_gate_grads(r)
     lstm_sum.start()
     middle_sum.across_chips()
@@ -1489,19 +1516,14 @@
     smem, vmem, anywhere = (
         pl.BlockSpec(memory_space=space) for space in (pltpu.SMEM, pltpu.VMEM, pl.ANY)
     )
-    moved = (
-        jax.ShapeDtypeStruct(features.shape, jnp.bfloat16),
-        jax.ShapeDtypeStruct(slopes.shape, jnp.float32),
-        jax.ShapeDtypeStruct(features.shape, jnp.bfloat16),
-    )
+    moved = ((features.shape, jnp.bfloat16), (slopes.shape, jnp.float32))
+    moved += moved[:1]
     out, predicted, input_grad, *finals = pl.pallas_call(
         series_kernel,
-        out_shape=moved
-        + tuple(
-            jax.ShapeDtypeStruct((2, rows, lanes), jnp.float32) for lanes in GROUP_LANES.values()
-        ),
+        out_shape=tuple(pltpu.VMEM(*one) for one in moved)
+        + tuple(pltpu.VMEM((2, rows, lanes), jnp.float32) for lanes in GROUP_LANES.values()),
         in_specs=[smem, smem, anywhere, anywhere, vmem] + [anywhere] * len(params),
-        out_specs=(anywhere, vmem, anywhere) + (vmem,) * 3,
+        out_specs=(vmem,) * 6,
         scratch_shapes=list(names.values()),
         compiler_params=pltpu.CompilerParams(
             vmem_limit_bytes=VMEM_BYTES, collective_id=0, has_side_effects=True
@@ -1516,9 +1538,11 @@
     )
     *grads, level_grad, table_grad, out, predicted, input_grad = pl.pallas_call(
         unpack_kernel,
-        out_shape=tuple(jax.ShapeDtypeStruct(param.shape, jnp.float32) for param in params) + moved,
+        out_shape=tuple(jax.ShapeDtypeStruct(param.shape, jnp.float32) for param in params)
+        + tuple(jax.ShapeDtypeStruct(*one) for one in moved),
         in_specs=[vmem] * 6,
         out_specs=(vmem,) * (len(params) + 3),
+        compiler_params=pltpu.CompilerParams(vmem_limit_bytes=VMEM_BYTES // 6),
     )(*finals, out, predicted, input_grad)
     return (
         out.swapaxes(1, 2),

time: 60.9 us -> 57.5 us (0.944)
  Pallas kernels: 59.9 us -> 56.6 us
    pallas_call x1, Pallas kernels: 57.6 us -> 55.5 us  [whole_series(): pl.pallas_call(series_kernel, out_shape=tuple((pltpu.VMEM(*one) for one i...]
    pallas_call x1, Pallas kernels: 2.31 us -> 1.03 us  [whole_series(): pl.pallas_call(unpack_kernel, out_shape=tuple((jax.ShapeDtypeStruct(param...]
where the time goes in v5:
time: 57.5 us; the launch traced here: 57.3 us
  Pallas kernels  56.6 us (98%)
  between operations  0.7 us (1%)
    pallas_call x1, Pallas kernels, whole_series(): pl.pallas_call(series_kernel, out_shape=tuple((pltpu.VMEM(*one) for one i...  55.5 us

profile of v5, /device:TPU:0, one launch (start us, length us, event | category | flops | bytes accessed | tf_op | source)
XLA Modules:
  0.0 57.3 jit_solution(153005638432330141)
XLA Ops:
  0.7 55.5 %shard_map.246 = (bf16[8,160,128]{2,1,0:T(8,128)(2,1)S(1)}, f32[3,8,128]{2,1,0:T(8,128)S(1)}, bf16[8,160,128]{2,1,0:T(8,128)(2,1)S(1)}, f32[2,40,512]{2,1,0:T(8,...) custom-call(s32[8]{0:T(128)} %begins.1, s32[8]{0:T(128)} %reaches.1, bf16[8,160,128]{2,1,0:T(8,128)(2,1)} %bitcast.10, ...), custom_call_target="tpu_custom_call" | custom-call | tf_op jit(solution)/shard_map/pallas_call | solution.py:1521
  56.2 1.0 %shard_map.247 = (f32[40,640]{1,0:T(8,128)}, f32[40,320]{1,0:T(8,128)}, f32[40,360]{1,0:T(8,128)}, f32[10,160]{1,0:T(8,128)}, f32[40,320]{1,0:T(8,128)}, /*index...) custom-call(f32[2,40,512]{2,1,0:T(8,128)S(1)} %get-tuple-element.32., ...), custom_call_target="tpu_custom_call" | custom-call | tf_op jit(solution)/shard_map/pallas_call | solution.py:1539

commit v6 on v5

--- a/solution.py
+++ b/solution.py
@@ -484,7 +484,8 @@
 PACKED = 3968
 VECTORS = 24
 LANES = 128
-CHUNKS = 8
+SUBLANES = 8
+CHUNKS = 64
 TILE = 256
 
 
@@ -635,33 +636,43 @@
     r.exit_gate[...] = sigmoid(pre(EXIT, 3))
 
 
+def scan_state():
+    zeros = jnp.zeros((SUBLANES, LANES), jnp.float32)
+    return ((zeros, zeros + 1.0),) * (2 * CHUNKS // SUBLANES)
+
+
+def scan_step(r, steps, t, after, state):
+    out = []
+    for index, (value, mult) in enumerate(state):
+        half, start = index % 2, index // 2 * SUBLANES * steps
+        at = pl.ds(start + t, SUBLANES, stride=steps)
+        forget = r.forget[half, pl.ds(start + t + after, SUBLANES, stride=steps), :]
+        value = forget * value + r.local[half, at, :]
+        mult = mult * forget
+        r.local[half, at, :] = value
+        r.mult[half, at, :] = mult
+        out.append((value, mult))
+    return tuple(out)
+
+
+def scan_carry(r, ends, order):
+    for half in range(2):
+        state = jnp.zeros((1, LANES), jnp.float32)
+        for chunk in order:
+            r.carry[half, chunk : chunk + 1, :] = state
+            value, mult = ends[chunk // SUBLANES * 2 + half]
+            at = chunk % SUBLANES
+            state = value[at : at + 1] + mult[at : at + 1] * state
+
+
 def series_forward_scan(r):
-    span = r.x.shape[0]
-    steps = span // CHUNKS
-    zeros = jnp.zeros((CHUNKS, LANES), jnp.float32)
-
-    def step(t, state):
-        out = []
-        at = pl.ds(t, CHUNKS, stride=steps)
-        for half in range(2):
-            cell, mult = state[half]
-            forget = r.forget[half, at, :]
-            cell = forget * cell + r.local[half, at, :]
-            mult = mult * forget
-            r.local[half, at, :] = cell
-            r.mult[half, at, :] = mult
-            out.append((cell, mult))
-        return tuple(out)
-
-    ends = lax.fori_loop(0, steps, step, ((zeros, zeros + 1.0),) * 2, unroll=8)
+    steps = r.x.shape[0] // CHUNKS
+    ends = scan_state()
+    for t in range(steps):
+        ends = scan_step(r, steps, t, 0, ends)
+    scan_carry(r, ends, range(CHUNKS))
     for half in range(2):
-        cells, mults = ends[half]
-        state = jnp.zeros((1, LANES), jnp.float32)
-        r.carry[half, 0:1, :] = state
-        for chunk in range(CHUNKS - 1):
-            state = cells[chunk : chunk + 1] + mults[chunk : chunk + 1] * state
-            r.carry[half, chunk + 1 : chunk + 2, :] = state
-        r.cell[half, 0:8, :] = zeros
+        r.cell[half, 0:8, :] = jnp.zeros((8, LANES), jnp.float32)
 
 
 def series_forward_first(r):
@@ -900,37 +911,16 @@
     send[0, :, 2 * width : 3 * width] = low(nn(r.x_flat[...], exit_grad))
 
 
-def series_backward_scan(r, between):
+def series_backward_scan(r):
     span = r.x.shape[0]
     steps = span // CHUNKS
-    zeros = jnp.zeros((CHUNKS, LANES), jnp.float32)
     for half in range(2):
-        r.forget[half, span:, :] = zeros
-
-    def step(count, state):
-        t = steps - 1 - count
-        out = []
-        at, after = pl.ds(t, CHUNKS, stride=steps), pl.ds(t + 1, CHUNKS, stride=steps)
-        for half in range(2):
-            grad, mult = state[half]
-            forget = r.forget[half, after, :]
-            grad = forget * grad + r.local[half, at, :]
-            mult = mult * forget
-            r.local[half, at, :] = grad
-            r.mult[half, at, :] = mult
-            out.append((grad, mult))
-        return tuple(out)
-
-    ends = lax.fori_loop(0, steps // 2, step, ((zeros, zeros + 1.0),) * 2, unroll=8)
-    between()
-    ends = lax.fori_loop(steps // 2, steps, step, ends, unroll=8)
-    for half in range(2):
-        grads, mults = ends[half]
-        state = jnp.zeros((1, LANES), jnp.float32)
-        r.carry[half, CHUNKS - 1 : CHUNKS, :] = state
-        for chunk in range(CHUNKS - 1, 0, -1):
-            state = grads[chunk : chunk + 1] + mults[chunk : chunk + 1] * state
-            r.carry[half, chunk - 1 : chunk, :] = state
+        r.forget[half, span:, :] = jnp.zeros((8, LANES), jnp.float32)
+
+    ends = scan_state()
+    for t in range(steps - 1, -1, -1):
+        ends = scan_step(r, steps, t, 1, ends)
+    scan_carry(r, ends, range(CHUNKS - 1, -1, -1))
 
 
 def series_gate_grads(r):
@@ -971,40 +961,39 @@
 
 
 class Exchange:
-    def __init__(self, sems, devices, source, target):
+    def __init__(self, sems, devices, source, target, sources, targets):
         self.sems, self.source, self.target = sems, source, target
+        self.sources, self.targets = sources, targets
         self.count, self.me, self.device = devices
 
     def other(self, step):
         return lax.rem(self.me + step, self.count)
 
-    def copy(self, to, origin):
+    def copy(self, to, source, target):
         return pltpu.make_async_remote_copy(
-            src_ref=self.source(to),
-            dst_ref=self.target(origin),
-            send_sem=self.sems.at[0, to],
-            recv_sem=self.sems.at[1, origin],
+            src_ref=source,
+            dst_ref=target,
+            send_sem=self.sems.at[0],
+            recv_sem=self.sems.at[1],
             device_id=self.device(to),
             device_id_type=pl.DeviceIdType.MESH,
         )
 
-    def send(self, to):
-        self.copy(to, self.me).start()
-
-    def arrive(self, origin):
-        self.copy(origin, origin).wait_recv()
+    def one(self, to):
+        return self.copy(to, self.source(to), self.target(self.me))
 
     def start(self):
         for step in range(1, self.count):
-            self.send(self.other(step))
-
-    def arrive_all(self):
-        for step in range(1, self.count):
-            self.arrive(self.other(step))
+            self.one(self.other(step)).start()
+
+    def all(self):
+        return self.copy(self.other(1), self.sources, self.targets)
+
+    def arrive(self):
+        self.all().wait_recv()
 
     def sent(self):
-        for step in range(1, self.count):
-            self.copy(self.other(step), self.me).wait_send()
+        self.all().wait_send()
 
 
 def over_time():
@@ -1066,12 +1055,14 @@
     )
     for index, param in enumerate(params):
         out["param%d" % index] = pltpu.VMEM(param.shape, jnp.float32)
-    out["load_sems"] = pltpu.SemaphoreType.DMA((len(params),))
+    out["load_sems"] = pltpu.SemaphoreType.DMA((len(params) + 3,))
+    out["begins"] = pltpu.SMEM((count,), jnp.int32)
+    out["reaches"] = pltpu.SMEM((count,), jnp.int32)
+    out["slope_in"] = pltpu.VMEM((LEVEL_TALLY, count, steps), jnp.bfloat16)
     for group, columns in enumerate(GROUP_COLUMNS):
         slab = -(-rows * columns // LANES // 16) * 16
         out["params%d" % group] = pltpu.VMEM((2, groups, slab, LANES), jnp.bfloat16)
-        out["params%d_dp" % group] = pltpu.SemaphoreType.DMA((2, groups))
-        out["params%d_core" % group] = pltpu.SemaphoreType.DMA((2, groups))
+        out["params%d_sems" % group] = pltpu.SemaphoreType.DMA((3 + groups,))
     for name, lanes in GROUP_LANES.items():
         out[name + "_near"] = pltpu.VMEM((width, lanes), jnp.bfloat16)
         folded = (2 * rows, lanes // 2)
@@ -1080,44 +1071,58 @@
         places = count if name in DIRECT else count // 2
         out[name + "_chips"] = pltpu.VMEM((places,) + folded, jnp.bfloat16)
         out[name + "_core_sems"] = pltpu.SemaphoreType.DMA((2, 2))
-        out[name + "_dp_sems"] = pltpu.SemaphoreType.DMA((2, groups))
-        out[name + "_chip_sems"] = pltpu.SemaphoreType.DMA((2, places))
+        out[name + "_dp_sems"] = pltpu.SemaphoreType.DMA((2,))
+        out[name + "_chip_sems"] = pltpu.SemaphoreType.DMA((2,))
     for name in ("x", "adjoint", "out", "input", "slope", "predicted"):
-        out[name + "_sems"] = pltpu.SemaphoreType.DMA((2, count))
+        out[name + "_sems"] = pltpu.SemaphoreType.DMA((2,))
     out["own_sems"] = pltpu.SemaphoreType.DMA((4,))
     return out
 
 
 class Parameters:
     def __init__(self, r, group):
-        self.buffer = buffer = getattr(r, "params%d" % group)
-        self.core = core = my_core()
-        self.over = Exchange(
-            getattr(r, "params%d_dp" % group),
-            over_series(),
-            lambda to: buffer.at[core, lax.axis_index("dp")],
-            lambda origin: buffer.at[core, origin],
-        )
-        self.sems = getattr(r, "params%d_core" % group)
-
-    def hand(self, origin, core):
-        block = self.buffer.at[core, origin]
-        return to_other_core(block, block, self.sems, origin)
+        self.buffer = getattr(r, "params%d" % group)
+        self.sems = getattr(r, "params%d_sems" % group)
+        self.core, self.mine, self.count = my_core(), lax.axis_index("dp"), lax.axis_size("dp")
+
+    def other(self, step):
+        return lax.rem(self.mine + step, self.count)
+
+    def move(self, blocks, device, send, arrive):
+        return pltpu.make_async_remote_copy(
+            src_ref=blocks,
+            dst_ref=blocks,
+            send_sem=self.sems.at[send],
+            recv_sem=self.sems.at[arrive],
+            device_id=device,
+            device_id_type=pl.DeviceIdType.MESH,
+        )
+
+    def over(self, to, origin):
+        return self.move(self.buffer.at[self.core, origin], {"dp": to}, 0, 3 + origin)
+
+    def hand(self, blocks):
+        return self.move(blocks, {"tm": lax.axis_index("tm") + 1 - 2 * self.core}, 1, 2)
+
+    def others(self, core):
+        return self.buffer.at[core, pl.ds(0, self.count - 1)]
+
+    def start(self):
+        for step in range(1, self.count):
+            self.over(self.other(step), self.mine).start()
 
     def pass_on(self):
-        for step in range(1, self.over.count):
-            origin = self.over.other(step)
-            self.over.arrive(origin)
-            self.hand(origin, self.core).start()
+        for step in range(1, self.count):
+            origin = self.other(step)
+            self.over(origin, origin).wait_recv()
+            self.hand(self.buffer.at[self.core, origin]).start()
 
     def arrive(self):
-        for step in range(1, self.over.count):
-            self.hand(self.over.other(step), 1 - self.core).wait_recv()
+        self.hand(self.others(1 - self.core)).wait_recv()
 
     def sent(self):
-        self.over.sent()
-        for step in range(1, self.over.count):
-            self.hand(self.over.other(step), self.core).wait_send()
+        self.move(self.others(self.core), {"dp": self.other(1)}, 0, 3).wait_send()
+        self.hand(self.others(self.core)).wait_send()
 
 
 class Reduction:
@@ -1133,6 +1138,8 @@
             over_series(),
             lambda to: part.at[to],
             lambda origin: parts.at[origin],
+            part.at[pl.ds(0, part.shape[0] - 1)],
+            parts.at[pl.ds(0, part.shape[0] - 1)],
         )
         self.direct = name in DIRECT
         devices = over_time() if self.direct else over_chips()
@@ -1142,6 +1149,8 @@
             devices,
             lambda to: chips.at[place],
             lambda origin: chips.at[origin],
+            chips.at[pl.ds(0, chips.shape[0] - 1)],
+            chips.at[pl.ds(0, chips.shape[0] - 1)],
         )
 
     def out(self):
@@ -1167,13 +1176,13 @@
         self.to_series.start()
 
     def across_chips(self):
-        self.to_series.arrive_all()
+        self.to_series.arrive()
         self.parts[self.to_series.me] = self.part[self.to_series.me]
         self.chips[self.to_chips.me] = low(self.sum_of(self.parts))
         self.to_chips.start()
 
     def to_both(self):
-        self.to_chips.arrive_all()
+        self.to_chips.arrive()
         if self.direct:
             for core in range(2):
                 self.final[core] = unfold(self.sum_of(self.chips, core, 2))
@@ -1288,7 +1297,7 @@
         r.w[:head_width, ATTN_OUT : ATTN_OUT + width] = low(r.attn_stage[:head_width, :])
 
 
-def series_kernel(begins, reaches, x_hbm, adjoint_hbm, slopes, *others):
+def series_kernel(begins_hbm, reaches_hbm, x_hbm, adjoint_hbm, slopes_hbm, *others):
     params, others = others[:10], others[10:]
     (out_hbm, predicted_out, input_hbm, final_middle, final_first, final_lstm), scratch = (
         others[:6],
@@ -1306,29 +1315,51 @@
     def block(ref, index):
         return ref.at[:, rows_of(index, steps)]
 
-    x_over = Exchange(
-        r.x_sems, over_time(), lambda to: x_hbm.at[to], lambda origin: block(r.x_flat, origin)
-    )
-    adjoint_over = Exchange(
-        r.adjoint_sems,
+    def whole(ref):
+        return ref.at[:, pl.ds(0, (count - 1) * steps)]
+
+    def rest(ref):
+        return ref.at[pl.ds(0, count - 1)]
+
+    def inward(sems, source, target):
+        return Exchange(
+            sems,
+            over_time(),
+            lambda to: source.at[to],
+            lambda origin: block(target, origin),
+            rest(source),
+            whole(target),
+        )
+
+    def outward(sems, source, target):
+        return Exchange(
+            sems,
+            over_time(),
+            lambda to: block(source, to),
+            lambda origin: target.at[origin],
+            whole(source),
+            rest(target),
+        )
+
+    x_over = inward(r.x_sems, x_hbm, r.x_flat)
+    adjoint_over = inward(r.adjoint_sems, adjoint_hbm, r.adjoint)
+    out_over = outward(r.out_sems, r.out, out_hbm)
+    input_over = outward(r.input_sems, r.input_grad, input_hbm)
+    slope_over = Exchange(
+        r.slope_sems,
         over_time(),
-        lambda to: adjoint_hbm.at[to],
-        lambda origin: block(r.adjoint, origin),
-    )
-    out_over = Exchange(
-        r.out_sems, over_time(), lambda to: block(r.out, to), lambda origin: out_hbm.at[origin]
-    )
-    input_over = Exchange(
-        r.input_sems,
+        lambda to: r.slopes.at[to],
+        lambda origin: r.slope,
+        rest(r.slopes),
+        r.slope,
+    )
+    predicted_over = Exchange(
+        r.predicted_sems,
         over_time(),
-        lambda to: block(r.input_grad, to),
-        lambda origin: input_hbm.at[origin],
-    )
-    slope_over = Exchange(
-        r.slope_sems, over_time(), lambda to: r.slopes.at[to], lambda origin: r.slope
-    )
-    predicted_over = Exchange(
-        r.predicted_sems, over_time(), lambda to: r.predicted, lambda origin: r.levels.at[origin]
+        lambda to: r.predicted,
+        lambda origin: r.levels.at[origin],
+        r.predicted,
+        rest(r.levels),
     )
     travelling = [Parameters(r, group) for group in range(3)]
     middle_sum = Reduction(r, "middle", final_middle)
@@ -1341,8 +1372,14 @@
     held = [getattr(r, "param%d" % index) for index in range(len(params))]
     loads = [
         pltpu.make_async_copy(param, here, r.load_sems.at[index])
-        for index, (param, here) in enumerate(zip(params, held))
+        for index, (param, here) in enumerate(
+            zip(
+                params + (begins_hbm, reaches_hbm, slopes_hbm),
+                held + [r.begins, r.reaches, r.slope_in],
+            )
+        )
     ]
+    begins, reaches, slopes = r.begins, r.reaches, r.slope_in
 
     def pack(group, *indices):
         for index in indices:
@@ -1356,10 +1393,13 @@
     own_adjoint.start()
     pack(0, 0, 9, 8)
     everyone_here()
-    travelling[0].over.start()
+    travelling[0].start()
     x_over.start()
     pack(1, 1, 2)
+    travelling[1].start()
     pack(2, 4, 7, 5, 6, 3)
+    for load in loads[len(params) :]:
+        load.wait()
     for track in range(count):
         r.slopes[track] = jnp.concatenate(
             [
@@ -1377,18 +1417,15 @@
     own_x.wait()
     series_turn(r, me, steps)
     travelling[0].pass_on()
-    travelling[1].over.start()
-
-    def arriving(step, _):
-        origin = x_over.other(step)
-        x_over.arrive(origin)
-        series_turn(r, origin, steps)
-        return 0
-
-    lax.fori_loop(1, count, arriving, 0)
+
+    x_over.arrive()
+    for step in range(1, count):
+        series_turn(r, x_over.other(step), steps)
     travelling[0].arrive()
     unpack_params(r, 0, rows, attn_rows)
     series_gates(r, begin)
+    travelling[1].pass_on()
+    travelling[2].start()
     adjoint_over.start()
 
     @pl.when(me == last)
@@ -1397,8 +1434,6 @@
         r.slope[...] = r.slopes[last]
 
     series_forward_scan(r)
-    travelling[1].pass_on()
-    travelling[2].over.start()
     travelling[1].arrive()
     unpack_params(r, 1, rows, attn_rows)
     series_forward_first(r)
@@ -1407,11 +1442,11 @@
     travelling[2].arrive()
     unpack_params(r, 2, rows, attn_rows)
     own_adjoint.wait()
-    adjoint_over.arrive_all()
+    adjoint_over.arrive()
 
     @pl.when(me != last)
     def _():
-        slope_over.arrive(last)
+        slope_over.arrive()
 
     def forward_done():
         own_out.start()
@@ -1419,7 +1454,7 @@
 
         @pl.when(me != last)
         def _():
-            predicted_over.send(last)
+            predicted_over.one(last).start()
 
     series_middle(r, horizon, forward_done)
     middle_sum.start()
@@ -1431,26 +1466,27 @@
     series_backward_attention(r, between)
     series_backward_first(r)
     first_sum.start()
-    series_backward_scan(r, first_sum.across_series)
+    series_backward_scan(r)
     series_gate_grads(r)
     lstm_sum.start()
+    first_sum.across_series()
     middle_sum.across_chips()
     series_input_grad(r)
     own_input.start()
     input_over.start()
     lstm_sum.across_series()
+    first_sum.across_chips()
     middle_sum.to_both()
-    first_sum.across_chips()
 
     @pl.when(me != last)
     def _():
-        predicted_over.copy(last, me).wait_send()
+        predicted_over.sent()
         predicted_out[...] = jnp.zeros_like(predicted_out)
 
     @pl.when(me == last)
     def _():
         slope_over.sent()
-        predicted_over.arrive_all()
+        predicted_over.arrive()
         r.levels[last] = r.predicted[...]
         for level_at in range(LEVEL_TALLY):
             predicted_out[level_at] = jnp.concatenate(
@@ -1464,13 +1500,13 @@
     for group in travelling:
         group.sent()
     own_out.wait()
-    out_over.arrive_all()
+    out_over.arrive()
     out_over.sent()
     middle_sum.finish()
     first_sum.finish()
     lstm_sum.to_both()
     own_input.wait()
-    input_over.arrive_all()
+    input_over.arrive()
     input_over.sent()
     lstm_sum.finish()
 
@@ -1522,7 +1558,7 @@
         series_kernel,
         out_shape=tuple(pltpu.VMEM(*one) for one in moved)
         + tuple(pltpu.VMEM((2, rows, lanes), jnp.float32) for lanes in GROUP_LANES.values()),
-        in_specs=[smem, smem, anywhere, anywhere, vmem] + [anywhere] * len(params),
+        in_specs=[anywhere] * (5 + len(params)),
         out_specs=(vmem,) * 6,
         scratch_shapes=list(names.values()),
         compiler_params=pltpu.CompilerParams(
@@ -1556,7 +1592,7 @@
 
 def on_device(embedded_features, *others):
     count, steps, _ = embedded_features.shape
-    one_each = count == lax.axis_size("tm") == CHUNKS and steps == LANES
+    one_each = count == lax.axis_size("tm") == SUBLANES and steps == LANES
     return (whole_series if one_each else shards)(embedded_features, *others)
 
 

time: 57.5 us -> 51.6 us (0.90)
  Pallas kernels: 56.6 us -> 50.7 us
    pallas_call x1, Pallas kernels: 55.5 us -> 49.7 us  [whole_series(): pl.pallas_call(series_kernel, out_shape=tuple((pltpu.VMEM(*one) for one i...]
where the time goes in v6:
time: 51.6 us; the launch traced here: 51.4 us
  Pallas kernels  50.7 us (98%)
  between operations  0.7 us (1%)
    pallas_call x1, Pallas kernels, whole_series(): pl.pallas_call(series_kernel, out_shape=tuple((pltpu.VMEM(*one) for one i...  49.7 us
    pallas_call x1, Pallas kernels, whole_series(): pl.pallas_call(unpack_kernel, out_shape=tuple((jax.ShapeDtypeStruct(param...  1.03 us

profile of v6, /device:TPU:0, one launch (start us, length us, event | category | flops | bytes accessed | tf_op | source)
XLA Modules:
  0.0 51.4 jit_solution(7672072316192346620)
XLA Ops:
  0.7 49.7 %shard_map.246 = (bf16[8,160,128]{2,1,0:T(8,128)(2,1)S(1)}, f32[3,8,128]{2,1,0:T(8,128)S(1)}, bf16[8,160,128]{2,1,0:T(8,128)(2,1)S(1)}, f32[2,40,512]{2,1,0:T(8,...) custom-call(s32[8]{0:T(128)} %begins_hbm.1, s32[8]{0:T(128)} %reaches_hbm.1, ...), custom_call_target="tpu_custom_call" | custom-call | tf_op jit(solution)/shard_map/pallas_call | solution.py:1557
  50.3 1.0 %shard_map.247 = (f32[40,640]{1,0:T(8,128)}, f32[40,320]{1,0:T(8,128)}, f32[40,360]{1,0:T(8,128)}, f32[10,160]{1,0:T(8,128)}, f32[40,320]{1,0:T(8,128)}, /*index...) custom-call(f32[2,40,512]{2,1,0:T(8,128)S(1)} %get-tuple-element.32., ...), custom_call_target="tpu_custom_call" | custom-call | tf_op jit(solution)/shard_map/pallas_call | solution.py:1575

commit v7 on v6

--- a/solution.py
+++ b/solution.py
@@ -572,9 +572,9 @@
         unit_one=full,
         inverse_one=column,
         first_low=half,
-        keys=half,
+        keys=pltpu.VMEM((span, width + 1), jnp.bfloat16),
         values=narrow,
-        head_queries=pltpu.VMEM((HEADS, span, width), jnp.bfloat16),
+        head_queries=pltpu.VMEM((HEADS, span, width + 1), jnp.bfloat16),
         head_keys=pltpu.VMEM((HEADS, span, width), jnp.bfloat16),
         **{
             "chances%d" % tile: pltpu.VMEM((HEADS, TILE, (tile + 1) * TILE), jnp.float32)
@@ -675,7 +675,7 @@
         r.cell[half, 0:8, :] = jnp.zeros((8, LANES), jnp.float32)
 
 
-def series_forward_first(r):
+def series_forward_first(r, begin):
     w, vec = r.w, r.vec
     span, width = r.x.shape
     head_width = width // HEADS
@@ -705,40 +705,55 @@
     r.first_low[...] = out
     query = low(nn(out, w[:, QUERY : QUERY + width]))
     key = low(nn(out, w[:, KEY : KEY + width]))
-    r.keys[...] = key
+    time = lax.broadcasted_iota(jnp.int32, (span, 1), 0)
+    r.keys[...] = jnp.concatenate([key, low(jnp.where(time < begin, NEG_BIG, 0.0))], axis=1)
+    one = jnp.ones((span, 1), jnp.bfloat16)
     r.values[...] = low(nn(out, w[:, VALUE : VALUE + head_width]))
     for head in range(HEADS):
         mine = lane_head((span, width), head_width, head)
-        r.head_queries[head] = jnp.where(mine, query, jnp.zeros_like(query))
+        r.head_queries[head] = jnp.concatenate(
+            [jnp.where(mine, query, jnp.zeros_like(query)), one], axis=1
+        )
         r.head_keys[head] = jnp.where(mine, key, jnp.zeros_like(key))
 
 
-def series_forward_attention(r, begin):
+def series_forward_attention(r, begin, between):
     span, head_width = r.values.shape
+    width = head_width * HEADS
     scale = head_width ** (-0.5) * LOG2_E
+    row = lax.broadcasted_iota(jnp.int32, (TILE, TILE), 0)
+    col = lax.broadcasted_iota(jnp.int32, (TILE, TILE), 1)
     for tile in range(span // TILE):
-        rows = slice(tile * TILE, (tile + 1) * TILE)
-        seen = (tile + 1) * TILE
-        row = tile * TILE + lax.broadcasted_iota(jnp.int32, (TILE, seen), 0)
-        col = lax.broadcasted_iota(jnp.int32, (TILE, seen), 1)
+        start, seen = tile * TILE, (tile + 1) * TILE
+        rows = slice(start, seen)
         chances = getattr(r, "chances%d" % tile)
-        r.block[:, :seen] = jnp.where(
-            (col <= row) & (col >= jnp.minimum(begin, row)), 0.0, NEG_BIG
+        r.block[:, :TILE] = jnp.where(
+            (col <= row) & (col >= jnp.minimum(begin - start, row)), 0.0, NEG_BIG
         )
         for head in range(HEADS):
-            scores = (
-                nt(r.head_queries[head, rows, :], r.keys[:seen, :]) * scale + r.block[:, :seen]
+            near = (
+                nt(r.head_queries[head, rows, :width], r.keys[rows, :width]) + r.block[:, :TILE]
             )
-            top = jnp.max(scores, axis=-1, keepdims=True)
-            raised = jnp.exp2(scores - top)
-            total = jnp.sum(raised, axis=-1, keepdims=True)
-            chances[head] = raised * (1.0 / total)
+            top = jnp.max(near, axis=-1, keepdims=True)
+            if tile:
+                far = nt(r.head_queries[head, rows, :], r.keys[:start, :])
+                top = jnp.maximum(top, jnp.max(far, axis=-1, keepdims=True))
+                far = jnp.exp2((far - top) * scale)
+            near = jnp.exp2((near - top) * scale)
+            total = jnp.sum(near, axis=-1, keepdims=True)
+            if tile:
+                total = total + jnp.sum(far, axis=-1, keepdims=True)
+            share = 1.0 / total
+            chances[head, :, start:] = near * share
+            if tile:
+                chances[head, :, :start] = far * share
         weights = chances[0]
         for head in range(1, HEADS):
             weights = weights + chances[head]
         weights = low(weights)
         r.chance_sum[rows, :seen] = weights
         r.mixed[rows, :] = low(nn(weights, r.values[:seen, :]) * (1.0 / HEADS))
+        between(tile)
 
 
 def series_middle(r, horizon, after_forward):
@@ -860,7 +875,8 @@
         total = jnp.zeros((TILE, width), jnp.float32)
         for head in range(HEADS):
             total = total + tn(
-                getattr(r, "score_grads%d" % tile)[head], r.head_queries[head, start:, :]
+                getattr(r, "score_grads%d" % tile)[head],
+                r.head_queries[head, start:, :width],
             )
         r.key_grad[cols, :] = low(total)
         r.value_grad[cols, :] = low(
@@ -1426,7 +1442,6 @@
     series_gates(r, begin)
     travelling[1].pass_on()
     travelling[2].start()
-    adjoint_over.start()
 
     @pl.when(me == last)
     def _():
@@ -1436,9 +1451,14 @@
     series_forward_scan(r)
     travelling[1].arrive()
     unpack_params(r, 1, rows, attn_rows)
-    series_forward_first(r)
-    series_forward_attention(r, begin)
-    travelling[2].pass_on()
+    adjoint_over.start()
+    series_forward_first(r, begin)
+
+    def within(tile):
+        if tile == 2:
+            travelling[2].pass_on()
+
+    series_forward_attention(r, begin, within)
     travelling[2].arrive()
     unpack_params(r, 2, rows, attn_rows)
     own_adjoint.wait()

time: 51.6 us -> 51 us (0.988)
    pallas_call x1, Pallas kernels: 49.7 us -> 49.1 us  [whole_series(): pl.pallas_call(series_kernel, out_shape=tuple((pltpu.VMEM(*one) for one i...]
where the time goes in v7:
time: 51 us; the launch traced here: 50.9 us
  Pallas kernels  50.2 us (98%)
  between operations  0.7 us (1%)
    pallas_call x1, Pallas kernels, whole_series(): pl.pallas_call(series_kernel, out_shape=tuple((pltpu.VMEM(*one) for one i...  49.1 us
    pallas_call x1, Pallas kernels, whole_series(): pl.pallas_call(unpack_kernel, out_shape=tuple((jax.ShapeDtypeStruct(param...  1.03 us

profile of v7, /device:TPU:0, one launch (start us, length us, event | category | flops | bytes accessed | tf_op | source)
XLA Modules:
  0.0 50.9 jit_solution(5361297641398050268)
XLA Ops:
  0.7 49.1 %shard_map.246 = (bf16[8,160,128]{2,1,0:T(8,128)(2,1)S(1)}, f32[3,8,128]{2,1,0:T(8,128)S(1)}, bf16[8,160,128]{2,1,0:T(8,128)(2,1)S(1)}, f32[2,40,512]{2,1,0:T(8,...) custom-call(s32[8]{0:T(128)} %begins_hbm.1, s32[8]{0:T(128)} %reaches_hbm.1, ...), custom_call_target="tpu_custom_call" | custom-call | tf_op jit(solution)/shard_map/pallas_call | solution.py:1577
  49.8 1.0 %shard_map.247 = (f32[40,640]{1,0:T(8,128)}, f32[40,320]{1,0:T(8,128)}, f32[40,360]{1,0:T(8,128)}, f32[10,160]{1,0:T(8,128)}, f32[40,320]{1,0:T(8,128)}, /*index...) custom-call(f32[2,40,512]{2,1,0:T(8,128)S(1)} %get-tuple-element.32., ...), custom_call_target="tpu_custom_call" | custom-call | tf_op jit(solution)/shard_map/pallas_call | solution.py:1595

commit v8 on v7

--- a/solution.py
+++ b/solution.py
@@ -1078,7 +1078,7 @@
     for group, columns in enumerate(GROUP_COLUMNS):
         slab = -(-rows * columns // LANES // 16) * 16
         out["params%d" % group] = pltpu.VMEM((2, groups, slab, LANES), jnp.bfloat16)
-        out["params%d_sems" % group] = pltpu.SemaphoreType.DMA((3 + groups,))
+        out["params%d_sems" % group] = pltpu.SemaphoreType.DMA((4,))
     for name, lanes in GROUP_LANES.items():
         out[name + "_near"] = pltpu.VMEM((width, lanes), jnp.bfloat16)
         folded = (2 * rows, lanes // 2)
@@ -1115,7 +1115,7 @@
         )
 
     def over(self, to, origin):
-        return self.move(self.buffer.at[self.core, origin], {"dp": to}, 0, 3 + origin)
+        return self.move(self.buffer.at[self.core, origin], {"dp": to}, 0, 3)
 
     def hand(self, blocks):
         return self.move(blocks, {"tm": lax.axis_index("tm") + 1 - 2 * self.core}, 1, 2)
@@ -1128,10 +1128,9 @@
             self.over(self.other(step), self.mine).start()
 
     def pass_on(self):
+        self.move(self.others(self.core), {"dp": self.other(1)}, 0, 3).wait_recv()
         for step in range(1, self.count):
-            origin = self.other(step)
-            self.over(origin, origin).wait_recv()
-            self.hand(self.buffer.at[self.core, origin]).start()
+            self.hand(self.buffer.at[self.core, self.other(step)]).start()
 
     def arrive(self):
         self.hand(self.others(1 - self.core)).wait_recv()

time: 51 us -> 50.9 us (level)
  no operation moved by 1% of the time
where the time goes in v8:
time: 50.9 us; the launch traced here: 50.7 us
  Pallas kernels  50 us (98%)
  between operations  0.7 us (1%)
    pallas_call x1, Pallas kernels, whole_series(): pl.pallas_call(series_kernel, out_shape=tuple((pltpu.VMEM(*one) for one i...  49 us
    pallas_call x1, Pallas kernels, whole_series(): pl.pallas_call(unpack_kernel, out_shape=tuple((jax.ShapeDtypeStruct(param...  1.03 us

profile of v8, /device:TPU:0, one launch (start us, length us, event | category | flops | bytes accessed | tf_op | source)
XLA Modules:
  0.0 50.7 jit_solution(3892233883479207909)
XLA Ops:
  0.7 49.0 %shard_map.246 = (bf16[8,160,128]{2,1,0:T(8,128)(2,1)S(1)}, f32[3,8,128]{2,1,0:T(8,128)S(1)}, bf16[8,160,128]{2,1,0:T(8,128)(2,1)S(1)}, f32[2,40,512]{2,1,0:T(8,...) custom-call(s32[8]{0:T(128)} %begins_hbm.1, s32[8]{0:T(128)} %reaches_hbm.1, ...), custom_call_target="tpu_custom_call" | custom-call | tf_op jit(solution)/shard_map/pallas_call | solution.py:1576
  49.6 1.0 %shard_map.247 = (f32[40,640]{1,0:T(8,128)}, f32[40,320]{1,0:T(8,128)}, f32[40,360]{1,0:T(8,128)}, f32[10,160]{1,0:T(8,128)}, f32[40,320]{1,0:T(8,128)}, /*index...) custom-call(f32[2,40,512]{2,1,0:T(8,128)S(1)} %get-tuple-element.32., ...), custom_call_target="tpu_custom_call" | custom-call | tf_op jit(solution)/shard_map/pallas_call | solution.py:1594
